TPU v7x, 32 devices: a whole 2x2x4 slice. The times are simulated.
32 devices in a mesh: section: 8 (over y, x, core), dp: 4 (over z).
Axes of the slice: x: 2, y: 2, z: 4, core: 2. Of those that a mesh axis runs over, the one named last changes fastest.
Arguments:
- inputs: bfloat16 [8, 2, 1024, 2048], P('section', None, 'dp'), may hold values from -6 to 6
- cotangent: bfloat16 [8, 2, 1024, 2048], P('section', None, 'dp'), may hold values from -6 to 6
- w_gate: bfloat16 [8, 2, 2048, 256], P('section'), may hold values from -0.125 to 0.125
- w_up: bfloat16 [8, 2, 2048, 256], P('section'), may hold values from -0.125 to 0.125
- w_down: bfloat16 [8, 2, 256, 2048], P('section'), may hold values from -0.375 to 0.375
- mom_gate: float32 [8, 2048, 256], P('section', 'dp'), may hold values from -6 to 6
- mom_up: float32 [8, 2048, 256], P('section', 'dp'), may hold values from -6 to 6
- mom_down: float32 [8, 2048, 256], P('section', 'dp'), may hold values from -6 to 6
Outputs:
- grad_in: bfloat16 [8, 2, 1024, 2048], P('section', None, 'dp')
- new_gate: float32 [8, 2048, 256], P('section', 'dp')
- new_up: float32 [8, 2048, 256], P('section', 'dp')
- new_down: float32 [8, 2048, 256], P('section', 'dp')
All inputs are finite; a program needn't handle non-finite values.
Results may differ from a plain program's by a relative error of at most 0.009.
Values may be sent and summed in bfloat16 or wider, within the bound.
No kernel may reach another device: no remote copies, remote signals or barrier semaphores. Data moves between devices by JAX's collectives and lax.ppermute only.
A program may use at most 128 MiB of HBM per device.

v0:
```python
import jax
import jax.numpy as jnp
from jax import lax
from jax.sharding import PartitionSpec as P


def from_behind(value, axis, steps):
    count = lax.axis_size(axis)
    first, last = (max(0, -steps), min(count, count - steps))
    return lax.ppermute(value, axis, [(source, source + steps) for source in range(first, last)])


def from_partner(value, axis, stride):
    mask = 2**stride
    pairs = [(source, source ^ mask) for source in range(lax.axis_size(axis))]
    return lax.ppermute(value, axis, pairs)


def contract_rows(left, right):
    return lax.dot_general(
        left, right, (((0,), (0,)), ((), ())), preferred_element_type=jnp.float32
    )


def backward_block(block_in, block_cot, gate_mat, up_mat, down_mat):
    gate_pre = jnp.dot(block_in, gate_mat, preferred_element_type=jnp.float32)
    up_pre = jnp.dot(block_in, up_mat, preferred_element_type=jnp.float32)
    sigmoid_val = jax.nn.sigmoid(gate_pre)
    activated = gate_pre * sigmoid_val
    hidden = (activated * up_pre).astype(jnp.bfloat16)
    hidden_grad = lax.dot_general(
        block_cot, down_mat, (((1,), (1,)), ((), ())), preferred_element_type=jnp.float32
    )
    gate_grad = (
        hidden_grad * up_pre * sigmoid_val * (1.0 + gate_pre * (1.0 - sigmoid_val))
    ).astype(jnp.bfloat16)
    up_grad = (hidden_grad * activated).astype(jnp.bfloat16)
    input_grad = (
        lax.dot_general(
            gate_grad, gate_mat, (((1,), (1,)), ((), ())), preferred_element_type=jnp.float32
        )
        + lax.dot_general(
            up_grad, up_mat, (((1,), (1,)), ((), ())), preferred_element_type=jnp.float32
        )
    ).astype(jnp.bfloat16)
    grad_gate_w = contract_rows(block_in, gate_grad)
    grad_up_w = contract_rows(block_in, up_grad)
    grad_down_w = contract_rows(block_cot, hidden)
    return (input_grad, grad_gate_w, grad_up_w, grad_down_w)


def body(inputs, cotangent, w_gate, w_up, w_down, mom_gate, mom_up, mom_down):
    first = backward_block(inputs[0, 0], cotangent[0, 0], w_gate[0, 0], w_up[0, 0], w_down[0, 0])
    second = backward_block(inputs[0, 1], cotangent[0, 1], w_gate[0, 1], w_up[0, 1], w_down[0, 1])
    recv_first = from_behind(first[0], "section", -1)
    recv_second = from_behind(second[0], "section", 1)
    grad_in = jnp.stack([recv_first, recv_second])[None]
    second_rounded = jnp.stack([second[1], second[2], second[3]]).astype(jnp.bfloat16)
    bit_count = lax.axis_size("section").bit_length() - 1
    second_float = second_rounded.astype(jnp.float32)
    reduced = (
        lax.psum_scatter(
            first[1].astype(jnp.bfloat16), "dp", scatter_dimension=0, tiled=True
        ).astype(jnp.float32),
        lax.psum_scatter(
            first[2].astype(jnp.bfloat16), "dp", scatter_dimension=0, tiled=True
        ).astype(jnp.float32),
        lax.psum_scatter(
            first[3].astype(jnp.bfloat16), "dp", scatter_dimension=0, tiled=True
        ).astype(jnp.float32),
        lax.psum_scatter(
            second_float[0].astype(jnp.bfloat16), "dp", scatter_dimension=0, tiled=True
        ).astype(jnp.float32),
        lax.psum_scatter(
            second_float[1].astype(jnp.bfloat16), "dp", scatter_dimension=0, tiled=True
        ).astype(jnp.float32),
        lax.psum_scatter(
            second_float[2].astype(jnp.bfloat16), "dp", scatter_dimension=0, tiled=True
        ).astype(jnp.float32),
    )
    mirrored = jnp.stack([reduced[3], reduced[4], reduced[5]])
    for bit_index in range(bit_count):
        mirrored = from_partner(mirrored.astype(jnp.bfloat16), "section", bit_index).astype(
            mirrored.dtype
        )
    summed_gate = reduced[0] + mirrored[0]
    summed_up = reduced[1] + mirrored[1]
    summed_down = reduced[2] + mirrored[2]
    total_rows = inputs.shape[2] * lax.axis_size("dp")
    scale_factor = 1.0 / jnp.sqrt(jnp.float32(total_rows))
    new_gate = 0.9 * mom_gate[0] + summed_gate * scale_factor
    new_up = 0.9 * mom_up[0] + summed_up * scale_factor
    new_down = 0.9 * mom_down[0] + summed_down * scale_factor
    return (grad_in, new_gate[None], new_up[None], new_down[None])


def solution(mesh):
    placed = (
        P("section", None, "dp", None),
        P("section", None, "dp", None),
        P("section", None, None, None),
        P("section", None, None, None),
        P("section", None, None, None),
        P("section", "dp", None),
        P("section", "dp", None),
        P("section", "dp", None),
    )
    return jax.shard_map(
        body,
        mesh=mesh,
        in_specs=placed,
        out_specs=(
            P("section", None, "dp", None),
            P("section", "dp", None),
            P("section", "dp", None),
            P("section", "dp", None),
        ),
        check_vma=False,
    )
```

profile of v0, /device:TPU:0, one launch (start us, length us, event | category | flops | bytes accessed | tf_op | source)
XLA Modules:
  0.0 197.7 jit_solution(15021469634592396028)
XLA Ops:
  7.2 2.1 %fusion.10 = f32[256,256]{1,0:T(8,128)S(1)} fusion(bf16[1,2,2048,256]{3,2,1,0:T(8,128)(2,1)} %param.10, bf16[1,2,256,2048]{3,2,1,0:T(8,128)(2,1)} %param.8), kind=kOutput, calls=%fused_computation.19 | convolution fusion | flops 268435456 | bytes 2359296 | tf_op jit(solution)/shard_map/dot_general | solution.py:26
  9.4 1.8 fusion.13
  11.3 1.5 fusion.5
  12.8 2.0 %multiply_convert_fusion.2 = (bf16[256,256]{1,0:T(8,128)(2,1)S(1)}, bf16[256,256]{1,0:T(8,128)(2,1)S(1)}) fusion(f32[256,256]{1,0:T(8,128)S(1)} %fusion.10, f32[256,256]{1,0:T(8,128)S(1)} %fusion.13, bf16[1,2,256,2048]{3,2,1,0:T(8,128)(2,1)} %param.12, bf16[1,2,256,2048]{3,2,1,0:T(8,128)(2,1)} %param.9), kind=kOutput, calls=%fused_computation.87 | convolution fusion | flops 269287424 | bytes 2883584 | tf_op jit(solution)/shard_map/dot_general | solution.py:31
  14.9 1.5 fusion.4
  16.4 1.4 fusion.3
  17.9 1.8 fusion.25
  21.4 1.5 fusion.7
  23.0 2.0 %multiply_convert_fusion.4 = (bf16[256,256]{1,0:T(8,128)(2,1)S(1)}, bf16[256,256]{1,0:T(8,128)(2,1)S(1)}) fusion(f32[256,256]{1,0:T(8,128)S(1)} %fusion.25, f32[256,256]{1,0:T(8,128)S(1)} %fusion.28, bf16[1,2,256,2048]{3,2,1,0:T(8,128)(2,1)} %param.12, bf16[1,2,256,2048]{3,2,1,0:T(8,128)(2,1)} %param.9), kind=kOutput, calls=%fused_computation.91 | convolution fusion | flops 269287424 | bytes 2883584 | tf_op jit(solution)/shard_map/dot_general | solution.py:31
  25.0 1.5 fusion.6
  28.0 14.8 %reduce-scatter.13.cloned.1.call-done = bf16[512,256]{0,1:T(8,128)(2,1)} async-done(((bf16[2048,256]{0,1:T(8,128)(2,1)}), bf16[512,256]{0,1:T(8,128)(2,1)}) %reduce-scatter.13.cloned.1.call-update) | async-done | bytes 262160 | tf_op jit(solution)/shard_map/reduce_scatter | solution.py:77
  42.8 28.2 %reduce-scatter.11.cloned.1.call-done = bf16[512,256]{0,1:T(8,128)(2,1)} async-done(((bf16[2048,256]{0,1:T(8,128)(2,1)}), bf16[512,256]{0,1:T(8,128)(2,1)}) %reduce-scatter.11.cloned.1.call-update) | async-done | bytes 262160 | tf_op jit(solution)/shard_map/reduce_scatter | solution.py:74
  71.0 28.1 %reduce-scatter.9.cloned.1.call-done = bf16[512,256]{0,1:T(8,128)(2,1)} async-done(((bf16[2048,256]{0,1:T(8,128)(2,1)}), bf16[512,256]{0,1:T(8,128)(2,1)}) %reduce-scatter.9.cloned.1.call-update) | async-done | bytes 262160 | tf_op jit(solution)/shard_map/reduce_scatter | solution.py:71
  101.0 1.5 fusion
  104.3 2.8 %collective-permute-start.3 = (bf16[3,512,256]{1,2,0:T(8,128)(2,1)S(1)}, bf16[3,512,256]{1,2,0:T(8,128)(2,1)}, u32[]{:S(2)}, u32[]{:S(2)}) collective-permute-start(bf16[3,512,256]{1,2,0:T(8,128)(2,1)S(1)} %collective-permute-done.2), channel_id=1, source_target_pairs={{0,8},{4,12},{8,0},{12,4},{16,24},{20,28},{24,16},{28,20},{1,9},{5... | collective-permute-start | bytes 2359304 | tf_op jit(solution)/shard_map/ppermute | solution.py:16
  107.1 1.5 fusion.1
  108.6 2.6 %collective-permute-start.1 = (bf16[256,2048]{1,0:T(8,128)(2,1)}, bf16[256,2048]{1,0:T(8,128)(2,1)}, u32[]{:S(2)}, u32[]{:S(2)}) collective-permute-start(bf16[256,2048]{1,0:T(8,128)(2,1)} %fusion.1), channel_id=1, source_target_pairs={{0,4},{4,8},{8,12},{12,16},{16,20},{20,24},{24,28},{1,5},{5,9},{9,... | collective-permute-start | bytes 3145736 | tf_op jit(solution)/shard_map/ppermute | solution.py:10
  111.2 36.4 %collective-permute-done.3 = bf16[3,512,256]{1,2,0:T(8,128)(2,1)} collective-permute-done((bf16[3,512,256]{1,2,0:T(8,128)(2,1)S(1)}, bf16[3,512,256]{1,2,0:T(8,128)(2,1)}, u32[]{:S(2)}, u32[]{:S(2)}) %collective-permute-start.3) | collective-permute-done | bytes 786464 | tf_op jit(solution)/shard_map/ppermute | solution.py:16
  148.6 2.7 %maximum_bitcast_fusion = bf16[1,2,256,2048]{3,2,1,0:T(8,128)(2,1)} fusion(bf16[1,256,2048]{2,1,0:T(8,128)(2,1)} %bitcast.11, bf16[1,256,2048]{2,1,0:T(8,128)(2,1)S(1)} %bitcast.131), kind=kLoop, calls=%fused_computation.16 | loop fusion | flops 1048576 | bytes 4194304 | tf_op jit(solution)/shard_map/broadcast_in_dim | solution.py:57
  151.3 8.5 %collective-permute-done.4 = bf16[3,512,256]{1,2,0:T(8,128)(2,1)} collective-permute-done((bf16[3,512,256]{1,2,0:T(8,128)(2,1)}, bf16[3,512,256]{1,2,0:T(8,128)(2,1)}, u32[]{:S(2)}, u32[]{:S(2)}) %collective-permute-start.4) | collective-permute-done | bytes 786464 | tf_op jit(solution)/shard_map/ppermute | solution.py:16
  161.2 22.0 %reduce-scatter.7.cloned.1.call-done = bf16[512,256]{0,1:T(8,128)(2,1)} async-done(((bf16[2048,256]{0,1:T(8,128)(2,1)}), bf16[512,256]{0,1:T(8,128)(2,1)}) %reduce-scatter.7.cloned.1.call-update) | async-done | bytes 262160 | tf_op jit(solution)/shard_map/reduce_scatter | solution.py:62
  183.2 2.5 %fusion.63 = (f32[1,512,256]{1,2,0:T(8,128)}, f32[1,512,256]{1,2,0:T(8,128)}, f32[1,512,256]{1,2,0:T(8,128)}) fusion(f32[3,512,256]{1,2,0:T(8,128)S(1)} %convert_element_type.80, bf16[512,256]{0,1:T(8,128)(2,1)} %reduce-scatter.17.cloned.1.call-done, f32[1,512,256]{1,2,0:T(8,128)S(1)} %copy.14, bf16[512,256]{0,1:T(8,128)(2,1)} %reduce-scatter.15.cloned.1.call-done, ...), kind=kLoop, calls=%fused_computation.74 | loop fusion | flops 1966080 | bytes 5505024 | tf_op jit(solution)/shard_map/broadcast_in_dim | solution.py:94
  185.7 2.1 %copy.17 = f32[1,512,256]{2,1,0:T(8,128)} copy(f32[1,512,256]{1,2,0:T(8,128)} %get-tuple-element.8) | data formatting | bytes 1048576
  187.8 2.0 %copy.16 = f32[1,512,256]{2,1,0:T(8,128)} copy(f32[1,512,256]{1,2,0:T(8,128)} %get-tuple-element.9) | data formatting | bytes 1048576
  (50 shorter events, 10.6 us)
Async XLA Ops:
  7.2 2.2 %copy-start = (bf16[1,2,256,2048]{3,2,1,0:T(8,128)(2,1)S(1)}, bf16[1,2,256,2048]{3,2,1,0:T(8,128)(2,1)}, u32[]{:S(2)}) copy-start(bf16[1,2,256,2048]{3,2,1,0:T(8,128)(2,1)} %param.8) | copy-start | bytes 6291460
  7.2 35.6 %reduce-scatter.13.cloned.1.call-start = ((), (), s32[]{:S(2)}) async-start(), calls=%async_computation.9 | async-start | bytes 1310720 | tf_op jit(solution)/shard_map/reduce_scatter | solution.py:77
  9.4 1.9 copy-start.8
  12.8 58.2 %reduce-scatter.11.cloned.1.call-start = ((), (), s32[]{:S(2)}) async-start(), calls=%async_computation.8 | async-start | bytes 1310720 | tf_op jit(solution)/shard_map/reduce_scatter | solution.py:74
  16.3 82.7 %reduce-scatter.9.cloned.1.call-start = ((), (), s32[]{:S(2)}) async-start(), calls=%async_computation.7 | async-start | bytes 1310720 | tf_op jit(solution)/shard_map/reduce_scatter | solution.py:71
  17.9 143.3 %reduce-scatter.17.cloned.1.call-start = ((), (), s32[]{:S(2)}) async-start(), calls=%async_computation.11 | async-start | bytes 1310720 | tf_op jit(solution)/shard_map/reduce_scatter | solution.py:68
  17.9 1.9 copy-start.2
  19.8 1.6 copy-start.9
  22.9 138.3 %reduce-scatter.15.cloned.1.call-start = ((), (), s32[]{:S(2)}) async-start(), calls=%async_computation.10 | async-start | bytes 1310720 | tf_op jit(solution)/shard_map/reduce_scatter | solution.py:65
  26.5 156.8 %reduce-scatter.7.cloned.1.call-start = ((), (), s32[]{:S(2)}) async-start(), calls=%async_computation.6 | async-start | bytes 1310720 | tf_op jit(solution)/shard_map/reduce_scatter | solution.py:62
  28.0 72.6 %copy-start.1 = (bf16[1,2,2048,256]{3,2,1,0:T(8,128)(2,1)S(1)}, bf16[1,2,2048,256]{3,2,1,0:T(8,128)(2,1)}, u32[]{:S(2)}) copy-start(bf16[1,2,2048,256]{3,2,1,0:T(8,128)(2,1)} %param.10) | copy-start | bytes 6291460
  99.1 1.9 copy-start.3
  100.4 3.8 %collective-permute-start.2 = (bf16[3,512,256]{1,2,0:T(8,128)(2,1)S(1)}, bf16[3,512,256]{1,2,0:T(8,128)(2,1)S(1)}, u32[]{:S(2)}, u32[]{:S(2)}) collective-permute-start(bf16[3,512,256]{1,2,0:T(8,128)(2,1)S(1)} %pad_maximum_fusion), channel_id=1, source_target_pairs={{0,4},{4,0},{8,12},{12,8},{16,20},{20,16},{24,28},{28,24},{1,5},{5... | collective-permute-start | bytes 2359304 | tf_op jit(solution)/shard_map/ppermute | solution.py:16
  102.5 46.1 %collective-permute-start = (bf16[256,2048]{1,0:T(8,128)(2,1)}, bf16[256,2048]{1,0:T(8,128)(2,1)S(1)}, u32[]{:S(2)}, u32[]{:S(2)}) collective-permute-start(bf16[256,2048]{1,0:T(8,128)(2,1)} %fusion), channel_id=1, source_target_pairs={{4,0},{8,4},{12,8},{16,12},{20,16},{24,20},{28,24},{5,1},{9,5},{13... | collective-permute-start | bytes 3145736 | tf_op jit(solution)/shard_map/ppermute | solution.py:10
  104.3 43.7 %copy-start.5 = (f32[1,512,256]{2,1,0:T(8,128)S(1)}, f32[1,512,256]{2,1,0:T(8,128)}, u32[]{:S(2)}) copy-start(f32[1,512,256]{2,1,0:T(8,128)} %param.13) | copy-start | bytes 1572868
  104.3 43.9 %copy-start.6 = (f32[1,512,256]{2,1,0:T(8,128)S(1)}, f32[1,512,256]{2,1,0:T(8,128)}, u32[]{:S(2)}) copy-start(f32[1,512,256]{2,1,0:T(8,128)} %param.14) | copy-start | bytes 1572868
  104.3 43.2 %collective-permute-start.3 = (bf16[3,512,256]{1,2,0:T(8,128)(2,1)S(1)}, bf16[3,512,256]{1,2,0:T(8,128)(2,1)}, u32[]{:S(2)}, u32[]{:S(2)}) collective-permute-start(bf16[3,512,256]{1,2,0:T(8,128)(2,1)S(1)} %collective-permute-done.2), channel_id=1, source_target_pairs={{0,8},{4,12},{8,0},{12,4},{16,24},{20,28},{24,16},{28,20},{1,9},{5... | collective-permute-start | bytes 2359304 | tf_op jit(solution)/shard_map/ppermute | solution.py:16
  108.6 39.8 %copy-start.7 = (f32[1,512,256]{2,1,0:T(8,128)S(1)}, f32[1,512,256]{2,1,0:T(8,128)}, u32[]{:S(2)}) copy-start(f32[1,512,256]{2,1,0:T(8,128)} %param.15) | copy-start | bytes 1572868
  108.6 40.0 %collective-permute-start.1 = (bf16[256,2048]{1,0:T(8,128)(2,1)}, bf16[256,2048]{1,0:T(8,128)(2,1)}, u32[]{:S(2)}, u32[]{:S(2)}) collective-permute-start(bf16[256,2048]{1,0:T(8,128)(2,1)} %fusion.1), channel_id=1, source_target_pairs={{0,4},{4,8},{8,12},{12,16},{16,20},{20,24},{24,28},{1,5},{5,9},{9,... | collective-permute-start | bytes 3145736 | tf_op jit(solution)/shard_map/ppermute | solution.py:10
  147.5 12.3 %collective-permute-start.4 = (bf16[3,512,256]{1,2,0:T(8,128)(2,1)}, bf16[3,512,256]{1,2,0:T(8,128)(2,1)}, u32[]{:S(2)}, u32[]{:S(2)}) collective-permute-start(bf16[3,512,256]{1,2,0:T(8,128)(2,1)} %collective-permute-done.3), channel_id=1, source_target_pairs={{0,16},{4,20},{8,24},{12,28},{16,0},{20,4},{24,8},{28,12},{1,17},{... | collective-permute-start | bytes 2359304 | tf_op jit(solution)/shard_map/ppermute | solution.py:16
  185.7 4.1 %copy-start.4 = (f32[1,512,256]{1,2,0:T(8,128)S(1)}, f32[1,512,256]{1,2,0:T(8,128)}, u32[]{:S(2)}) copy-start(f32[1,512,256]{1,2,0:T(8,128)} %get-tuple-element.10) | copy-start | bytes 1572868
Sparse Core Ops, SparseCore 0:
  12.9 29.8 reduce-scatter.12
  45.2 25.7 reduce-scatter.10
  73.3 25.7 reduce-scatter.8
  101.3 25.8 reduce-scatter.16
  129.3 25.7 reduce-scatter.14
  157.4 25.8 reduce-scatter.6
where the time goes:
time: 198 us
  waiting for transfers between devices  138 us (70%)
  matrix products  22.8 us (12%)
  between operations  14.3 us (7%)
  other arithmetic  7.9 us (4%)
  starting transfers between devices  7.42 us (4%)
  local copies, waits for them, and re-layouts  7.11 us (4%)
    ppermute x3, waiting for transfers between devices, from_partner(): return lax.ppermute(value, axis, pairs)  44.8 us
    reduce_scatter x1, waiting for transfers between devices, body(): lax.psum_scatter(second_float[1].astype(jnp.bfloat16), 'dp', scatter_dime...  28.2 us
    reduce_scatter x1, waiting for transfers between devices, body(): lax.psum_scatter(second_float[0].astype(jnp.bfloat16), 'dp', scatter_dime...  28.1 us
    reduce_scatter x1, waiting for transfers between devices, body(): lax.psum_scatter(first[1].astype(jnp.bfloat16), 'dp', scatter_dimension=0...  22 us
    reduce_scatter x1, waiting for transfers between devices, body(): lax.psum_scatter(second_float[2].astype(jnp.bfloat16), 'dp', scatter_dime...  14.8 us
    dot_general x6, matrix products, contract_rows(): lax.dot_general(left, right, (((0,), (0,)), ((), ())), preferred_element_...  8.73 us
    unnamed x26, local copies, waits for them, and re-layouts  7.11 us
    dot_general x2, matrix products, backward_block(): lax.dot_general(block_cot, down_mat, (((1,), (1,)), ((), ())), preferred_...  4.05 us
  transfers between devices with their start and end apart: 11, of which 6 were waited for; matrix products, arithmetic and copies ran while one was open for 12% of the time, Pallas kernels for 0%

commit v1 on v0

v1 whole, which is shorter than its diff:
```python
import functools
import math

import jax
import jax.numpy as jnp
from jax import lax
from jax.experimental import pallas as pl
from jax.experimental.pallas import tpu as pltpu
from jax.sharding import PartitionSpec as P

BF16 = jnp.bfloat16
F32 = jnp.float32
VMEM_LIMIT = 48 * 1024 * 1024


def rows_dot(left, right):
    return lax.dot_general(left, right, (((0,), (0,)), ((), ())), preferred_element_type=F32)


def cols_dot(left, right):
    return lax.dot_general(left, right, (((1,), (1,)), ((), ())), preferred_element_type=F32)


def slot_offsets(count):
    bits = count.bit_length() - 1
    return [sum(((p >> i) & 1) << (bits - 1 - i) for i in range(bits)) for p in range(count)]


def block_kernel(offsets, shard, mine, x_ref, y_ref, wg_ref, wu_ref, wd_ref, dgu_ref, pd_ref, dx_ref):
    ff = wg_ref.shape[3]
    x, y = x_ref[0, 0], y_ref[0, 0]
    gate = jnp.dot(x, wg_ref[0, 0], preferred_element_type=F32)
    up = jnp.dot(x, wu_ref[0, 0], preferred_element_type=F32)
    sig = jax.nn.sigmoid(gate)
    act = gate * sig
    hidden = (act * up).astype(BF16)
    dhid = cols_dot(y, wd_ref[0, 0])
    dgate = (dhid * up * sig * (1.0 + gate * (1.0 - sig))).astype(BF16)
    dup = (dhid * act).astype(BF16)
    dgu_ref[0, :, :ff] = dgate
    dgu_ref[0, :, ff:] = dup
    hidden_t = hidden.T
    for slot, offset in enumerate(offsets):
        start = pl.multiple_of((mine[0] ^ offset) * shard, shard)
        columns = y_ref[0, 0, :, pl.ds(start, shard)]
        pd_ref[0, slot] = jnp.dot(hidden_t, columns, preferred_element_type=F32).astype(BF16)
    width = x_ref.shape[3]
    step = min(512, width)
    for at in range(0, width, step):
        rows = pl.ds(at, step)
        dx_ref[0, :, rows] = (
            cols_dot(dgate, wg_ref[0, 0, rows, :]) + cols_dot(dup, wu_ref[0, 0, rows, :])
        ).astype(BF16)


def blocks(mine, inputs, cotangent, w_gate, w_up, w_down, offsets, shard):
    _, _, rows, width = inputs.shape
    ff = w_gate.shape[3]
    count = len(offsets)
    whole = lambda b, z: (0, b, 0, 0)
    return pl.pallas_call(
        functools.partial(block_kernel, offsets, shard),
        out_shape=(
            jax.ShapeDtypeStruct((2, rows, 2 * ff), BF16),
            jax.ShapeDtypeStruct((2, count, ff, shard), BF16),
            jax.ShapeDtypeStruct((2, rows, width), BF16),
        ),
        grid_spec=pltpu.PrefetchScalarGridSpec(
            num_scalar_prefetch=1,
            grid=(2,),
            in_specs=[
                pl.BlockSpec((1, 1, rows, width), whole),
                pl.BlockSpec((1, 1, rows, width), whole),
                pl.BlockSpec((1, 1, width, ff), whole),
                pl.BlockSpec((1, 1, width, ff), whole),
                pl.BlockSpec((1, 1, ff, width), whole),
            ],
            out_specs=[
                pl.BlockSpec((1, rows, 2 * ff), lambda b, z: (b, 0, 0)),
                pl.BlockSpec((1, count, ff, shard), lambda b, z: (b, 0, 0, 0)),
                pl.BlockSpec((1, rows, width), lambda b, z: (b, 0, 0)),
            ],
        ),
        compiler_params=pltpu.CompilerParams(vmem_limit_bytes=VMEM_LIMIT),
        name="blocks",
    )(mine, inputs, cotangent, w_gate, w_up, w_down)


def pair_kernel(mine, x0_ref, x1_ref, d0_ref, d1_ref, gate_ref, up_ref):
    ff = gate_ref.shape[1]
    x0, x1 = x0_ref[0, 0], x1_ref[0]
    for out, at in ((gate_ref, 0), (up_ref, ff)):
        out[0] = (rows_dot(d0_ref[0, :, at : at + ff], x0) + rows_dot(d1_ref[:, at : at + ff], x1)).astype(BF16)


def pair(mine, inputs, mirrored_x, dgu, mirrored_dgu, offsets, shard):
    _, _, rows, _ = inputs.shape
    ff = dgu.shape[2] // 2
    count = len(offsets)

    def column(j, z):
        offset = sum(jnp.where(j == i, o, 0) for i, o in enumerate(offsets))
        return (0, 0, 0, z[0] ^ offset)

    return pl.pallas_call(
        pair_kernel,
        out_shape=(jax.ShapeDtypeStruct((count, ff, shard), BF16),) * 2,
        grid_spec=pltpu.PrefetchScalarGridSpec(
            num_scalar_prefetch=1,
            grid=(count,),
            in_specs=[
                pl.BlockSpec((1, 1, rows, shard), column),
                pl.BlockSpec((1, rows, shard), lambda j, z: (j, 0, 0)),
                pl.BlockSpec((1, rows, 2 * ff), lambda j, z: (0, 0, 0)),
                pl.BlockSpec((rows, 2 * ff), lambda j, z: (0, 0)),
            ],
            out_specs=[pl.BlockSpec((1, ff, shard), lambda j, z: (j, 0, 0))] * 2,
        ),
        compiler_params=pltpu.CompilerParams(vmem_limit_bytes=VMEM_LIMIT),
        name="pair",
    )(mine, inputs, mirrored_x, dgu, mirrored_dgu)


def momentum_kernel(scale, mom_ref, *refs):
    out_ref = refs[-1]
    total = refs[0][0].astype(F32)
    for ref in refs[1:-1]:
        total = total + ref[0].astype(F32)
    out_ref[0] = 0.9 * mom_ref[0] + total.T * scale


def momentum(mom, parts, scale):
    _, shard, ff = mom.shape
    return pl.pallas_call(
        functools.partial(momentum_kernel, scale),
        out_shape=jax.ShapeDtypeStruct(mom.shape, F32),
        grid=(1,),
        in_specs=[pl.BlockSpec((1, shard, ff), lambda i: (0, 0, 0))]
        + [pl.BlockSpec((1, ff, shard), lambda i: (0, 0, 0))] * len(parts),
        out_specs=pl.BlockSpec((1, shard, ff), lambda i: (0, 0, 0)),
        compiler_params=pltpu.CompilerParams(vmem_limit_bytes=VMEM_LIMIT),
        name="momentum",
    )(mom, *parts)


def shifted(value, steps):
    count = lax.axis_size("section")
    first, last = max(0, -steps), min(count, count - steps)
    return lax.ppermute(value, "section", [(i, i + steps) for i in range(first, last)])


def mirrored(value):
    count = lax.axis_size("section")
    return lax.ppermute(value, "section", [(i, count - 1 - i) for i in range(count)])


def swapped(value, mask):
    return lax.ppermute(value, "dp", [(i, i ^ mask) for i in range(lax.axis_size("dp"))])


def halve(keep, received):
    half = keep.shape[0] // 2
    add = lambda a, b: (a.astype(F32) + b.astype(F32)).astype(BF16)
    return keep[:half], received[:half], add(keep[half:], received[half:])


def body(inputs, cotangent, w_gate, w_up, w_down, mom_gate, mom_up, mom_down):
    replicas = lax.axis_size("dp")
    _, _, rows, width = inputs.shape
    shard = width // replicas
    offsets = slot_offsets(replicas)
    half = replicas // 2
    z = lax.axis_index("dp")
    mine = z[None]
    scale = 1.0 / math.sqrt(rows * replicas)

    def columns(value, chosen):
        return jnp.stack([lax.dynamic_slice_in_dim(value, (z ^ o) * shard, shard, 1) for o in chosen])

    x_send = mirrored(columns(inputs[0, 1], offsets[half:]))
    dgu, pd, dx = blocks(mine, inputs, cotangent, w_gate, w_up, w_down, offsets, shard)
    dgu_mirror = mirrored(dgu[1])
    x_keep = mirrored(columns(inputs[0, 1], offsets[:half]))
    pd_mirror = mirrored(pd[1])
    add = lambda a, b: (a.astype(F32) + b.astype(F32)).astype(BF16)
    gate_send, up_send = pair(mine, inputs, x_send, dgu, dgu_mirror, offsets[half:], shard)
    gate_keep, up_keep = pair(mine, inputs, x_keep, dgu, dgu_mirror, offsets[:half], shard)
    down_send = add(pd[0, half:], pd_mirror[half:])
    down_keep = add(pd[0, :half], pd_mirror[:half])
    recv0 = shifted(dx[0], -1)
    recv1 = shifted(dx[1], 1)
    results = []
    for mom, keep, send in (
        (mom_gate, gate_keep, gate_send),
        (mom_up, up_keep, up_send),
        (mom_down, down_keep, down_send),
    ):
        mask = 1
        while mask < replicas:
            received = swapped(send, mask)
            m = keep.shape[0] // 2
            if m:
                send = add(keep[m:], received[m:])
                keep = add(keep[:m], received[:m])
            else:
                results.append(momentum(mom, (keep, received), scale))
            mask *= 2
    grad_in = jnp.stack([recv0, recv1])[None]
    return (grad_in, *results)


def solution(mesh):
    tokens = P("section", None, "dp", None)
    weights = P("section", None, None, None)
    moments = P("section", "dp", None)
    return jax.shard_map(
        body,
        mesh=mesh,
        in_specs=(tokens, tokens, weights, weights, weights, moments, moments, moments),
        out_specs=(tokens, moments, moments, moments),
        check_vma=False,
    )
```

time: 198 us -> 112 us (0.57)
  waiting for transfers between devices: 138 us -> 74.2 us
  matrix products: 22.8 us -> 0 us
  between operations: 14.3 us -> 0.81 us
  starting transfers between devices: 7.42 us -> 20.9 us
  Pallas kernels: 0 us -> 11.5 us
  other arithmetic: 7.9 us -> 2.32 us
  local copies, waits for them, and re-layouts: 7.11 us -> 1.65 us
    reduce_scatter x6 -> x0, waiting for transfers between devices: 93.2 us -> none  [the longest x1 28.2 us: body(): lax.psum_scatter(second_float[1].astype(jnp.bfloat16), 'dp', scatter_dime...]
    ppermute x5 -> x12, waiting for transfers between devices: 44.9 us -> 74.2 us  [the longest x6 40.7 us: swapped(): lax.ppermute(value, 'dp', [(i, i ^ mask) for i in range(lax.axis_size('dp...]
    dot_general x16 -> x0, matrix products: 22.8 us -> none  [the longest x6 8.73 us: contract_rows(): lax.dot_general(left, right, (((0,), (0,)), ((), ())), preferred_element_...]
    ppermute x5 -> x12, starting transfers between devices: 7.17 us -> 20.9 us  [the longest x6 10.2 us: swapped(): lax.ppermute(value, 'dp', [(i, i ^ mask) for i in range(lax.axis_size('dp...]
    pallas_call x0 -> x6, Pallas kernels: none -> 11.5 us  [the longest x1 6.52 us: blocks(): pl.pallas_call(functools.partial(block_kernel, offsets, shard), out_shape...]
    unnamed x26 -> x8, local copies, waits for them, and re-layouts: 7.11 us -> 0.02 us
    broadcast_in_dim x2 -> x1, other arithmetic: 5.22 us -> 1.5 us  [body(): grad_in = jnp.stack([recv0, recv1])[None]]
  transfers between devices with their start and end apart: 11 -> 12, of which waited for: 6 -> 7; matrix products, arithmetic and copies ran while one was open for 12% -> 2% of each run, Pallas kernels for 0% -> 9%
where the time goes in v1:
time: 112 us; the launch traced here: 111 us
  waiting for transfers between devices  74.2 us (66%)
  starting transfers between devices  20.9 us (19%)
  Pallas kernels  11.5 us (10%)
  other arithmetic  2.32 us (2%)
  local copies, waits for them, and re-layouts  1.65 us (1%)
    ppermute x6, waiting for transfers between devices, swapped(): lax.ppermute(value, 'dp', [(i, i ^ mask) for i in range(lax.axis_size('dp...  40.7 us
    ppermute x4, waiting for transfers between devices, mirrored(): lax.ppermute(value, 'section', [(i, count - 1 - i) for i in range(count)])  33.5 us
    ppermute x6, starting transfers between devices, swapped(): lax.ppermute(value, 'dp', [(i, i ^ mask) for i in range(lax.axis_size('dp...  10.2 us
    pallas_call x1, Pallas kernels, blocks(): pl.pallas_call(functools.partial(block_kernel, offsets, shard), out_shape...  6.52 us
    ppermute x4, starting transfers between devices, mirrored(): lax.ppermute(value, 'section', [(i, count - 1 - i) for i in range(count)])  6.27 us
    ppermute x2, starting transfers between devices, shifted(): lax.ppermute(value, 'section', [(i, i + steps) for i in range(first, last)])  4.39 us
    pallas_call x3, Pallas kernels, momentum(): pl.pallas_call(functools.partial(momentum_kernel, scale), out_shape=jax.S...  3 us
  transfers between devices with their start and end apart: 12, of which 7 were waited for; matrix products, arithmetic and copies ran while one was open for 2% of the time, Pallas kernels for 9%

profile of v1, /device:TPU:0, one launch (start us, length us, event | category | flops | bytes accessed | tf_op | source)
XLA Modules:
  0.0 111.4 jit_solution(4147653195421941314)
XLA Ops:
  0.7 1.2 %slice-done = bf16[1,1,256,2048]{3,2,1,0:T(8,128)(2,1)S(1)} async-done(((bf16[1,2,256,2048]{3,2,1,0:T(8,128)(2,1)}), bf16[1,1,256,2048]{3,2,1,0:T(8,128)(2,1)S(1)}, s32[]{:S(2)}) %slice-start) | async-done | bytes 1048600 | tf_op jit(solution)/shard_map/slice | solution.py:183
  2.0 3.4 %collective-permute-start.4 = (bf16[2,256,512]{2,1,0:T(8,128)(2,1)S(1)}, bf16[2,256,512]{2,1,0:T(8,128)(2,1)S(1)}, u32[]{:S(2)}, u32[]{:S(2)}) collective-permute-start(bf16[2,256,512]{2,1,0:T(8,128)(2,1)S(1)} %pad_maximum_fusion.1), channel_id=1, source_target_pairs={{0,28},{4,24},{8,20},{12,16},{16,12},{20,8},{24,4},{28,0},{1,29},{... | collective-permute-start | bytes 1572872 | tf_op jit(solution)/shard_map/ppermute | solution.py:154
  5.4 6.5 %blocks.1 = (bf16[2,256,512]{2,1,0:T(8,128)(2,1)S(1)}, bf16[2,4,256,512]{3,2,1,0:T(8,128)(2,1)S(1)}, bf16[2,256,2048]{2,1,0:T(8,128)(2,1)S(1)}) custom-call(s32[1]{0:T(128)} %bitcast.mine, bf16[1,2,256,2048]{3,2,1,0:T(8,128)(2,1)} %x0_ref.3, bf16[1,2,256,2048]{3,2,1,0:T(8,128)(2,1)} %y_ref.1, bf16[1,2,2048,256]{3,2,1,0:T(8,128)(2,1)} %wg_ref.1, ...), custom_call_target="tpu_custom_call" | custom-call | tf_op jit(solution)/shard_map/blocks/pallas_call | solution.py:61
  12.2 2.7 %collective-permute-start.3 = (bf16[256,512]{1,0:T(8,128)(2,1)S(1)}, bf16[256,512]{1,0:T(8,128)(2,1)S(1)}, u32[]{:S(2)}, u32[]{:S(2)}) collective-permute-start(bf16[256,512]{1,0:T(8,128)(2,1)S(1)} %slice_bitcast_fusion.3), channel_id=1, source_target_pairs={{0,28},{4,24},{8,20},{12,16},{16,12},{20,8},{24,4},{28,0},{1,29},{... | collective-permute-start | bytes 786440 | tf_op jit(solution)/shard_map/ppermute | solution.py:154
  15.0 30.8 %collective-permute-done.3.d1_ref = bf16[256,512]{1,0:T(8,128)(2,1)S(1)} collective-permute-done((bf16[256,512]{1,0:T(8,128)(2,1)S(1)}, bf16[256,512]{1,0:T(8,128)(2,1)S(1)}, u32[]{:S(2)}, u32[]{:S(2)}) %collective-permute-start.3) | collective-permute-done | bytes 262176 | tf_op jit(solution)/shard_map/ppermute | solution.py:154
  45.8 1.0 pair.3
  46.9 2.5 %collective-permute-start.7 = (bf16[2,256,512]{2,1,0:T(8,128)(2,1)S(1)}, bf16[2,256,512]{2,1,0:T(8,128)(2,1)S(1)}, u32[]{:S(2)}, u32[]{:S(2)}) collective-permute-start(bf16[2,256,512]{2,1,0:T(8,128)(2,1)S(1)} %get-tuple-element.16), channel_id=1, source_target_pairs={{0,1},{1,0},{2,3},{3,2},{4,5},{5,4},{6,7},{7,6},{8,9},{9,8},{10,11... | collective-permute-start | bytes 1572872 | tf_op jit(solution)/shard_map/ppermute | solution.py:158
  49.6 1.3 %collective-permute-start = (bf16[256,2048]{1,0:T(8,128)(2,1)S(1)}, bf16[256,2048]{1,0:T(8,128)(2,1)S(1)}, u32[]{:S(2)}, u32[]{:S(2)}) collective-permute-start(bf16[256,2048]{1,0:T(8,128)(2,1)S(1)} %get-tuple-element.20), channel_id=1, source_target_pairs={{4,0},{8,4},{12,8},{16,12},{20,16},{24,20},{28,24},{5,1},{9,5},{13... | collective-permute-start | bytes 3145736 | tf_op jit(solution)/shard_map/ppermute | solution.py:149
  50.9 3.1 %collective-permute-start.1 = (bf16[256,2048]{1,0:T(8,128)(2,1)S(1)}, bf16[256,2048]{1,0:T(8,128)(2,1)S(1)}, u32[]{:S(2)}, u32[]{:S(2)}) collective-permute-start(bf16[256,2048]{1,0:T(8,128)(2,1)S(1)} %get-tuple-element.21), channel_id=1, source_target_pairs={{0,4},{4,8},{8,12},{12,16},{16,20},{20,24},{24,28},{1,5},{5,9},{9,... | collective-permute-start | bytes 3145736 | tf_op jit(solution)/shard_map/ppermute | solution.py:149
  54.1 0.3 fusion.1
  54.4 2.7 %collective-permute-done.2.x1_ref = bf16[2,256,512]{2,1,0:T(8,128)(2,1)S(1)} collective-permute-done((bf16[2,256,512]{2,1,0:T(8,128)(2,1)S(1)}, bf16[2,256,512]{2,1,0:T(8,128)(2,1)S(1)}, u32[]{:S(2)}, u32[]{:S(2)}) %collective-permute-start.2) | collective-permute-done | bytes 524320 | tf_op jit(solution)/shard_map/ppermute | solution.py:154
  57.1 2.4 %collective-permute-start.10 = (bf16[2,256,512]{2,1,0:T(8,128)(2,1)S(1)}, bf16[2,256,512]{2,1,0:T(8,128)(2,1)S(1)}, u32[]{:S(2)}, u32[]{:S(2)}) collective-permute-start(bf16[2,256,512]{2,1,0:T(8,128)(2,1)S(1)} %get-tuple-element.19), channel_id=1, source_target_pairs={{0,1},{1,0},{2,3},{3,2},{4,5},{5,4},{6,7},{7,6},{8,9},{9,8},{10,11... | collective-permute-start | bytes 1572872 | tf_op jit(solution)/shard_map/ppermute | solution.py:158
  59.5 1.0 pair.2
  60.5 1.6 %collective-permute-done.7 = bf16[2,256,512]{2,1,0:T(8,128)(2,1)S(1)} collective-permute-done((bf16[2,256,512]{2,1,0:T(8,128)(2,1)S(1)}, bf16[2,256,512]{2,1,0:T(8,128)(2,1)S(1)}, u32[]{:S(2)}, u32[]{:S(2)}) %collective-permute-start.7) | collective-permute-done | bytes 524320 | tf_op jit(solution)/shard_map/ppermute | solution.py:158
  62.2 3.1 %collective-permute-start.8 = (bf16[1,256,512]{2,1,0:T(8,128)(2,1)S(1)}, bf16[1,256,512]{2,1,0:T(8,128)(2,1)S(1)}, u32[]{:S(2)}, u32[]{:S(2)}) collective-permute-start(bf16[1,256,512]{2,1,0:T(8,128)(2,1)S(1)} %get-tuple-element.24), channel_id=1, source_target_pairs={{0,2},{1,3},{2,0},{3,1},{4,6},{5,7},{6,4},{7,5},{8,10},{9,11},{10,... | collective-permute-start | bytes 786440 | tf_op jit(solution)/shard_map/ppermute | solution.py:158
  65.3 13.6 %collective-permute-done.5 = bf16[2,256,512]{2,1,0:T(8,128)(2,1)S(1)} collective-permute-done((bf16[2,256,512]{2,1,0:T(8,128)(2,1)S(1)}, bf16[2,256,512]{2,1,0:T(8,128)(2,1)S(1)}, u32[]{:S(2)}, u32[]{:S(2)}) %collective-permute-start.5) | collective-permute-done | bytes 524320 | tf_op jit(solution)/shard_map/ppermute | solution.py:158
  79.1 2.2 %collective-permute-start.6 = (bf16[1,256,512]{2,1,0:T(8,128)(2,1)S(1)}, bf16[1,256,512]{2,1,0:T(8,128)(2,1)S(1)}, u32[]{:S(2)}, u32[]{:S(2)}) collective-permute-start(bf16[1,256,512]{2,1,0:T(8,128)(2,1)S(1)} %get-tuple-element.26), channel_id=1, source_target_pairs={{0,2},{1,3},{2,0},{3,1},{4,6},{5,7},{6,4},{7,5},{8,10},{9,11},{10,... | collective-permute-start | bytes 786440 | tf_op jit(solution)/shard_map/ppermute | solution.py:158
  81.2 12.9 %collective-permute-done.10 = bf16[2,256,512]{2,1,0:T(8,128)(2,1)S(1)} collective-permute-done((bf16[2,256,512]{2,1,0:T(8,128)(2,1)S(1)}, bf16[2,256,512]{2,1,0:T(8,128)(2,1)S(1)}, u32[]{:S(2)}, u32[]{:S(2)}) %collective-permute-start.10) | collective-permute-done | bytes 524320 | tf_op jit(solution)/shard_map/ppermute | solution.py:158
  94.4 1.5 %maximum_bitcast_fusion = bf16[1,2,256,2048]{3,2,1,0:T(8,128)(2,1)} fusion(bf16[1,256,2048]{2,1,0:T(8,128)(2,1)S(1)} %bitcast.28, bf16[1,256,2048]{2,1,0:T(8,128)(2,1)S(1)} %bitcast.27), kind=kLoop, calls=%fused_computation | loop fusion | flops 1048576 | bytes 4194304 | tf_op jit(solution)/shard_map/broadcast_in_dim | solution.py:208
  95.9 1.0 momentum.4
  96.9 9.2 %collective-permute-done.6.refs_1_ = bf16[1,256,512]{2,1,0:T(8,128)(2,1)S(1)} collective-permute-done((bf16[1,256,512]{2,1,0:T(8,128)(2,1)S(1)}, bf16[1,256,512]{2,1,0:T(8,128)(2,1)S(1)}, u32[]{:S(2)}, u32[]{:S(2)}) %collective-permute-start.6) | collective-permute-done | bytes 262176 | tf_op jit(solution)/shard_map/ppermute | solution.py:158
  106.1 1.0 momentum.3
  107.1 3.3 %collective-permute-done.11.refs_1_ = bf16[1,256,512]{2,1,0:T(8,128)(2,1)S(1)} collective-permute-done((bf16[1,256,512]{2,1,0:T(8,128)(2,1)S(1)}, bf16[1,256,512]{2,1,0:T(8,128)(2,1)S(1)}, u32[]{:S(2)}, u32[]{:S(2)}) %collective-permute-start.11) | collective-permute-done | bytes 262176 | tf_op jit(solution)/shard_map/ppermute | solution.py:158
  110.4 1.0 momentum.5
  (27 shorter events, 1.3 us)
Async XLA Ops:
  0.6 1.2 %slice-start = ((bf16[1,2,256,2048]{3,2,1,0:T(8,128)(2,1)}), bf16[1,1,256,2048]{3,2,1,0:T(8,128)(2,1)S(1)}, s32[]{:S(2)}) async-start(bf16[1,2,256,2048]{3,2,1,0:T(8,128)(2,1)} %x0_ref.3), calls=%async_computation | async-start | bytes 2097152 | tf_op jit(solution)/shard_map/slice | solution.py:183
  2.0 43.8 %collective-permute-start.4 = (bf16[2,256,512]{2,1,0:T(8,128)(2,1)S(1)}, bf16[2,256,512]{2,1,0:T(8,128)(2,1)S(1)}, u32[]{:S(2)}, u32[]{:S(2)}) collective-permute-start(bf16[2,256,512]{2,1,0:T(8,128)(2,1)S(1)} %pad_maximum_fusion.1), channel_id=1, source_target_pairs={{0,28},{4,24},{8,20},{12,16},{16,12},{20,8},{24,4},{28,0},{1,29},{... | collective-permute-start | bytes 1572872 | tf_op jit(solution)/shard_map/ppermute | solution.py:154
  11.9 33.9 %copy-start = (bf16[1,2,256,2048]{3,2,1,0:T(8,128)(2,1)S(1)}, bf16[1,2,256,2048]{3,2,1,0:T(8,128)(2,1)}, u32[]{:S(2)}) copy-start(bf16[1,2,256,2048]{3,2,1,0:T(8,128)(2,1)} %x0_ref.3) | copy-start | bytes 6291460
  12.0 41.9 %collective-permute-start.9 = (bf16[4,256,512]{2,1,0:T(8,128)(2,1)S(1)}, bf16[4,256,512]{2,1,0:T(8,128)(2,1)S(1)}, u32[]{:S(2)}, u32[]{:S(2)}) collective-permute-start(bf16[4,256,512]{2,1,0:T(8,128)(2,1)S(1)} %slice_bitcast_fusion), channel_id=1, source_target_pairs={{0,28},{4,24},{8,20},{12,16},{16,12},{20,8},{24,4},{28,0},{1,29},{... | collective-permute-start | bytes 3145736 | tf_op jit(solution)/shard_map/ppermute | solution.py:154
  12.2 33.7 %collective-permute-start.3 = (bf16[256,512]{1,0:T(8,128)(2,1)S(1)}, bf16[256,512]{1,0:T(8,128)(2,1)S(1)}, u32[]{:S(2)}, u32[]{:S(2)}) collective-permute-start(bf16[256,512]{1,0:T(8,128)(2,1)S(1)} %slice_bitcast_fusion.3), channel_id=1, source_target_pairs={{0,28},{4,24},{8,20},{12,16},{16,12},{20,8},{24,4},{28,0},{1,29},{... | collective-permute-start | bytes 786440 | tf_op jit(solution)/shard_map/ppermute | solution.py:154
  14.9 42.2 %collective-permute-start.2 = (bf16[2,256,512]{2,1,0:T(8,128)(2,1)S(1)}, bf16[2,256,512]{2,1,0:T(8,128)(2,1)S(1)}, u32[]{:S(2)}, u32[]{:S(2)}) collective-permute-start(bf16[2,256,512]{2,1,0:T(8,128)(2,1)S(1)} %pad_maximum_fusion), channel_id=1, source_target_pairs={{0,28},{4,24},{8,20},{12,16},{16,12},{20,8},{24,4},{28,0},{1,29},{... | collective-permute-start | bytes 1572872 | tf_op jit(solution)/shard_map/ppermute | solution.py:154
  46.9 15.2 %collective-permute-start.7 = (bf16[2,256,512]{2,1,0:T(8,128)(2,1)S(1)}, bf16[2,256,512]{2,1,0:T(8,128)(2,1)S(1)}, u32[]{:S(2)}, u32[]{:S(2)}) collective-permute-start(bf16[2,256,512]{2,1,0:T(8,128)(2,1)S(1)} %get-tuple-element.16), channel_id=1, source_target_pairs={{0,1},{1,0},{2,3},{3,2},{4,5},{5,4},{6,7},{7,6},{8,9},{9,8},{10,11... | collective-permute-start | bytes 1572872 | tf_op jit(solution)/shard_map/ppermute | solution.py:158
  49.6 44.8 %collective-permute-start = (bf16[256,2048]{1,0:T(8,128)(2,1)S(1)}, bf16[256,2048]{1,0:T(8,128)(2,1)S(1)}, u32[]{:S(2)}, u32[]{:S(2)}) collective-permute-start(bf16[256,2048]{1,0:T(8,128)(2,1)S(1)} %get-tuple-element.20), channel_id=1, source_target_pairs={{4,0},{8,4},{12,8},{16,12},{20,16},{24,20},{28,24},{5,1},{9,5},{13... | collective-permute-start | bytes 3145736 | tf_op jit(solution)/shard_map/ppermute | solution.py:149
  50.9 43.5 %collective-permute-start.1 = (bf16[256,2048]{1,0:T(8,128)(2,1)S(1)}, bf16[256,2048]{1,0:T(8,128)(2,1)S(1)}, u32[]{:S(2)}, u32[]{:S(2)}) collective-permute-start(bf16[256,2048]{1,0:T(8,128)(2,1)S(1)} %get-tuple-element.21), channel_id=1, source_target_pairs={{0,4},{4,8},{8,12},{12,16},{16,20},{20,24},{24,28},{1,5},{5,9},{9,... | collective-permute-start | bytes 3145736 | tf_op jit(solution)/shard_map/ppermute | solution.py:149
  54.0 25.0 %collective-permute-start.5 = (bf16[2,256,512]{2,1,0:T(8,128)(2,1)S(1)}, bf16[2,256,512]{2,1,0:T(8,128)(2,1)S(1)}, u32[]{:S(2)}, u32[]{:S(2)}) collective-permute-start(bf16[2,256,512]{2,1,0:T(8,128)(2,1)S(1)} %get-tuple-element.14), channel_id=1, source_target_pairs={{0,1},{1,0},{2,3},{3,2},{4,5},{5,4},{6,7},{7,6},{8,9},{9,8},{10,11... | collective-permute-start | bytes 1572872 | tf_op jit(solution)/shard_map/ppermute | solution.py:158
  57.1 37.0 %collective-permute-start.10 = (bf16[2,256,512]{2,1,0:T(8,128)(2,1)S(1)}, bf16[2,256,512]{2,1,0:T(8,128)(2,1)S(1)}, u32[]{:S(2)}, u32[]{:S(2)}) collective-permute-start(bf16[2,256,512]{2,1,0:T(8,128)(2,1)S(1)} %get-tuple-element.19), channel_id=1, source_target_pairs={{0,1},{1,0},{2,3},{3,2},{4,5},{5,4},{6,7},{7,6},{8,9},{9,8},{10,11... | collective-permute-start | bytes 1572872 | tf_op jit(solution)/shard_map/ppermute | solution.py:158
  62.2 33.6 %collective-permute-start.8 = (bf16[1,256,512]{2,1,0:T(8,128)(2,1)S(1)}, bf16[1,256,512]{2,1,0:T(8,128)(2,1)S(1)}, u32[]{:S(2)}, u32[]{:S(2)}) collective-permute-start(bf16[1,256,512]{2,1,0:T(8,128)(2,1)S(1)} %get-tuple-element.24), channel_id=1, source_target_pairs={{0,2},{1,3},{2,0},{3,1},{4,6},{5,7},{6,4},{7,5},{8,10},{9,11},{10,... | collective-permute-start | bytes 786440 | tf_op jit(solution)/shard_map/ppermute | solution.py:158
  79.1 27.0 %collective-permute-start.6 = (bf16[1,256,512]{2,1,0:T(8,128)(2,1)S(1)}, bf16[1,256,512]{2,1,0:T(8,128)(2,1)S(1)}, u32[]{:S(2)}, u32[]{:S(2)}) collective-permute-start(bf16[1,256,512]{2,1,0:T(8,128)(2,1)S(1)} %get-tuple-element.26), channel_id=1, source_target_pairs={{0,2},{1,3},{2,0},{3,1},{4,6},{5,7},{6,4},{7,5},{8,10},{9,11},{10,... | collective-permute-start | bytes 786440 | tf_op jit(solution)/shard_map/ppermute | solution.py:158
  94.2 16.2 %collective-permute-start.11 = (bf16[1,256,512]{2,1,0:T(8,128)(2,1)S(1)}, bf16[1,256,512]{2,1,0:T(8,128)(2,1)S(1)}, u32[]{:S(2)}, u32[]{:S(2)}) collective-permute-start(bf16[1,256,512]{2,1,0:T(8,128)(2,1)S(1)} %get-tuple-element.22), channel_id=1, source_target_pairs={{0,2},{1,3},{2,0},{3,1},{4,6},{5,7},{6,4},{7,5},{8,10},{9,11},{10,... | collective-permute-start | bytes 786440 | tf_op jit(solution)/shard_map/ppermute | solution.py:158
  94.3 1.5 %copy-start.1 = (f32[1,512,256]{2,1,0:T(8,128)S(1)}, f32[1,512,256]{2,1,0:T(8,128)}, u32[]{:S(2)}) copy-start(f32[1,512,256]{2,1,0:T(8,128)} %mom_ref.4) | copy-start | bytes 1572868
  94.4 11.8 %copy-start.2 = (f32[1,512,256]{2,1,0:T(8,128)S(1)}, f32[1,512,256]{2,1,0:T(8,128)}, u32[]{:S(2)}) copy-start(f32[1,512,256]{2,1,0:T(8,128)} %mom_ref.3) | copy-start | bytes 1572868
  95.9 14.6 %copy-start.3 = (f32[1,512,256]{2,1,0:T(8,128)S(1)}, f32[1,512,256]{2,1,0:T(8,128)}, u32[]{:S(2)}) copy-start(f32[1,512,256]{2,1,0:T(8,128)} %mom_ref.5) | copy-start | bytes 1572868

commit v2 on v1

v2 whole, which is shorter than its diff:
```python
import functools
import math

import jax
import jax.numpy as jnp
from jax import lax
from jax.experimental import pallas as pl
from jax.experimental.pallas import tpu as pltpu
from jax.sharding import PartitionSpec as P

BF16 = jnp.bfloat16
F32 = jnp.float32
VMEM_LIMIT = 8 * 1024 * 1024
COST = pl.CostEstimate(flops=1000, bytes_accessed=1000, transcendentals=0)


def rows_dot(left, right):
    return lax.dot_general(left, right, (((0,), (0,)), ((), ())), preferred_element_type=F32)


def cols_dot(left, right):
    return lax.dot_general(left, right, (((1,), (1,)), ((), ())), preferred_element_type=F32)


def slot_offsets(count, masks):
    offsets = [0]
    for mask in reversed(masks):
        offsets = offsets + [o ^ mask for o in offsets]
    return offsets


def columns_of(mine, offset, shard):
    return pl.ds(pl.multiple_of((mine[0] ^ offset) * shard, shard), shard)


def activations_kernel(cut, mine, *refs):
    sources, outs, held, made = refs[:5], refs[5:11], refs[11:16], refs[16:19]
    in_sems, out_sems = refs[19:]
    dgu_out, x_send_out, x_keep_out, hidden_out, send_out = outs[0:2], *outs[2:6]
    dgu_ref, hidden_ref, send_ref = made
    copies = {}

    def read(b):
        for i in (0, 2, 3, 1, 4):
            copies[b, i] = pltpu.make_async_copy(sources[i].at[0, b], held[i].at[b], in_sems.at[b, i])
            copies[b, i].start()

    written = []

    def write(source, target):
        copy = pltpu.make_async_copy(source, target, out_sems.at[len(written)])
        copy.start()
        written.append(copy)

    read(1)
    for b in (1, 0):
        x_ref, y_ref, wg_ref, wu_ref, wd_ref = (ref.at[b] for ref in held)
        half, ff, shard = send_ref.shape[1:]
        copies[b, 0].wait()
        copies[b, 2].wait()
        gate = jnp.dot(x_ref[...], wg_ref[...], preferred_element_type=F32)
        copies[b, 3].wait()
        up = jnp.dot(x_ref[...], wu_ref[...], preferred_element_type=F32)
        copies[b, 1].wait()
        copies[b, 4].wait()
        if b:
            read(0)
            for slot, offset in enumerate(cut):
                target = x_keep_out if slot < half else x_send_out
                write(x_ref.at[:, columns_of(mine, offset, shard)], target.at[slot % half])
        dhid = cols_dot(y_ref[...], wd_ref[...])
        sig = jax.nn.sigmoid(gate)
        act = gate * sig
        hidden = (act * up).astype(BF16)
        dgu_ref[b, :, :ff] = (dhid * up * sig * (1.0 + gate * (1.0 - sig))).astype(BF16)
        dgu_ref[b, :, ff:] = (dhid * act).astype(BF16)
        write(dgu_ref.at[b], dgu_out[b])
        hidden_ref[b] = hidden
        hidden_t = hidden.T
        for slot in range(half):
            columns = y_ref[:, columns_of(mine, cut[half + slot], shard)]
            send_ref[b, slot] = jnp.dot(hidden_t, columns, preferred_element_type=F32).astype(BF16)
        write(send_ref.at[b], send_out.at[b])
    write(hidden_ref, hidden_out)
    for copy in written:
        copy.wait()


def activations(mine, inputs, cotangent, w_gate, w_up, w_down, cut, shard):
    _, _, rows, width = inputs.shape
    ff = w_gate.shape[3]
    half = len(cut) // 2
    outs = [(rows, 2 * ff)] * 2 + [(half, rows, shard)] * 2 + [(2, rows, ff), (2, half, ff, shard)]
    made = [(2, rows, 2 * ff), (2, rows, ff), (2, half, ff, shard)]
    return pl.pallas_call(
        functools.partial(activations_kernel, cut),
        out_shape=tuple(jax.ShapeDtypeStruct(dims, BF16) for dims in outs),
        in_specs=[pl.BlockSpec(memory_space=pltpu.SMEM)] + [pl.BlockSpec(memory_space=pl.ANY)] * 5,
        out_specs=[pl.BlockSpec(memory_space=pl.ANY)] * len(outs),
        scratch_shapes=[pltpu.VMEM((2, *array.shape[2:]), BF16) for array in (inputs, cotangent, w_gate, w_up, w_down)]
        + [pltpu.VMEM(dims, BF16) for dims in made]
        + [pltpu.SemaphoreType.DMA((2, 5)), pltpu.SemaphoreType.DMA((len(cut) + 5,))],
        compiler_params=pltpu.CompilerParams(vmem_limit_bytes=48 * 1024 * 1024),
        name="activations",
    )(mine, inputs, cotangent, w_gate, w_up, w_down)


def rest_kernel(cut, mine, y_ref, wg_ref, wu_ref, dgu0_ref, dgu1_ref, hidden_ref, keep_ref, dx_ref):
    half, ff, shard = keep_ref.shape[1:]
    width = y_ref.shape[3]
    hidden_t = hidden_ref[0].T
    for slot in range(half):
        columns = y_ref[0, 0, :, columns_of(mine, cut[slot], shard)]
        keep_ref[0, slot] = jnp.dot(hidden_t, columns, preferred_element_type=F32).astype(BF16)
    first = pl.program_id(0) == 0
    dgu = jnp.where(first, dgu0_ref[...], dgu1_ref[...])
    dgate, dup = dgu[:, :ff], dgu[:, ff:]
    step = min(512, width)
    for start in range(0, width, step):
        rows = pl.ds(start, step)
        dx_ref[0, :, rows] = (
            cols_dot(dgate, wg_ref[0, 0, rows, :]) + cols_dot(dup, wu_ref[0, 0, rows, :])
        ).astype(BF16)


def rest(mine, cotangent, w_gate, w_up, dgu0, dgu1, hidden, cut, shard):
    _, _, rows, width = cotangent.shape
    ff = w_gate.shape[3]
    half = len(cut) // 2
    whole = lambda b, z: (0, b, 0, 0)
    return pl.pallas_call(
        functools.partial(rest_kernel, cut),
        out_shape=(
            jax.ShapeDtypeStruct((2, half, ff, shard), BF16),
            jax.ShapeDtypeStruct((2, rows, width), BF16),
        ),
        grid_spec=pltpu.PrefetchScalarGridSpec(
            num_scalar_prefetch=1,
            grid=(2,),
            in_specs=[
                pl.BlockSpec((1, 1, rows, width), whole),
                pl.BlockSpec((1, 1, width, ff), whole),
                pl.BlockSpec((1, 1, width, ff), whole),
                pl.BlockSpec((rows, 2 * ff), lambda b, z: (0, 0)),
                pl.BlockSpec((rows, 2 * ff), lambda b, z: (0, 0)),
                pl.BlockSpec((1, rows, ff), lambda b, z: (b, 0, 0)),
            ],
            out_specs=[
                pl.BlockSpec((1, half, ff, shard), lambda b, z: (b, 0, 0, 0)),
                pl.BlockSpec((1, rows, width), lambda b, z: (b, 0, 0)),
            ],
        ),
        compiler_params=pltpu.CompilerParams(vmem_limit_bytes=48 * 1024 * 1024),
        cost_estimate=COST,
        name="rest",
    )(mine, cotangent, w_gate, w_up, dgu0, dgu1, hidden)


def pair_kernel(mine, x0_ref, x1_ref, d0_ref, d1_ref, out_ref):
    out_ref[0] = (rows_dot(d0_ref[...], x0_ref[0, 0]) + rows_dot(d1_ref[...], x1_ref[0])).astype(BF16)


def pair(mine, inputs, mirrored_x, dgu, mirrored_dgu, offsets, shard):
    _, _, rows, _ = inputs.shape
    both = dgu.shape[1]
    count = len(offsets)

    def column(j, z):
        offset = sum(jnp.where(j == i, o, 0) for i, o in enumerate(offsets))
        return (0, 0, 0, z[0] ^ offset)

    return pl.pallas_call(
        pair_kernel,
        out_shape=jax.ShapeDtypeStruct((count, both, shard), BF16),
        grid_spec=pltpu.PrefetchScalarGridSpec(
            num_scalar_prefetch=1,
            grid=(count,),
            in_specs=[
                pl.BlockSpec((1, 1, rows, shard), column),
                pl.BlockSpec((1, rows, shard), lambda j, z: (j, 0, 0)),
                pl.BlockSpec((rows, both), lambda j, z: (0, 0)),
                pl.BlockSpec((rows, both), lambda j, z: (0, 0)),
            ],
            out_specs=pl.BlockSpec((1, both, shard), lambda j, z: (j, 0, 0)),
        ),
        compiler_params=pltpu.CompilerParams(vmem_limit_bytes=VMEM_LIMIT),
        cost_estimate=COST,
        name="pair",
    )(mine, inputs, mirrored_x, dgu, mirrored_dgu)


def momentum_kernel(scale, count, *refs):
    moms, parts, outs = refs[:count], refs[count:-count], refs[-count:]
    ff = moms[0].shape[2]
    for i in range(count):
        total = parts[0][0, i * ff : (i + 1) * ff].astype(F32)
        for ref in parts[1:]:
            total = total + ref[0, i * ff : (i + 1) * ff].astype(F32)
        outs[i][0] = 0.9 * moms[i][0] + total.T * scale


def momentum(moms, parts, scale):
    shape = moms[0].shape
    _, shard, ff = shape
    count = len(moms)
    whole = pl.BlockSpec((1, shard, ff), lambda i: (0, 0, 0))
    return pl.pallas_call(
        functools.partial(momentum_kernel, scale, count),
        out_shape=(jax.ShapeDtypeStruct(shape, F32),) * count,
        grid=(1,),
        in_specs=[whole] * count + [pl.BlockSpec((1, ff * count, shard), lambda i: (0, 0, 0))] * len(parts),
        out_specs=[whole] * count,
        compiler_params=pltpu.CompilerParams(vmem_limit_bytes=2 * VMEM_LIMIT),
        cost_estimate=COST,
        name="momentum",
    )(*moms, *parts)


def shifted(value, steps, name):
    count = lax.axis_size("section")
    first, last = max(0, -steps), min(count, count - steps)
    with jax.named_scope(name):
        return lax.ppermute(value, "section", [(i, i + steps) for i in range(first, last)])


def mirrored(value, name):
    count = lax.axis_size("section")
    with jax.named_scope(name):
        return lax.ppermute(value, "section", [(i, count - 1 - i) for i in range(count)])


def swapped(value, mask, name):
    with jax.named_scope(name):
        return lax.ppermute(value, "dp", [(i, i ^ mask) for i in range(lax.axis_size("dp"))])


def after(value, earlier):
    return lax.optimization_barrier((value, earlier))[0]


def add(left, right):
    return (left.astype(F32) + right.astype(F32)).astype(BF16)


def finish(keep, received, masks, name, axis):
    for mask in masks[1:]:
        (stay, go), (stayed, gone) = (jnp.split(v, 2, axis) for v in (keep, received))
        keep = add(stay, stayed)
        received = swapped(add(go, gone), mask, name)
    return keep, received


def body(inputs, cotangent, w_gate, w_up, w_down, mom_gate, mom_up, mom_down):
    replicas = lax.axis_size("dp")
    _, _, rows, width = inputs.shape
    shard = width // replicas
    half = replicas // 2
    masks = [1 << i for i in range(replicas.bit_length() - 1)]
    cut = slot_offsets(replicas, masks)
    mine = lax.axis_index("dp")[None]
    scale = 1.0 / math.sqrt(rows * replicas)

    dgu0, dgu1, x_send, x_keep, hidden, down_send = activations(
        mine, inputs, cotangent, w_gate, w_up, w_down, cut, shard
    )
    down_keep, dx = rest(mine, cotangent, w_gate, w_up, dgu0, dgu1, hidden, cut, shard)
    x_send, dgu1 = mirrored(x_send, "x_send"), mirrored(dgu1, "dgu")
    down_first = swapped(down_send, masks[0], "down_first")
    x_keep = mirrored(x_keep, "x_keep")
    recv0 = shifted(after(dx[0], x_keep), -1, "dx_first")
    recv1 = shifted(after(dx[1], x_keep), 1, "dx_second")
    pair_send = pair(mine, inputs, x_send, dgu0, dgu1, cut[half:], shard)
    pair_first = swapped(pair_send, masks[0], "pair_first")
    down_keep, down_last = finish(down_keep, down_first, masks, "down_rest", 1)
    mirror = add(down_keep[1], down_last[1])
    mirror = mirrored(after(mirror, (recv0, recv1)), "down_mirror")
    pair_keep = pair(mine, inputs, x_keep, dgu0, dgu1, cut[:half], shard)
    pair_parts = finish(pair_keep, pair_first, masks, "pair_rest", 0)
    new_down = momentum([mom_down], (down_keep[0], down_last[0], mirror), scale)
    results = [*momentum([mom_gate, mom_up], pair_parts, scale), *new_down]
    grad_in = jnp.stack([recv0, recv1])[None]
    return (grad_in, *results)


def solution(mesh):
    tokens = P("section", None, "dp", None)
    weights = P("section", None, None, None)
    moments = P("section", "dp", None)
    return jax.shard_map(
        body,
        mesh=mesh,
        in_specs=(tokens, tokens, weights, weights, weights, moments, moments, moments),
        out_specs=(tokens, moments, moments, moments),
        check_vma=False,
    )
```

time: 112 us -> 98.6 us (0.88)
  waiting for transfers between devices: 74.2 us -> 60.7 us
  Pallas kernels: 11.5 us -> 14.7 us
  starting transfers between devices: 20.9 us -> 18.1 us
    ppermute x4, waiting for transfers between devices: 33.5 us -> 22.8 us  [mirrored(): lax.ppermute(value, 'section', [(i, count - 1 - i) for i in range(count)])]
    pallas_call x6, Pallas kernels: 11.5 us -> 14.7 us  [the longest x1 7.05 us: activations(): pl.pallas_call(functools.partial(activations_kernel, cut), out_shape=tupl...]
    ppermute x6 -> x4, waiting for transfers between devices: 40.7 us -> 37.9 us  [swapped(): lax.ppermute(value, 'dp', [(i, i ^ mask) for i in range(lax.axis_size('dp...]
    ppermute x6 -> x4, starting transfers between devices: 10.2 us -> 7.58 us  [swapped(): lax.ppermute(value, 'dp', [(i, i ^ mask) for i in range(lax.axis_size('dp...]
    unnamed x8 -> x12, local copies, waits for them, and re-layouts: 0.02 us -> 1.61 us
    slice x2 -> x0, local copies, waits for them, and re-layouts: 1.2 us -> none  [body(): x_keep = mirrored(columns(inputs[0, 1], offsets[:half]))]
  transfers between devices with their start and end apart: 12 -> 10, of which waited for: 7 -> 5; matrix products, arithmetic and copies ran while one was open for 2% -> 3% of each run, Pallas kernels for 9% -> 7%
where the time goes in v2:
time: 98.6 us; the launch traced here: 98.4 us
  waiting for transfers between devices  60.7 us (62%)
  starting transfers between devices  18.1 us (18%)
  Pallas kernels  14.7 us (15%)
  other arithmetic  2.19 us (2%)
  local copies, waits for them, and re-layouts  1.89 us (2%)
    ppermute x4, waiting for transfers between devices, swapped(): lax.ppermute(value, 'dp', [(i, i ^ mask) for i in range(lax.axis_size('dp...  37.9 us
    ppermute x4, waiting for transfers between devices, mirrored(): lax.ppermute(value, 'section', [(i, count - 1 - i) for i in range(count)])  22.8 us
    ppermute x4, starting transfers between devices, swapped(): lax.ppermute(value, 'dp', [(i, i ^ mask) for i in range(lax.axis_size('dp...  7.58 us
    pallas_call x1, Pallas kernels, activations(): pl.pallas_call(functools.partial(activations_kernel, cut), out_shape=tupl...  7.05 us
    ppermute x4, starting transfers between devices, mirrored(): lax.ppermute(value, 'section', [(i, count - 1 - i) for i in range(count)])  6.15 us
    ppermute x2, starting transfers between devices, shifted(): lax.ppermute(value, 'section', [(i, i + steps) for i in range(first, last)])  4.38 us
    pallas_call x1, Pallas kernels, rest(): pl.pallas_call(functools.partial(rest_kernel, cut), out_shape=(jax.ShapeD...  3.47 us
    pallas_call x2, Pallas kernels, momentum(): pl.pallas_call(functools.partial(momentum_kernel, scale, count), out_shap...  2.17 us
  transfers between devices with their start and end apart: 10, of which 5 were waited for; matrix products, arithmetic and copies ran while one was open for 3% of the time, Pallas kernels for 7%

profile of v2, /device:TPU:0, one launch (start us, length us, event | category | flops | bytes accessed | tf_op | source)
XLA Modules:
  0.0 98.4 jit_solution(15357334846753388849)
XLA Ops:
  0.6 1.6 %copy-done = bf16[1,2,256,2048]{3,2,1,0:T(8,128)(2,1)S(1)} copy-done((bf16[1,2,256,2048]{3,2,1,0:T(8,128)(2,1)S(1)}, bf16[1,2,256,2048]{3,2,1,0:T(8,128)(2,1)}, u32[]{:S(2)}) %copy-start) | copy-done | bytes 2097176
  2.2 7.1 %activations.1 = (bf16[256,512]{1,0:T(8,128)(2,1)S(1)}, bf16[256,512]{1,0:T(8,128)(2,1)S(1)}, bf16[2,256,512]{2,1,0:T(8,128)(2,1)S(1)}, bf16[2,256,512]{2,1,0:T(...) custom-call(s32[1]{0:T(128)} %bitcast.mine, ...), custom_call_target="tpu_custom_call" | custom-call | tf_op jit(solution)/shard_map/activations/pallas_call | solution.py:95
  9.3 3.4 %collective-permute-start.4 = (bf16[2,256,512]{2,1,0:T(8,128)(2,1)S(1)}, bf16[2,256,512]{2,1,0:T(8,128)(2,1)S(1)}, u32[]{:S(2)}, u32[]{:S(2)}) collective-permute-start(bf16[2,256,512]{2,1,0:T(8,128)(2,1)S(1)} %get-tuple-element.24), channel_id=1, source_target_pairs={{0,28},{4,24},{8,20},{12,16},{16,12},{20,8},{24,4},{28,0},{1,29},{... | collective-permute-start | bytes 1572872 | tf_op jit(solution)/shard_map/x_send/ppermute | solution.py:229
  12.7 1.6 %collective-permute-start.7 = (bf16[2,2,256,512]{3,2,1,0:T(8,128)(2,1)S(1)}, bf16[2,2,256,512]{3,2,1,0:T(8,128)(2,1)S(1)}, u32[]{:S(2)}, u32[]{:S(2)}) collective-permute-start(bf16[2,2,256,512]{3,2,1,0:T(8,128)(2,1)S(1)} %get-tuple-element.28), channel_id=1, source_target_pairs={{0,1},{1,0},{2,3},{3,2},{4,5},{5,4},{6,7},{7,6},{8,9},{9,8},{10,11... | collective-permute-start | bytes 3145736 | tf_op jit(solution)/shard_map/down_first/ppermute | solution.py:234
  14.3 0.5 collective-permute-start.3
  14.7 2.2 %collective-permute-start = (bf16[2,256,512]{2,1,0:T(8,128)(2,1)S(1)}, bf16[2,256,512]{2,1,0:T(8,128)(2,1)S(1)}, u32[]{:S(2)}, u32[]{:S(2)}) collective-permute-start(bf16[2,256,512]{2,1,0:T(8,128)(2,1)S(1)} %get-tuple-element.21), channel_id=1, source_target_pairs={{0,28},{4,24},{8,20},{12,16},{16,12},{20,8},{24,4},{28,0},{1,29},{... | collective-permute-start | bytes 1572872 | tf_op jit(solution)/shard_map/x_keep/ppermute | solution.py:229
  16.9 3.5 %rest.1 = (bf16[2,2,256,512]{3,2,1,0:T(8,128)(2,1)S(1)}, bf16[2,256,2048]{2,1,0:T(8,128)(2,1)S(1)}) custom-call(s32[1]{0:T(128)} %bitcast.mine, bf16[1,2,256,2048]{3,2,1,0:T(8,128)(2,1)S(1)} %copy-done.2, bf16[1,2,2048,256]{3,2,1,0:T(8,128)(2,1)} %wg_ref.1, bf16[1,2,2048,256]{3,2,1,0:T(8,128)(2,1)} %wu_ref.1, ...), custom_call_target="tpu_custom_call" | custom-call | flops 1000 | bytes 1000 | tf_op jit(solution)/shard_map/rest/pallas_call | solution.py:131
  20.4 10.2 %collective-permute-done.3.d1_ref = bf16[256,512]{1,0:T(8,128)(2,1)S(1)} collective-permute-done((bf16[256,512]{1,0:T(8,128)(2,1)S(1)}, bf16[256,512]{1,0:T(8,128)(2,1)S(1)}, u32[]{:S(2)}, u32[]{:S(2)}) %collective-permute-start.3) | collective-permute-done | bytes 262176 | tf_op jit(solution)/shard_map/dgu/ppermute | solution.py:229
  30.6 1.0 %pair.3 = bf16[2,512,512]{2,1,0:T(8,128)(2,1)S(1)} custom-call(s32[1]{0:T(128)} %bitcast.mine, bf16[1,2,256,2048]{3,2,1,0:T(8,128)(2,1)S(1)} %copy-done.1, bf16[2,256,512]{2,1,0:T(8,128)(2,1)S(1)} %collective-permute-done.4.x1_ref, bf16[256,512]{1,0:T(8,128)(2,1)S(1)} %get-tuple-element.17.dgu0_ref.d0_ref, bf16[256,512]{1,0:T(8,128)(2,1)S(1)} %collective-permute-done.3.d1_ref), custom_call_target="tpu_custom_call" | custom-call | flops 1000 | bytes 1000 | tf_op jit(solution)/shard_map/pair/pallas_call | solution.py:172
  31.7 2.5 %collective-permute-start.5 = (bf16[2,512,512]{2,1,0:T(8,128)(2,1)S(1)}, bf16[2,512,512]{2,1,0:T(8,128)(2,1)S(1)}, u32[]{:S(2)}, u32[]{:S(2)}) collective-permute-start(bf16[2,512,512]{2,1,0:T(8,128)(2,1)S(1)} %pair.3), channel_id=1, source_target_pairs={{0,1},{1,0},{2,3},{3,2},{4,5},{5,4},{6,7},{7,6},{8,9},{9,8},{10,11... | collective-permute-start | bytes 3145736 | tf_op jit(solution)/shard_map/pair_first/ppermute | solution.py:234
  34.1 0.2 slice_bitcast_fusion.1
  34.4 7.5 %collective-permute-done.x1_ref = bf16[2,256,512]{2,1,0:T(8,128)(2,1)S(1)} collective-permute-done((bf16[2,256,512]{2,1,0:T(8,128)(2,1)S(1)}, bf16[2,256,512]{2,1,0:T(8,128)(2,1)S(1)}, u32[]{:S(2)}, u32[]{:S(2)}) %collective-permute-start) | collective-permute-done | bytes 524320 | tf_op jit(solution)/shard_map/x_keep/ppermute | solution.py:229
  41.9 1.3 %collective-permute-start.1 = (bf16[256,2048]{1,0:T(8,128)(2,1)S(1)}, bf16[256,2048]{1,0:T(8,128)(2,1)S(1)}, u32[]{:S(2)}, u32[]{:S(2)}) collective-permute-start(bf16[256,2048]{1,0:T(8,128)(2,1)S(1)} %get-tuple-element.22), channel_id=1, source_target_pairs={{4,0},{8,4},{12,8},{16,12},{20,16},{24,20},{28,24},{5,1},{9,5},{13... | collective-permute-start | bytes 3145736 | tf_op jit(solution)/shard_map/dx_first/ppermute | solution.py:223
  43.1 3.1 %collective-permute-start.2 = (bf16[256,2048]{1,0:T(8,128)(2,1)S(1)}, bf16[256,2048]{1,0:T(8,128)(2,1)S(1)}, u32[]{:S(2)}, u32[]{:S(2)}) collective-permute-start(bf16[256,2048]{1,0:T(8,128)(2,1)S(1)} %get-tuple-element.23), channel_id=1, source_target_pairs={{0,4},{4,8},{8,12},{12,16},{16,20},{20,24},{24,28},{1,5},{5,9},{9,... | collective-permute-start | bytes 3145736 | tf_op jit(solution)/shard_map/dx_second/ppermute | solution.py:223
  46.3 0.3 add_convert_fusion
  46.6 3.5 %collective-permute-start.8 = (bf16[2,1,256,512]{3,2,1,0:T(8,128)(2,1)S(1)}, bf16[2,1,256,512]{3,2,1,0:T(8,128)(2,1)S(1)}, u32[]{:S(2)}, u32[]{:S(2)}) collective-permute-start(bf16[2,1,256,512]{3,2,1,0:T(8,128)(2,1)S(1)} %get-tuple-element.30), channel_id=1, source_target_pairs={{0,2},{1,3},{2,0},{3,1},{4,6},{5,7},{6,4},{7,5},{8,10},{9,11},{10,... | collective-permute-start | bytes 1572872 | tf_op jit(solution)/shard_map/down_rest/ppermute | solution.py:234
  50.1 1.0 %pair.2 = bf16[2,512,512]{2,1,0:T(8,128)(2,1)S(1)} custom-call(s32[1]{0:T(128)} %bitcast.mine, bf16[1,2,256,2048]{3,2,1,0:T(8,128)(2,1)S(1)} %copy-done.1, bf16[2,256,512]{2,1,0:T(8,128)(2,1)S(1)} %collective-permute-done.x1_ref, bf16[256,512]{1,0:T(8,128)(2,1)S(1)} %get-tuple-element.17.dgu0_ref.d0_ref, bf16[256,512]{1,0:T(8,128)(2,1)S(1)} %collective-permute-done.3.d1_ref), custom_call_target="tpu_custom_call" | custom-call | flops 1000 | bytes 1000 | tf_op jit(solution)/shard_map/pair/pallas_call | solution.py:172
  51.1 21.0 %collective-permute-done.5 = bf16[2,512,512]{2,1,0:T(8,128)(2,1)S(1)} collective-permute-done((bf16[2,512,512]{2,1,0:T(8,128)(2,1)S(1)}, bf16[2,512,512]{2,1,0:T(8,128)(2,1)S(1)}, u32[]{:S(2)}, u32[]{:S(2)}) %collective-permute-start.5) | collective-permute-done | bytes 1048608 | tf_op jit(solution)/shard_map/pair_first/ppermute | solution.py:234
  72.1 0.3 add_convert_fusion.2
  72.8 1.5 %maximum_bitcast_fusion = bf16[1,2,256,2048]{3,2,1,0:T(8,128)(2,1)} fusion(bf16[1,256,2048]{2,1,0:T(8,128)(2,1)S(1)} %bitcast.16, bf16[1,256,2048]{2,1,0:T(8,128)(2,1)S(1)} %bitcast.15), kind=kLoop, calls=%fused_computation | loop fusion | flops 1048576 | bytes 4194304 | tf_op jit(solution)/shard_map/broadcast_in_dim | solution.py:281
  74.3 5.1 %collective-permute-done.9.refs_3_ = bf16[1,256,512]{2,1,0:T(8,128)(2,1)S(1)} collective-permute-done((bf16[1,256,512]{2,1,0:T(8,128)(2,1)S(1)}, bf16[1,256,512]{2,1,0:T(8,128)(2,1)S(1)}, u32[]{:S(2)}, u32[]{:S(2)}) %collective-permute-start.9) | collective-permute-done | bytes 262176 | tf_op jit(solution)/shard_map/down_mirror/ppermute | solution.py:229
  79.4 1.0 %momentum.3 = f32[1,512,256]{2,1,0:T(8,128)} custom-call(f32[1,512,256]{2,1,0:T(8,128)S(1)} %copy-done.3, bf16[1,256,512]{2,1,0:T(8,128)(2,1)S(1)} %slice_bitcast_fusion.3.refs_1_, bf16[1,256,512]{2,1,0:T(8,128)(2,1)S(1)} %slice_bitcast_fusion.2.refs_2_, bf16[1,256,512]{2,1,0:T(8,128)(2,1)S(1)} %collective-permute-done.9.refs_3_), custom_call_target="tpu_custom_call" | custom-call | flops 1000 | bytes 1000 | tf_op jit(solution)/shard_map/momentum/pallas_call | solution.py:207
  80.4 16.9 %collective-permute-done.6.refs_3_ = bf16[1,512,512]{2,1,0:T(8,128)(2,1)S(1)} collective-permute-done((bf16[1,512,512]{2,1,0:T(8,128)(2,1)S(1)}, bf16[1,512,512]{2,1,0:T(8,128)(2,1)S(1)}, u32[]{:S(2)}, u32[]{:S(2)}) %collective-permute-start.6) | collective-permute-done | bytes 524320 | tf_op jit(solution)/shard_map/pair_rest/ppermute | solution.py:234
  97.3 1.2 %momentum.2 = (f32[1,512,256]{2,1,0:T(8,128)}, f32[1,512,256]{2,1,0:T(8,128)}) custom-call(f32[1,512,256]{2,1,0:T(8,128)S(1)} %copy-done.4, f32[1,512,256]{2,1,0:T(8,128)S(1)} %copy-done.5, bf16[1,512,512]{2,1,0:T(8,128)(2,1)S(1)} %get-tuple-element.33.refs_2_, bf16[1,512,512]{2,1,0:T(8,128)(2,1)S(1)} %collective-permute-done.6.refs_3_), custom_call_target="tpu_custom_call" | custom-call | flops 1000 | bytes 1000 | tf_op jit(solution)/shard_map/momentum/pallas_call | solution.py:207
  (21 shorter events, 0.3 us)
Async XLA Ops:
  0.6 1.6 %copy-start = (bf16[1,2,256,2048]{3,2,1,0:T(8,128)(2,1)S(1)}, bf16[1,2,256,2048]{3,2,1,0:T(8,128)(2,1)}, u32[]{:S(2)}) copy-start(bf16[1,2,256,2048]{3,2,1,0:T(8,128)(2,1)} %x0_ref.3) | copy-start | bytes 6291460
  2.2 14.7 %copy-start.2 = (bf16[1,2,256,2048]{3,2,1,0:T(8,128)(2,1)S(1)}, bf16[1,2,256,2048]{3,2,1,0:T(8,128)(2,1)}, u32[]{:S(2)}) copy-start(bf16[1,2,256,2048]{3,2,1,0:T(8,128)(2,1)} %y_ref.1) | copy-start | bytes 6291460
  9.3 21.3 %collective-permute-start.4 = (bf16[2,256,512]{2,1,0:T(8,128)(2,1)S(1)}, bf16[2,256,512]{2,1,0:T(8,128)(2,1)S(1)}, u32[]{:S(2)}, u32[]{:S(2)}) collective-permute-start(bf16[2,256,512]{2,1,0:T(8,128)(2,1)S(1)} %get-tuple-element.24), channel_id=1, source_target_pairs={{0,28},{4,24},{8,20},{12,16},{16,12},{20,8},{24,4},{28,0},{1,29},{... | collective-permute-start | bytes 1572872 | tf_op jit(solution)/shard_map/x_send/ppermute | solution.py:229
  12.7 33.6 %collective-permute-start.7 = (bf16[2,2,256,512]{3,2,1,0:T(8,128)(2,1)S(1)}, bf16[2,2,256,512]{3,2,1,0:T(8,128)(2,1)S(1)}, u32[]{:S(2)}, u32[]{:S(2)}) collective-permute-start(bf16[2,2,256,512]{3,2,1,0:T(8,128)(2,1)S(1)} %get-tuple-element.28), channel_id=1, source_target_pairs={{0,1},{1,0},{2,3},{3,2},{4,5},{5,4},{6,7},{7,6},{8,9},{9,8},{10,11... | collective-permute-start | bytes 3145736 | tf_op jit(solution)/shard_map/down_first/ppermute | solution.py:234
  14.3 16.4 %collective-permute-start.3 = (bf16[256,512]{1,0:T(8,128)(2,1)S(1)}, bf16[256,512]{1,0:T(8,128)(2,1)S(1)}, u32[]{:S(2)}, u32[]{:S(2)}) collective-permute-start(bf16[256,512]{1,0:T(8,128)(2,1)S(1)} %get-tuple-element.18.dgu1_ref), channel_id=1, source_target_pairs={{0,28},{4,24},{8,20},{12,16},{16,12},{20,8},{24,4},{28,0},{1,29},{... | collective-permute-start | bytes 786440 | tf_op jit(solution)/shard_map/dgu/ppermute | solution.py:229
  14.7 27.1 %collective-permute-start = (bf16[2,256,512]{2,1,0:T(8,128)(2,1)S(1)}, bf16[2,256,512]{2,1,0:T(8,128)(2,1)S(1)}, u32[]{:S(2)}, u32[]{:S(2)}) collective-permute-start(bf16[2,256,512]{2,1,0:T(8,128)(2,1)S(1)} %get-tuple-element.21), channel_id=1, source_target_pairs={{0,28},{4,24},{8,20},{12,16},{16,12},{20,8},{24,4},{28,0},{1,29},{... | collective-permute-start | bytes 1572872 | tf_op jit(solution)/shard_map/x_keep/ppermute | solution.py:229
  16.9 13.7 %copy-start.1 = (bf16[1,2,256,2048]{3,2,1,0:T(8,128)(2,1)S(1)}, bf16[1,2,256,2048]{3,2,1,0:T(8,128)(2,1)}, u32[]{:S(2)}) copy-start(bf16[1,2,256,2048]{3,2,1,0:T(8,128)(2,1)} %x0_ref.3) | copy-start | bytes 6291460
  31.7 40.5 %collective-permute-start.5 = (bf16[2,512,512]{2,1,0:T(8,128)(2,1)S(1)}, bf16[2,512,512]{2,1,0:T(8,128)(2,1)S(1)}, u32[]{:S(2)}, u32[]{:S(2)}) collective-permute-start(bf16[2,512,512]{2,1,0:T(8,128)(2,1)S(1)} %pair.3), channel_id=1, source_target_pairs={{0,1},{1,0},{2,3},{3,2},{4,5},{5,4},{6,7},{7,6},{8,9},{9,8},{10,11... | collective-permute-start | bytes 3145736 | tf_op jit(solution)/shard_map/pair_first/ppermute | solution.py:234
  41.9 30.7 %collective-permute-start.1 = (bf16[256,2048]{1,0:T(8,128)(2,1)S(1)}, bf16[256,2048]{1,0:T(8,128)(2,1)S(1)}, u32[]{:S(2)}, u32[]{:S(2)}) collective-permute-start(bf16[256,2048]{1,0:T(8,128)(2,1)S(1)} %get-tuple-element.22), channel_id=1, source_target_pairs={{4,0},{8,4},{12,8},{16,12},{20,16},{24,20},{28,24},{5,1},{9,5},{13... | collective-permute-start | bytes 3145736 | tf_op jit(solution)/shard_map/dx_first/ppermute | solution.py:223
  43.1 29.5 %collective-permute-start.2 = (bf16[256,2048]{1,0:T(8,128)(2,1)S(1)}, bf16[256,2048]{1,0:T(8,128)(2,1)S(1)}, u32[]{:S(2)}, u32[]{:S(2)}) collective-permute-start(bf16[256,2048]{1,0:T(8,128)(2,1)S(1)} %get-tuple-element.23), channel_id=1, source_target_pairs={{0,4},{4,8},{8,12},{12,16},{16,20},{20,24},{24,28},{1,5},{5,9},{9,... | collective-permute-start | bytes 3145736 | tf_op jit(solution)/shard_map/dx_second/ppermute | solution.py:223
  46.6 25.9 %collective-permute-start.8 = (bf16[2,1,256,512]{3,2,1,0:T(8,128)(2,1)S(1)}, bf16[2,1,256,512]{3,2,1,0:T(8,128)(2,1)S(1)}, u32[]{:S(2)}, u32[]{:S(2)}) collective-permute-start(bf16[2,1,256,512]{3,2,1,0:T(8,128)(2,1)S(1)} %get-tuple-element.30), channel_id=1, source_target_pairs={{0,2},{1,3},{2,0},{3,1},{4,6},{5,7},{6,4},{7,5},{8,10},{9,11},{10,... | collective-permute-start | bytes 1572872 | tf_op jit(solution)/shard_map/down_rest/ppermute | solution.py:234
  72.4 24.8 %collective-permute-start.6 = (bf16[1,512,512]{2,1,0:T(8,128)(2,1)S(1)}, bf16[1,512,512]{2,1,0:T(8,128)(2,1)S(1)}, u32[]{:S(2)}, u32[]{:S(2)}) collective-permute-start(bf16[1,512,512]{2,1,0:T(8,128)(2,1)S(1)} %get-tuple-element.32), channel_id=1, source_target_pairs={{0,2},{1,3},{2,0},{3,1},{4,6},{5,7},{6,4},{7,5},{8,10},{9,11},{10,... | collective-permute-start | bytes 1572872 | tf_op jit(solution)/shard_map/pair_rest/ppermute | solution.py:234
  72.6 6.8 %collective-permute-start.9 = (bf16[1,256,512]{2,1,0:T(8,128)(2,1)S(1)}, bf16[1,256,512]{2,1,0:T(8,128)(2,1)S(1)}, u32[]{:S(2)}, u32[]{:S(2)}) collective-permute-start(bf16[1,256,512]{2,1,0:T(8,128)(2,1)S(1)} %fusion), channel_id=1, source_target_pairs={{0,28},{4,24},{8,20},{12,16},{16,12},{20,8},{24,4},{28,0},{1,29},{... | collective-permute-start | bytes 786440 | tf_op jit(solution)/shard_map/down_mirror/ppermute | solution.py:229
  72.7 6.7 %copy-start.3 = (f32[1,512,256]{2,1,0:T(8,128)S(1)}, f32[1,512,256]{2,1,0:T(8,128)}, u32[]{:S(2)}) copy-start(f32[1,512,256]{2,1,0:T(8,128)} %refs_0_.5) | copy-start | bytes 1572868
  72.7 24.5 %copy-start.4 = (f32[1,512,256]{2,1,0:T(8,128)S(1)}, f32[1,512,256]{2,1,0:T(8,128)}, u32[]{:S(2)}) copy-start(f32[1,512,256]{2,1,0:T(8,128)} %refs_0_.4) | copy-start | bytes 1572868
  72.7 24.5 %copy-start.5 = (f32[1,512,256]{2,1,0:T(8,128)S(1)}, f32[1,512,256]{2,1,0:T(8,128)}, u32[]{:S(2)}) copy-start(f32[1,512,256]{2,1,0:T(8,128)} %refs_1_.3) | copy-start | bytes 1572868

commit v3 on v2

v3 whole, which is shorter than its diff:
```python
import functools
import math

import jax
import jax.numpy as jnp
from jax import lax
from jax.experimental import pallas as pl
from jax.experimental.pallas import tpu as pltpu
from jax.sharding import PartitionSpec as P

BF16 = jnp.bfloat16
F32 = jnp.float32
VMEM_LIMIT = 8 * 1024 * 1024
SECOND_LIMIT = 58 * 1024 * 1024
REST_LIMIT = 48 * 1024 * 1024
COST = pl.CostEstimate(flops=1000, bytes_accessed=1000, transcendentals=0)
LONG = pl.CostEstimate(flops=1000, bytes_accessed=10**9, transcendentals=0)


def rows_dot(left, right):
    return lax.dot_general(left, right, (((0,), (0,)), ((), ())), preferred_element_type=F32)


def cols_dot(left, right):
    return lax.dot_general(left, right, (((1,), (1,)), ((), ())), preferred_element_type=F32)


def slot_offsets(count, masks):
    offsets = [0]
    for mask in reversed(masks):
        offsets = offsets + [o ^ mask for o in offsets]
    return offsets


def columns_of(mine, offset, shard):
    return pl.ds(pl.multiple_of((mine[0] ^ offset) * shard, shard), shard)


def reader(pairs, sems):
    copies = [pltpu.make_async_copy(source, target, sems.at[i]) for i, (source, target) in enumerate(pairs)]
    for copy in copies:
        copy.start()
    return copies


def backward(gate, up, dhid):
    sig = jax.nn.sigmoid(gate)
    act = gate * sig
    hidden = (act * up).astype(BF16)
    return hidden, (dhid * up * sig * (1.0 + gate * (1.0 - sig))).astype(BF16), (dhid * act).astype(BF16)


def slots_into(out_ref, mine, offsets, hidden_t, y_ref):
    shard = out_ref.shape[2]
    for slot, offset in enumerate(offsets):
        columns = y_ref[:, columns_of(mine, offset, shard)]
        out_ref[slot] = jnp.dot(hidden_t, columns, preferred_element_type=F32).astype(BF16)


def second_kernel(cut, mine, x_hbm, y_hbm, wg_hbm, wu_hbm, wd_hbm, dgu_ref, hidden_ref, send_ref, x_send_ref, x_keep_ref, *held):
    (x_ref, wg_ref, wu_ref, y_ref, wd_ref), sems, slot_sems = held[:5], held[5], held[6]
    half, ff, shard = send_ref.shape
    hbm = (x_hbm, wg_hbm, wu_hbm, y_hbm, wd_hbm)
    copies = reader([(source.at[0, 1], target) for source, target in zip(hbm, held)], sems)
    copies[0].wait()
    slots = reader(
        [
            (x_ref.at[:, columns_of(mine, offset, shard)], (x_keep_ref if i < half else x_send_ref).at[i % half])
            for i, offset in enumerate(cut)
        ],
        slot_sems,
    )
    copies[1].wait()
    gate = jnp.dot(x_ref[...], wg_ref[...], preferred_element_type=F32)
    copies[2].wait()
    up = jnp.dot(x_ref[...], wu_ref[...], preferred_element_type=F32)
    copies[3].wait()
    copies[4].wait()
    dhid = cols_dot(y_ref[...], wd_ref[...])
    hidden, dgate, dup = backward(gate, up, dhid)
    dgu_ref[:, :ff] = dgate
    dgu_ref[:, ff:] = dup
    hidden_ref[...] = hidden
    slots_into(send_ref, mine, cut[half:], hidden.T, y_ref)
    for copy in slots:
        copy.wait()


def second(mine, inputs, cotangent, w_gate, w_up, w_down, cut, shard):
    _, _, rows, width = inputs.shape
    ff = w_gate.shape[3]
    half = len(cut) // 2
    outs = [(rows, 2 * ff), (rows, ff), (half, ff, shard), (half, rows, shard), (half, rows, shard)]
    return pl.pallas_call(
        functools.partial(second_kernel, cut),
        out_shape=tuple(jax.ShapeDtypeStruct(dims, BF16) for dims in outs),
        in_specs=[pl.BlockSpec(memory_space=pltpu.SMEM)] + [pl.BlockSpec(memory_space=pl.ANY)] * 5,
        out_specs=[pl.BlockSpec(memory_space=pltpu.VMEM)] * len(outs),
        scratch_shapes=[pltpu.VMEM(array.shape[2:], BF16) for array in (inputs, w_gate, w_up, cotangent, w_down)]
        + [pltpu.SemaphoreType.DMA((5,)), pltpu.SemaphoreType.DMA((len(cut),))],
        compiler_params=pltpu.CompilerParams(vmem_limit_bytes=SECOND_LIMIT),
        cost_estimate=LONG,
        name="second",
    )(mine, inputs, cotangent, w_gate, w_up, w_down)


def rest_kernel(cut, mine, x_hbm, y_hbm, wg_hbm, wu_hbm, wd_hbm, dgu1_ref, hidden1_ref, *refs):
    dgu_ref, send_ref, keep0_ref, keep1_ref, dx0_ref, dx1_ref = refs[:6]
    (x_ref, wg_ref, wu_ref, y_ref, wd_ref, y1_ref, wg1_ref, wu1_ref), sems = refs[6:14], refs[14]
    half, ff, shard = send_ref.shape
    width = x_ref.shape[1]
    hbm = (x_hbm, wg_hbm, wu_hbm, y_hbm, wd_hbm)
    sources = [source.at[0, 0] for source in hbm] + [source.at[0, 1] for source in (y_hbm, wg_hbm, wu_hbm)]
    copies = reader(list(zip(sources, refs[6:14])), sems)

    def input_gradient(out_ref, dgate, dup, wg, wu):
        step = min(512, width)
        for start in range(0, width, step):
            rows = pl.ds(start, step)
            out_ref[:, rows] = (cols_dot(dgate, wg[rows, :]) + cols_dot(dup, wu[rows, :])).astype(BF16)

    copies[0].wait()
    copies[1].wait()
    gate = jnp.dot(x_ref[...], wg_ref[...], preferred_element_type=F32)
    copies[2].wait()
    up = jnp.dot(x_ref[...], wu_ref[...], preferred_element_type=F32)
    copies[3].wait()
    copies[4].wait()
    hidden, dgate, dup = backward(gate, up, cols_dot(y_ref[...], wd_ref[...]))
    dgu_ref[:, :ff] = dgate
    dgu_ref[:, ff:] = dup
    hidden_t = hidden.T
    slots_into(send_ref, mine, cut[half:], hidden_t, y_ref)
    slots_into(keep0_ref, mine, cut[:half], hidden_t, y_ref)
    input_gradient(dx0_ref, dgate, dup, wg_ref, wu_ref)
    for copy in copies[5:]:
        copy.wait()
    slots_into(keep1_ref, mine, cut[:half], hidden1_ref[...].T, y1_ref)
    input_gradient(dx1_ref, dgu1_ref[:, :ff], dgu1_ref[:, ff:], wg1_ref, wu1_ref)


def rest(mine, inputs, cotangent, w_gate, w_up, w_down, dgu1, hidden1, cut, shard):
    _, _, rows, width = inputs.shape
    ff = w_gate.shape[3]
    half = len(cut) // 2
    outs = [(rows, 2 * ff)] + [(half, ff, shard)] * 3 + [(rows, width)] * 2
    held = (inputs, w_gate, w_up, cotangent, w_down, cotangent, w_gate, w_up)
    vmem = pl.BlockSpec(memory_space=pltpu.VMEM)
    return pl.pallas_call(
        functools.partial(rest_kernel, cut),
        out_shape=tuple(jax.ShapeDtypeStruct(dims, BF16) for dims in outs),
        in_specs=[pl.BlockSpec(memory_space=pltpu.SMEM)] + [pl.BlockSpec(memory_space=pl.ANY)] * 5 + [vmem] * 2,
        out_specs=[vmem] * len(outs),
        scratch_shapes=[pltpu.VMEM(array.shape[2:], BF16) for array in held] + [pltpu.SemaphoreType.DMA((8,))],
        compiler_params=pltpu.CompilerParams(vmem_limit_bytes=REST_LIMIT),
        cost_estimate=LONG,
        name="rest",
    )(mine, inputs, cotangent, w_gate, w_up, w_down, dgu1, hidden1)


def pair_kernel(mine, x0_ref, x1_ref, d0_ref, d1_ref, *outs):
    ff = outs[0].shape[1]
    x0, x1 = x0_ref[0, 0], x1_ref[0]
    for i, out in enumerate(outs):
        part = slice(i * ff, (i + 1) * ff)
        out[0] = (rows_dot(d0_ref[:, part], x0) + rows_dot(d1_ref[:, part], x1)).astype(BF16)


def pair(mine, inputs, mirrored_x, dgu, mirrored_dgu, offsets, shard, cost):
    _, _, rows, _ = inputs.shape
    both = dgu.shape[1]
    ff = both // 2
    count = len(offsets)

    def column(j, z):
        offset = sum(jnp.where(j == i, o, 0) for i, o in enumerate(offsets))
        return (0, 0, 0, z[0] ^ offset)

    return pl.pallas_call(
        pair_kernel,
        out_shape=(jax.ShapeDtypeStruct((count, ff, shard), BF16),) * 2,
        grid_spec=pltpu.PrefetchScalarGridSpec(
            num_scalar_prefetch=1,
            grid=(count,),
            in_specs=[
                pl.BlockSpec((1, 1, rows, shard), column),
                pl.BlockSpec((1, rows, shard), lambda j, z: (j, 0, 0)),
                pl.BlockSpec((rows, both), lambda j, z: (0, 0)),
                pl.BlockSpec((rows, both), lambda j, z: (0, 0)),
            ],
            out_specs=[pl.BlockSpec((1, ff, shard), lambda j, z: (j, 0, 0))] * 2,
        ),
        compiler_params=pltpu.CompilerParams(vmem_limit_bytes=VMEM_LIMIT),
        cost_estimate=cost,
        name="pair",
    )(mine, inputs, mirrored_x, dgu, mirrored_dgu)


def momentum_kernel(scale, count, *refs):
    moms, parts, outs = refs[:count], refs[count:-count], refs[-count:]
    ff = moms[0].shape[2]
    for i in range(count):
        total = parts[0][0, i * ff : (i + 1) * ff].astype(F32)
        for ref in parts[1:]:
            total = total + ref[0, i * ff : (i + 1) * ff].astype(F32)
        outs[i][0] = 0.9 * moms[i][0] + total.T * scale


def momentum(moms, parts, scale):
    shape = moms[0].shape
    _, shard, ff = shape
    count = len(moms)
    whole = pl.BlockSpec((1, shard, ff), lambda i: (0, 0, 0))
    return pl.pallas_call(
        functools.partial(momentum_kernel, scale, count),
        out_shape=(jax.ShapeDtypeStruct(shape, F32),) * count,
        grid=(1,),
        in_specs=[whole] * count + [pl.BlockSpec((1, ff * count, shard), lambda i: (0, 0, 0))] * len(parts),
        out_specs=[whole] * count,
        compiler_params=pltpu.CompilerParams(vmem_limit_bytes=2 * VMEM_LIMIT),
        cost_estimate=COST,
        name="momentum",
    )(*moms, *parts)


def shifted(value, steps, name):
    count = lax.axis_size("section")
    first, last = max(0, -steps), min(count, count - steps)
    with jax.named_scope(name):
        return lax.ppermute(value, "section", [(i, i + steps) for i in range(first, last)])


def mirrored(value, name):
    count = lax.axis_size("section")
    with jax.named_scope(name):
        return lax.ppermute(value, "section", [(i, count - 1 - i) for i in range(count)])


def swapped(value, mask, name):
    with jax.named_scope(name):
        return lax.ppermute(value, "dp", [(i, i ^ mask) for i in range(lax.axis_size("dp"))])


def after(value, earlier):
    return lax.optimization_barrier((value, earlier))[0]


def add(left, right):
    return (left.astype(F32) + right.astype(F32)).astype(BF16)


def halve(keep, received):
    (stay, go), (stayed, gone) = (jnp.split(v, 2, -3) for v in (keep, received))
    return add(stay, stayed), add(go, gone)


def join_kernel(first_ref, second_ref, out_ref):
    out_ref[0, 0] = first_ref[...]
    out_ref[0, 1] = second_ref[...]


def join(first, second):
    rows, width = first.shape
    step = min(64, rows)
    return pl.pallas_call(
        join_kernel,
        out_shape=jax.ShapeDtypeStruct((1, 2, rows, width), first.dtype),
        grid=(rows // step,),
        in_specs=[pl.BlockSpec((step, width), lambda i: (i, 0))] * 2,
        out_specs=pl.BlockSpec((1, 2, step, width), lambda i: (0, 0, i, 0)),
        compiler_params=pltpu.CompilerParams(vmem_limit_bytes=VMEM_LIMIT),
        cost_estimate=LONG,
        name="join",
    )(first, second)


def body(inputs, cotangent, w_gate, w_up, w_down, mom_gate, mom_up, mom_down):
    replicas = lax.axis_size("dp")
    _, _, rows, width = inputs.shape
    shard = width // replicas
    half = replicas // 2
    masks = [1 << i for i in range(replicas.bit_length() - 1)]
    cut = slot_offsets(replicas, masks)
    mine = lax.axis_index("dp")[None]
    scale = 1.0 / math.sqrt(rows * replicas)

    operands = (mine, inputs, cotangent, w_gate, w_up, w_down)

    dgu1, hidden1, send1, x_send, x_keep = second(*operands, cut, shard)
    dgu1_mirror = mirrored(dgu1, "dgu")
    x_send = mirrored(x_send, "x_send")
    first1 = swapped(send1, masks[0], "down1_first")
    x_keep = mirrored(x_keep, "x_keep")
    dgu0, send0, keep0, keep1, dx0, dx1 = rest(*operands, dgu1, hidden1, cut, shard)
    first0 = swapped(send0, masks[0], "down0_first")
    gate_send, up_send = pair(mine, inputs, x_send, dgu0, dgu1_mirror, cut[half:], shard, COST)
    gate = swapped(gate_send, masks[0], "gate_first")
    up = swapped(up_send, masks[0], "up_first")
    recv0 = shifted(after(dx0, gate_send), -1, "dx_first")
    recv1 = shifted(after(dx1, gate_send), 1, "dx_second")
    grad_in = join(recv0, recv1)
    gate_keep, up_keep = pair(mine, inputs, x_keep, dgu0, dgu1_mirror, cut[:half], shard, LONG)
    down_keep, down = jnp.stack([keep0, keep1]), jnp.stack([first0, first1])
    for mask in masks[1:]:
        down_keep, send = halve(down_keep, down)
        down = swapped(send, mask, "down_rest")
    for mask in masks[1:]:
        gate_keep, send = halve(gate_keep, gate)
        gate = swapped(send, mask, "gate_rest")
    for mask in masks[1:]:
        up_keep, send = halve(up_keep, up)
        up = swapped(after(send, down), mask, "up_rest")
    mirror = mirrored(add(down_keep[1], down[1]), "down_mirror")
    new_gate = momentum([mom_gate], (gate_keep, gate), scale)
    new_down = momentum([mom_down], (down_keep[0], down[0], mirror), scale)
    new_up = momentum([after(mom_up, (new_down, grad_in))], (up_keep, up), scale)
    return (grad_in, *new_gate, *new_up, *new_down)


def solution(mesh):
    tokens = P("section", None, "dp", None)
    weights = P("section", None, None, None)
    moments = P("section", "dp", None)
    return jax.shard_map(
        body,
        mesh=mesh,
        in_specs=(tokens, tokens, weights, weights, weights, moments, moments, moments),
        out_specs=(tokens, moments, moments, moments),
        check_vma=False,
    )
```

time: 98.6 us -> 94.4 us (0.957)
  waiting for transfers between devices: 60.7 us -> 50.5 us
  starting transfers between devices: 18.1 us -> 23.1 us
  Pallas kernels: 14.7 us -> 17.2 us
  other arithmetic: 2.19 us -> 0.66 us
    ppermute x4, waiting for transfers between devices: 22.8 us -> 6.8 us  [mirrored(): lax.ppermute(value, 'section', [(i, count - 1 - i) for i in range(count)])]
    ppermute x4 -> x7, starting transfers between devices: 7.58 us -> 13.5 us  [swapped(): lax.ppermute(value, 'dp', [(i, i ^ mask) for i in range(lax.axis_size('dp...]
    ppermute x4 -> x7, waiting for transfers between devices: 37.9 us -> 43.7 us  [swapped(): lax.ppermute(value, 'dp', [(i, i ^ mask) for i in range(lax.axis_size('dp...]
    pallas_call x4 -> x5, Pallas kernels: 12.5 us -> 14.2 us  [the longest x1 5.42 us: rest(): pl.pallas_call(functools.partial(rest_kernel, cut), out_shape=tuple((jax....]
    broadcast_in_dim x1 -> x0, other arithmetic: 1.5 us -> none  [body(): grad_in = jnp.stack([recv0, recv1])[None]]
    pallas_call x2 -> x3, Pallas kernels: 2.17 us -> 3 us  [momentum(): pl.pallas_call(functools.partial(momentum_kernel, scale, count), out_shap...]
  transfers between devices with their start and end apart: 10 -> 13, of which waited for: 5 -> 6; matrix products, arithmetic and copies ran while one was open for 3% -> 1% of each run, Pallas kernels for 7% -> 12%
where the time goes in v3:
time: 94.4 us; the launch traced here: 94.2 us
  waiting for transfers between devices  50.5 us (53%)
  starting transfers between devices  23.1 us (24%)
  Pallas kernels  17.2 us (18%)
  local copies, waits for them, and re-layouts  1.91 us (2%)
    ppermute x7, waiting for transfers between devices, swapped(): lax.ppermute(value, 'dp', [(i, i ^ mask) for i in range(lax.axis_size('dp...  43.7 us
    ppermute x7, starting transfers between devices, swapped(): lax.ppermute(value, 'dp', [(i, i ^ mask) for i in range(lax.axis_size('dp...  13.5 us
    ppermute x4, waiting for transfers between devices, mirrored(): lax.ppermute(value, 'section', [(i, count - 1 - i) for i in range(count)])  6.8 us
    pallas_call x1, Pallas kernels, rest(): pl.pallas_call(functools.partial(rest_kernel, cut), out_shape=tuple((jax....  5.42 us
    ppermute x4, starting transfers between devices, mirrored(): lax.ppermute(value, 'section', [(i, count - 1 - i) for i in range(count)])  5.29 us
    pallas_call x1, Pallas kernels, second(): pl.pallas_call(functools.partial(second_kernel, cut), out_shape=tuple((ja...  4.9 us
    ppermute x2, starting transfers between devices, shifted(): lax.ppermute(value, 'section', [(i, i + steps) for i in range(first, last)])  4.38 us
    pallas_call x3, Pallas kernels, momentum(): pl.pallas_call(functools.partial(momentum_kernel, scale, count), out_shap...  3 us
  transfers between devices with their start and end apart: 13, of which 6 were waited for; matrix products, arithmetic and copies ran while one was open for 1% of the time, Pallas kernels for 12%

profile of v3, /device:TPU:0, one launch (start us, length us, event | category | flops | bytes accessed | tf_op | source)
XLA Modules:
  0.0 94.2 jit_solution(3202024704690191044)
XLA Ops:
  0.6 4.9 %second.1 = (bf16[256,512]{1,0:T(8,128)(2,1)}, bf16[256,256]{1,0:T(8,128)(2,1)}, bf16[2,256,512]{2,1,0:T(8,128)(2,1)}, bf16[2,256,512]{2,1,0:T(8,128)(2,1)}, bf16[2,256,512]{2,1,0:T(8,128)(2,1)}) custom-call(s32[1]{0:T(128)} %bitcast.mine, bf16[1,2,256,2048]{3,2,1,0:T(8,128)(2,1)} %x0_ref.3, bf16[1,2,256,2048]{3,2,1,0:T(8,128)(2,1)} %y_hbm.3, ...), custom_call_target="tpu_custom_call" | custom-call | flops 1000 | bytes 1000000000 | tf_op jit(solution)/shard_map/second/pallas_call | solution.py:94
  5.5 3.4 %collective-permute-start = (bf16[2,256,512]{2,1,0:T(8,128)(2,1)}, bf16[2,256,512]{2,1,0:T(8,128)(2,1)S(1)}, u32[]{:S(2)}, u32[]{:S(2)}) collective-permute-start(bf16[2,256,512]{2,1,0:T(8,128)(2,1)} %get-tuple-element.26), channel_id=1, source_target_pairs={{0,28},{4,24},{8,20},{12,16},{16,12},{20,8},{24,4},{28,0},{1,29},{... | collective-permute-start | bytes 1572872 | tf_op jit(solution)/shard_map/x_send/ppermute | solution.py:236
  9.0 2.3 %collective-permute-start.8 = (bf16[2,256,512]{2,1,0:T(8,128)(2,1)}, bf16[2,256,512]{2,1,0:T(8,128)(2,1)S(1)}, u32[]{:S(2)}, u32[]{:S(2)}) collective-permute-start(bf16[2,256,512]{2,1,0:T(8,128)(2,1)} %get-tuple-element.37), channel_id=1, source_target_pairs={{0,1},{1,0},{2,3},{3,2},{4,5},{5,4},{6,7},{7,6},{8,9},{9,8},{10,11... | collective-permute-start | bytes 1572872 | tf_op jit(solution)/shard_map/down1_first/ppermute | solution.py:241
  11.3 0.9 %copy-done.4 = bf16[256,512]{1,0:T(8,128)(2,1)S(1)} copy-done((bf16[256,512]{1,0:T(8,128)(2,1)S(1)}, bf16[256,512]{1,0:T(8,128)(2,1)}, u32[]{:S(2)}) %copy-start.4) | copy-done | bytes 262168
  13.1 5.4 %rest.1 = (bf16[256,512]{1,0:T(8,128)(2,1)S(1)}, bf16[2,256,512]{2,1,0:T(8,128)(2,1)S(1)}, bf16[2,256,512]{2,1,0:T(8,128)(2,1)S(1)}, bf16[2,256,512]{2,1,0:T(8,1...) custom-call(s32[1]{0:T(128)} %bitcast.mine, bf16[1,2,256,2048]{3,2,1,0:T(8,128)(2,1)} %x0_ref.3, ...), custom_call_target="tpu_custom_call" | custom-call | flops 1000 | bytes 1000000000 | tf_op jit(solution)/shard_map/rest/pallas_call | solution.py:149
  18.7 1.7 %collective-permute-start.4 = (bf16[2,256,512]{2,1,0:T(8,128)(2,1)S(1)}, bf16[2,256,512]{2,1,0:T(8,128)(2,1)S(1)}, u32[]{:S(2)}, u32[]{:S(2)}) collective-permute-start(bf16[2,256,512]{2,1,0:T(8,128)(2,1)S(1)} %copy-done.6), channel_id=1, source_target_pairs={{0,28},{4,24},{8,20},{12,16},{16,12},{20,8},{24,4},{28,0},{1,29},{... | collective-permute-start | bytes 1572872 | tf_op jit(solution)/shard_map/x_keep/ppermute | solution.py:236
  20.4 6.8 %collective-permute-done.1.d1_ref = bf16[256,512]{1,0:T(8,128)(2,1)S(1)} collective-permute-done((bf16[256,512]{1,0:T(8,128)(2,1)}, bf16[256,512]{1,0:T(8,128)(2,1)S(1)}, u32[]{:S(2)}, u32[]{:S(2)}) %collective-permute-start.1) | collective-permute-done | bytes 262176 | tf_op jit(solution)/shard_map/dgu/ppermute | solution.py:236
  27.2 1.0 %pair.2 = (bf16[2,256,512]{2,1,0:T(8,128)(2,1)S(1)}, bf16[2,256,512]{2,1,0:T(8,128)(2,1)S(1)}) custom-call(s32[1]{0:T(128)} %bitcast.mine, bf16[1,2,256,2048]{3,2,1,0:T(8,128)(2,1)S(1)} %copy-done, bf16[2,256,512]{2,1,0:T(8,128)(2,1)S(1)} %collective-permute-done.x1_ref, bf16[256,512]{1,0:T(8,128)(2,1)S(1)} %get-tuple-element.27.d0_ref, ...), custom_call_target="tpu_custom_call" | custom-call | flops 1000 | bytes 1000 | tf_op jit(solution)/shard_map/pair/pallas_call | solution.py:179
  28.2 2.3 %collective-permute-start.5 = (bf16[2,256,512]{2,1,0:T(8,128)(2,1)S(1)}, bf16[2,256,512]{2,1,0:T(8,128)(2,1)S(1)}, u32[]{:S(2)}, u32[]{:S(2)}) collective-permute-start(bf16[2,256,512]{2,1,0:T(8,128)(2,1)S(1)} %get-tuple-element.28), channel_id=1, source_target_pairs={{0,1},{1,0},{2,3},{3,2},{4,5},{5,4},{6,7},{7,6},{8,9},{9,8},{10,11... | collective-permute-start | bytes 1572872 | tf_op jit(solution)/shard_map/gate_first/ppermute | solution.py:241
  30.6 4.8 %collective-permute-done.7 = bf16[2,256,512]{2,1,0:T(8,128)(2,1)S(1)} collective-permute-done((bf16[2,256,512]{2,1,0:T(8,128)(2,1)S(1)}, bf16[2,256,512]{2,1,0:T(8,128)(2,1)S(1)}, u32[]{:S(2)}, u32[]{:S(2)}) %collective-permute-start.7) | collective-permute-done | bytes 524320 | tf_op jit(solution)/shard_map/down0_first/ppermute | solution.py:241
  35.7 3.2 %collective-permute-start.9 = (bf16[2,1,256,512]{3,2,1,0:T(8,128)(2,1)S(1)}, bf16[2,1,256,512]{3,2,1,0:T(8,128)(2,1)S(1)}, u32[]{:S(2)}, u32[]{:S(2)}) collective-permute-start(bf16[2,1,256,512]{3,2,1,0:T(8,128)(2,1)S(1)} %get-tuple-element.42), channel_id=1, source_target_pairs={{0,2},{1,3},{2,0},{3,1},{4,6},{5,7},{6,4},{7,5},{8,10},{9,11},{10,... | collective-permute-start | bytes 1572872 | tf_op jit(solution)/shard_map/down_rest/ppermute | solution.py:241
  38.9 1.3 %collective-permute-start.2 = (bf16[256,2048]{1,0:T(8,128)(2,1)S(1)}, bf16[256,2048]{1,0:T(8,128)(2,1)S(1)}, u32[]{:S(2)}, u32[]{:S(2)}) collective-permute-start(bf16[256,2048]{1,0:T(8,128)(2,1)S(1)} %get-tuple-element.29), channel_id=1, source_target_pairs={{4,0},{8,4},{12,8},{16,12},{20,16},{24,20},{28,24},{5,1},{9,5},{13... | collective-permute-start | bytes 3145736 | tf_op jit(solution)/shard_map/dx_first/ppermute | solution.py:230
  40.2 3.1 %collective-permute-start.3 = (bf16[256,2048]{1,0:T(8,128)(2,1)S(1)}, bf16[256,2048]{1,0:T(8,128)(2,1)S(1)}, u32[]{:S(2)}, u32[]{:S(2)}) collective-permute-start(bf16[256,2048]{1,0:T(8,128)(2,1)S(1)} %get-tuple-element.31), channel_id=1, source_target_pairs={{0,4},{4,8},{8,12},{12,16},{16,20},{20,24},{24,28},{1,5},{5,9},{9,... | collective-permute-start | bytes 3145736 | tf_op jit(solution)/shard_map/dx_second/ppermute | solution.py:230
  43.3 1.0 %pair.3 = (bf16[2,256,512]{2,1,0:T(8,128)(2,1)S(1)}, bf16[2,256,512]{2,1,0:T(8,128)(2,1)S(1)}) custom-call(s32[1]{0:T(128)} %bitcast.mine, bf16[1,2,256,2048]{3,2,1,0:T(8,128)(2,1)S(1)} %copy-done, bf16[2,256,512]{2,1,0:T(8,128)(2,1)S(1)} %collective-permute-done.4.x1_ref, bf16[256,512]{1,0:T(8,128)(2,1)S(1)} %get-tuple-element.27.d0_ref, ...), custom_call_target="tpu_custom_call" | custom-call | flops 1000 | bytes 1000000000 | tf_op jit(solution)/shard_map/pair/pallas_call | solution.py:179
  44.4 13.5 %collective-permute-done.5 = bf16[2,256,512]{2,1,0:T(8,128)(2,1)S(1)} collective-permute-done((bf16[2,256,512]{2,1,0:T(8,128)(2,1)S(1)}, bf16[2,256,512]{2,1,0:T(8,128)(2,1)S(1)}, u32[]{:S(2)}, u32[]{:S(2)}) %collective-permute-start.5) | collective-permute-done | bytes 524320 | tf_op jit(solution)/shard_map/gate_first/ppermute | solution.py:241
  58.0 2.3 %collective-permute-start.6 = (bf16[1,256,512]{2,1,0:T(8,128)(2,1)S(1)}, bf16[1,256,512]{2,1,0:T(8,128)(2,1)S(1)}, u32[]{:S(2)}, u32[]{:S(2)}) collective-permute-start(bf16[1,256,512]{2,1,0:T(8,128)(2,1)S(1)} %get-tuple-element.46), channel_id=1, source_target_pairs={{0,2},{1,3},{2,0},{3,1},{4,6},{5,7},{6,4},{7,5},{8,10},{9,11},{10,... | collective-permute-start | bytes 786440 | tf_op jit(solution)/shard_map/gate_rest/ppermute | solution.py:241
  60.3 8.5 %collective-permute-done.11 = bf16[2,256,512]{2,1,0:T(8,128)(2,1)S(1)} collective-permute-done((bf16[2,256,512]{2,1,0:T(8,128)(2,1)S(1)}, bf16[2,256,512]{2,1,0:T(8,128)(2,1)S(1)}, u32[]{:S(2)}, u32[]{:S(2)}) %collective-permute-start.11) | collective-permute-done | bytes 524320 | tf_op jit(solution)/shard_map/up_first/ppermute | solution.py:241
  68.9 3.3 %collective-permute-start.12 = (bf16[1,256,512]{2,1,0:T(8,128)(2,1)S(1)}, bf16[1,256,512]{2,1,0:T(8,128)(2,1)S(1)}, u32[]{:S(2)}, u32[]{:S(2)}) collective-permute-start(bf16[1,256,512]{2,1,0:T(8,128)(2,1)S(1)} %get-tuple-element.41), channel_id=1, source_target_pairs={{0,2},{1,3},{2,0},{3,1},{4,6},{5,7},{6,4},{7,5},{8,10},{9,11},{10,... | collective-permute-start | bytes 786440 | tf_op jit(solution)/shard_map/up_rest/ppermute | solution.py:241
  72.4 15.2 %collective-permute-done.6.refs_2_ = bf16[1,256,512]{2,1,0:T(8,128)(2,1)S(1)} collective-permute-done((bf16[1,256,512]{2,1,0:T(8,128)(2,1)S(1)}, bf16[1,256,512]{2,1,0:T(8,128)(2,1)S(1)}, u32[]{:S(2)}, u32[]{:S(2)}) %collective-permute-start.6) | collective-permute-done | bytes 262176 | tf_op jit(solution)/shard_map/gate_rest/ppermute | solution.py:241
  87.6 1.0 %momentum.3 = f32[1,512,256]{2,1,0:T(8,128)} custom-call(f32[1,512,256]{2,1,0:T(8,128)S(1)} %copy-done.1, bf16[1,256,512]{2,1,0:T(8,128)(2,1)S(1)} %get-tuple-element.47.refs_1_, bf16[1,256,512]{2,1,0:T(8,128)(2,1)S(1)} %collective-permute-done.6.refs_2_), custom_call_target="tpu_custom_call" | custom-call | flops 1000 | bytes 1000 | tf_op jit(solution)/shard_map/momentum/pallas_call | solution.py:214
  88.7 1.0 %momentum.4 = f32[1,512,256]{2,1,0:T(8,128)} custom-call(f32[1,512,256]{2,1,0:T(8,128)S(1)} %copy-done.2, bf16[1,256,512]{2,1,0:T(8,128)(2,1)S(1)} %slice_bitcast_fusion.1.refs_1_, bf16[1,256,512]{2,1,0:T(8,128)(2,1)S(1)} %slice_bitcast_fusion.refs_2_, bf16[1,256,512]{2,1,0:T(8,128)(2,1)S(1)} %collective-permute-done.10.refs_3_), custom_call_target="tpu_custom_call" | custom-call | flops 1000 | bytes 1000 | tf_op jit(solution)/shard_map/momentum/pallas_call | solution.py:214
  89.7 1.9 %join.1 = bf16[1,2,256,2048]{3,2,1,0:T(8,128)(2,1)} custom-call(bf16[256,2048]{1,0:T(8,128)(2,1)S(1)} %collective-permute-done.2.first_ref, bf16[256,2048]{1,0:T(8,128)(2,1)S(1)} %collective-permute-done.3.second_ref), custom_call_target="tpu_custom_call" | custom-call | flops 1000 | bytes 1000000000 | tf_op jit(solution)/shard_map/join/pallas_call | solution.py:265
  91.5 1.6 %collective-permute-done.12.refs_2_ = bf16[1,256,512]{2,1,0:T(8,128)(2,1)S(1)} collective-permute-done((bf16[1,256,512]{2,1,0:T(8,128)(2,1)S(1)}, bf16[1,256,512]{2,1,0:T(8,128)(2,1)S(1)}, u32[]{:S(2)}, u32[]{:S(2)}) %collective-permute-start.12) | collective-permute-done | bytes 262176 | tf_op jit(solution)/shard_map/up_rest/ppermute | solution.py:241
  93.2 1.0 %momentum.5 = f32[1,512,256]{2,1,0:T(8,128)} custom-call(f32[1,512,256]{2,1,0:T(8,128)S(1)} %copy-done.3, bf16[1,256,512]{2,1,0:T(8,128)(2,1)S(1)} %get-tuple-element.45.refs_1_, bf16[1,256,512]{2,1,0:T(8,128)(2,1)S(1)} %collective-permute-done.12.refs_2_), custom_call_target="tpu_custom_call" | custom-call | flops 1000 | bytes 1000 | tf_op jit(solution)/shard_map/momentum/pallas_call | solution.py:214
  (30 shorter events, 2.0 us)
Async XLA Ops:
  5.5 21.7 %collective-permute-start = (bf16[2,256,512]{2,1,0:T(8,128)(2,1)}, bf16[2,256,512]{2,1,0:T(8,128)(2,1)S(1)}, u32[]{:S(2)}, u32[]{:S(2)}) collective-permute-start(bf16[2,256,512]{2,1,0:T(8,128)(2,1)} %get-tuple-element.26), channel_id=1, source_target_pairs={{0,28},{4,24},{8,20},{12,16},{16,12},{20,8},{24,4},{28,0},{1,29},{... | collective-permute-start | bytes 1572872 | tf_op jit(solution)/shard_map/x_send/ppermute | solution.py:236
  8.9 18.2 %collective-permute-start.1 = (bf16[256,512]{1,0:T(8,128)(2,1)}, bf16[256,512]{1,0:T(8,128)(2,1)S(1)}, u32[]{:S(2)}, u32[]{:S(2)}) collective-permute-start(bf16[256,512]{1,0:T(8,128)(2,1)} %get-tuple-element.23.dgu1_ref), channel_id=1, source_target_pairs={{0,28},{4,24},{8,20},{12,16},{16,12},{20,8},{24,4},{28,0},{1,29},{... | collective-permute-start | bytes 786440 | tf_op jit(solution)/shard_map/dgu/ppermute | solution.py:236
  9.0 21.6 %collective-permute-start.8 = (bf16[2,256,512]{2,1,0:T(8,128)(2,1)}, bf16[2,256,512]{2,1,0:T(8,128)(2,1)S(1)}, u32[]{:S(2)}, u32[]{:S(2)}) collective-permute-start(bf16[2,256,512]{2,1,0:T(8,128)(2,1)} %get-tuple-element.37), channel_id=1, source_target_pairs={{0,1},{1,0},{2,3},{3,2},{4,5},{5,4},{6,7},{7,6},{8,9},{9,8},{10,11... | collective-permute-start | bytes 1572872 | tf_op jit(solution)/shard_map/down1_first/ppermute | solution.py:241
  11.3 0.9 %copy-start.4 = (bf16[256,512]{1,0:T(8,128)(2,1)S(1)}, bf16[256,512]{1,0:T(8,128)(2,1)}, u32[]{:S(2)}) copy-start(bf16[256,512]{1,0:T(8,128)(2,1)} %get-tuple-element.23.dgu1_ref) | copy-start | bytes 786436
  12.2 0.9 copy-start.5
  13.1 5.5 %copy-start.6 = (bf16[2,256,512]{2,1,0:T(8,128)(2,1)S(1)}, bf16[2,256,512]{2,1,0:T(8,128)(2,1)}, u32[]{:S(2)}) copy-start(bf16[2,256,512]{2,1,0:T(8,128)(2,1)} %get-tuple-element.32) | copy-start | bytes 1572868
  13.1 14.1 %copy-start = (bf16[1,2,256,2048]{3,2,1,0:T(8,128)(2,1)S(1)}, bf16[1,2,256,2048]{3,2,1,0:T(8,128)(2,1)}, u32[]{:S(2)}) copy-start(bf16[1,2,256,2048]{3,2,1,0:T(8,128)(2,1)} %x0_ref.3) | copy-start | bytes 6291460
  18.6 16.9 %collective-permute-start.7 = (bf16[2,256,512]{2,1,0:T(8,128)(2,1)S(1)}, bf16[2,256,512]{2,1,0:T(8,128)(2,1)S(1)}, u32[]{:S(2)}, u32[]{:S(2)}) collective-permute-start(bf16[2,256,512]{2,1,0:T(8,128)(2,1)S(1)} %get-tuple-element.36), channel_id=1, source_target_pairs={{0,1},{1,0},{2,3},{3,2},{4,5},{5,4},{6,7},{7,6},{8,9},{9,8},{10,11... | collective-permute-start | bytes 1572872 | tf_op jit(solution)/shard_map/down0_first/ppermute | solution.py:241
  18.7 21.5 %collective-permute-start.4 = (bf16[2,256,512]{2,1,0:T(8,128)(2,1)S(1)}, bf16[2,256,512]{2,1,0:T(8,128)(2,1)S(1)}, u32[]{:S(2)}, u32[]{:S(2)}) collective-permute-start(bf16[2,256,512]{2,1,0:T(8,128)(2,1)S(1)} %copy-done.6), channel_id=1, source_target_pairs={{0,28},{4,24},{8,20},{12,16},{16,12},{20,8},{24,4},{28,0},{1,29},{... | collective-permute-start | bytes 1572872 | tf_op jit(solution)/shard_map/x_keep/ppermute | solution.py:236
  28.2 29.7 %collective-permute-start.5 = (bf16[2,256,512]{2,1,0:T(8,128)(2,1)S(1)}, bf16[2,256,512]{2,1,0:T(8,128)(2,1)S(1)}, u32[]{:S(2)}, u32[]{:S(2)}) collective-permute-start(bf16[2,256,512]{2,1,0:T(8,128)(2,1)S(1)} %get-tuple-element.28), channel_id=1, source_target_pairs={{0,1},{1,0},{2,3},{3,2},{4,5},{5,4},{6,7},{7,6},{8,9},{9,8},{10,11... | collective-permute-start | bytes 1572872 | tf_op jit(solution)/shard_map/gate_first/ppermute | solution.py:241
  30.6 38.2 %collective-permute-start.11 = (bf16[2,256,512]{2,1,0:T(8,128)(2,1)S(1)}, bf16[2,256,512]{2,1,0:T(8,128)(2,1)S(1)}, u32[]{:S(2)}, u32[]{:S(2)}) collective-permute-start(bf16[2,256,512]{2,1,0:T(8,128)(2,1)S(1)} %get-tuple-element.40), channel_id=1, source_target_pairs={{0,1},{1,0},{2,3},{3,2},{4,5},{5,4},{6,7},{7,6},{8,9},{9,8},{10,11... | collective-permute-start | bytes 1572872 | tf_op jit(solution)/shard_map/up_first/ppermute | solution.py:241
  35.7 33.2 %collective-permute-start.9 = (bf16[2,1,256,512]{3,2,1,0:T(8,128)(2,1)S(1)}, bf16[2,1,256,512]{3,2,1,0:T(8,128)(2,1)S(1)}, u32[]{:S(2)}, u32[]{:S(2)}) collective-permute-start(bf16[2,1,256,512]{3,2,1,0:T(8,128)(2,1)S(1)} %get-tuple-element.42), channel_id=1, source_target_pairs={{0,2},{1,3},{2,0},{3,1},{4,6},{5,7},{6,4},{7,5},{8,10},{9,11},{10,... | collective-permute-start | bytes 1572872 | tf_op jit(solution)/shard_map/down_rest/ppermute | solution.py:241
  38.9 50.7 %collective-permute-start.2 = (bf16[256,2048]{1,0:T(8,128)(2,1)S(1)}, bf16[256,2048]{1,0:T(8,128)(2,1)S(1)}, u32[]{:S(2)}, u32[]{:S(2)}) collective-permute-start(bf16[256,2048]{1,0:T(8,128)(2,1)S(1)} %get-tuple-element.29), channel_id=1, source_target_pairs={{4,0},{8,4},{12,8},{16,12},{20,16},{24,20},{28,24},{5,1},{9,5},{13... | collective-permute-start | bytes 3145736 | tf_op jit(solution)/shard_map/dx_first/ppermute | solution.py:230
  40.2 49.5 %collective-permute-start.3 = (bf16[256,2048]{1,0:T(8,128)(2,1)S(1)}, bf16[256,2048]{1,0:T(8,128)(2,1)S(1)}, u32[]{:S(2)}, u32[]{:S(2)}) collective-permute-start(bf16[256,2048]{1,0:T(8,128)(2,1)S(1)} %get-tuple-element.31), channel_id=1, source_target_pairs={{0,4},{4,8},{8,12},{12,16},{16,20},{20,24},{24,28},{1,5},{5,9},{9,... | collective-permute-start | bytes 3145736 | tf_op jit(solution)/shard_map/dx_second/ppermute | solution.py:230
  58.0 29.6 %copy-start.1 = (f32[1,512,256]{2,1,0:T(8,128)S(1)}, f32[1,512,256]{2,1,0:T(8,128)}, u32[]{:S(2)}) copy-start(f32[1,512,256]{2,1,0:T(8,128)} %refs_0_.2) | copy-start | bytes 1572868
  58.0 29.6 %collective-permute-start.6 = (bf16[1,256,512]{2,1,0:T(8,128)(2,1)S(1)}, bf16[1,256,512]{2,1,0:T(8,128)(2,1)S(1)}, u32[]{:S(2)}, u32[]{:S(2)}) collective-permute-start(bf16[1,256,512]{2,1,0:T(8,128)(2,1)S(1)} %get-tuple-element.46), channel_id=1, source_target_pairs={{0,2},{1,3},{2,0},{3,1},{4,6},{5,7},{6,4},{7,5},{8,10},{9,11},{10,... | collective-permute-start | bytes 786440 | tf_op jit(solution)/shard_map/gate_rest/ppermute | solution.py:241
  68.9 19.7 %copy-start.2 = (f32[1,512,256]{2,1,0:T(8,128)S(1)}, f32[1,512,256]{2,1,0:T(8,128)}, u32[]{:S(2)}) copy-start(f32[1,512,256]{2,1,0:T(8,128)} %refs_0_.3) | copy-start | bytes 1572868
  68.9 24.2 %collective-permute-start.12 = (bf16[1,256,512]{2,1,0:T(8,128)(2,1)S(1)}, bf16[1,256,512]{2,1,0:T(8,128)(2,1)S(1)}, u32[]{:S(2)}, u32[]{:S(2)}) collective-permute-start(bf16[1,256,512]{2,1,0:T(8,128)(2,1)S(1)} %get-tuple-element.41), channel_id=1, source_target_pairs={{0,2},{1,3},{2,0},{3,1},{4,6},{5,7},{6,4},{7,5},{8,10},{9,11},{10,... | collective-permute-start | bytes 786440 | tf_op jit(solution)/shard_map/up_rest/ppermute | solution.py:241
  72.3 16.4 %collective-permute-start.10 = (bf16[1,256,512]{2,1,0:T(8,128)(2,1)S(1)}, bf16[1,256,512]{2,1,0:T(8,128)(2,1)S(1)}, u32[]{:S(2)}, u32[]{:S(2)}) collective-permute-start(bf16[1,256,512]{2,1,0:T(8,128)(2,1)S(1)} %fusion.2), channel_id=1, source_target_pairs={{0,28},{4,24},{8,20},{12,16},{16,12},{20,8},{24,4},{28,0},{1,29},{... | collective-permute-start | bytes 786440 | tf_op jit(solution)/shard_map/down_mirror/ppermute | solution.py:236
  89.7 3.5 %copy-start.3 = (f32[1,512,256]{2,1,0:T(8,128)S(1)}, f32[1,512,256]{2,1,0:T(8,128)}, u32[]{:S(2)}) copy-start(f32[1,512,256]{2,1,0:T(8,128)} %refs_0_.4) | copy-start | bytes 1572868

commit v4 on v3

--- a/solution.py
+++ b/solution.py
@@ -12,7 +12,7 @@
 F32 = jnp.float32
 VMEM_LIMIT = 8 * 1024 * 1024
 SECOND_LIMIT = 58 * 1024 * 1024
-REST_LIMIT = 48 * 1024 * 1024
+REST_LIMIT = 54 * 1024 * 1024
 COST = pl.CostEstimate(flops=1000, bytes_accessed=1000, transcendentals=0)
 LONG = pl.CostEstimate(flops=1000, bytes_accessed=10**9, transcendentals=0)
 
@@ -57,7 +57,7 @@
         out_ref[slot] = jnp.dot(hidden_t, columns, preferred_element_type=F32).astype(BF16)
 
 
-def second_kernel(cut, mine, x_hbm, y_hbm, wg_hbm, wu_hbm, wd_hbm, dgu_ref, hidden_ref, send_ref, x_send_ref, x_keep_ref, *held):
+def second_kernel(cut, far_cut, mine, x_hbm, y_hbm, wg_hbm, wu_hbm, wd_hbm, dgu_ref, hidden_ref, send_ref, message_ref, x_keep_ref, *held):
     (x_ref, wg_ref, wu_ref, y_ref, wd_ref), sems, slot_sems = held[:5], held[5], held[6]
     half, ff, shard = send_ref.shape
     hbm = (x_hbm, wg_hbm, wu_hbm, y_hbm, wd_hbm)
@@ -65,7 +65,7 @@
     copies[0].wait()
     slots = reader(
         [
-            (x_ref.at[:, columns_of(mine, offset, shard)], (x_keep_ref if i < half else x_send_ref).at[i % half])
+            (x_ref.at[:, columns_of(mine, offset, shard)], (x_keep_ref if i < half else message_ref).at[i % half])
             for i, offset in enumerate(cut)
         ],
         slot_sems,
@@ -80,19 +80,21 @@
     hidden, dgate, dup = backward(gate, up, dhid)
     dgu_ref[:, :ff] = dgate
     dgu_ref[:, ff:] = dup
+    for i in range(half, message_ref.shape[0]):
+        message_ref[i] = dgu_ref[:, (i - half) * shard : (i - half + 1) * shard]
     hidden_ref[...] = hidden
-    slots_into(send_ref, mine, cut[half:], hidden.T, y_ref)
+    slots_into(send_ref, mine, far_cut[half:], hidden.T, y_ref)
     for copy in slots:
         copy.wait()
 
 
-def second(mine, inputs, cotangent, w_gate, w_up, w_down, cut, shard):
+def second(mine, inputs, cotangent, w_gate, w_up, w_down, cut, far_cut, shard):
     _, _, rows, width = inputs.shape
     ff = w_gate.shape[3]
     half = len(cut) // 2
-    outs = [(rows, 2 * ff), (rows, ff), (half, ff, shard), (half, rows, shard), (half, rows, shard)]
-    return pl.pallas_call(
-        functools.partial(second_kernel, cut),
+    outs = [(rows, 2 * ff), (rows, ff), (half, ff, shard), (half + 2 * ff // shard, rows, shard), (half, rows, shard)]
+    return pl.pallas_call(
+        functools.partial(second_kernel, cut, far_cut),
         out_shape=tuple(jax.ShapeDtypeStruct(dims, BF16) for dims in outs),
         in_specs=[pl.BlockSpec(memory_space=pltpu.SMEM)] + [pl.BlockSpec(memory_space=pl.ANY)] * 5,
         out_specs=[pl.BlockSpec(memory_space=pltpu.VMEM)] * len(outs),
@@ -104,7 +106,7 @@
     )(mine, inputs, cotangent, w_gate, w_up, w_down)
 
 
-def rest_kernel(cut, mine, x_hbm, y_hbm, wg_hbm, wu_hbm, wd_hbm, dgu1_ref, hidden1_ref, *refs):
+def rest_kernel(cut, far_cut, mine, x_hbm, y_hbm, wg_hbm, wu_hbm, wd_hbm, dgu1_ref, hidden1_ref, *refs):
     dgu_ref, send_ref, keep0_ref, keep1_ref, dx0_ref, dx1_ref = refs[:6]
     (x_ref, wg_ref, wu_ref, y_ref, wd_ref, y1_ref, wg1_ref, wu1_ref), sems = refs[6:14], refs[14]
     half, ff, shard = send_ref.shape
@@ -135,11 +137,11 @@
     input_gradient(dx0_ref, dgate, dup, wg_ref, wu_ref)
     for copy in copies[5:]:
         copy.wait()
-    slots_into(keep1_ref, mine, cut[:half], hidden1_ref[...].T, y1_ref)
+    slots_into(keep1_ref, mine, far_cut[:half], hidden1_ref[...].T, y1_ref)
     input_gradient(dx1_ref, dgu1_ref[:, :ff], dgu1_ref[:, ff:], wg1_ref, wu1_ref)
 
 
-def rest(mine, inputs, cotangent, w_gate, w_up, w_down, dgu1, hidden1, cut, shard):
+def rest(mine, inputs, cotangent, w_gate, w_up, w_down, dgu1, hidden1, cut, far_cut, shard):
     _, _, rows, width = inputs.shape
     ff = w_gate.shape[3]
     half = len(cut) // 2
@@ -147,7 +149,7 @@
     held = (inputs, w_gate, w_up, cotangent, w_down, cotangent, w_gate, w_up)
     vmem = pl.BlockSpec(memory_space=pltpu.VMEM)
     return pl.pallas_call(
-        functools.partial(rest_kernel, cut),
+        functools.partial(rest_kernel, cut, far_cut),
         out_shape=tuple(jax.ShapeDtypeStruct(dims, BF16) for dims in outs),
         in_specs=[pl.BlockSpec(memory_space=pltpu.SMEM)] + [pl.BlockSpec(memory_space=pl.ANY)] * 5 + [vmem] * 2,
         out_specs=[vmem] * len(outs),
@@ -161,12 +163,13 @@
 def pair_kernel(mine, x0_ref, x1_ref, d0_ref, d1_ref, *outs):
     ff = outs[0].shape[1]
     x0, x1 = x0_ref[0, 0], x1_ref[0]
+    d1 = jnp.concatenate([d1_ref[i] for i in range(d1_ref.shape[0])], axis=1)
     for i, out in enumerate(outs):
         part = slice(i * ff, (i + 1) * ff)
-        out[0] = (rows_dot(d0_ref[:, part], x0) + rows_dot(d1_ref[:, part], x1)).astype(BF16)
-
-
-def pair(mine, inputs, mirrored_x, dgu, mirrored_dgu, offsets, shard, cost):
+        out[0] = (rows_dot(d0_ref[:, part], x0) + rows_dot(d1[:, part], x1)).astype(BF16)
+
+
+def pair(mine, inputs, mirrored_x, dgu, message, offsets, shard):
     _, _, rows, _ = inputs.shape
     both = dgu.shape[1]
     ff = both // 2
@@ -176,6 +179,7 @@
         offset = sum(jnp.where(j == i, o, 0) for i, o in enumerate(offsets))
         return (0, 0, 0, z[0] ^ offset)
 
+    pieces = both // shard
     return pl.pallas_call(
         pair_kernel,
         out_shape=(jax.ShapeDtypeStruct((count, ff, shard), BF16),) * 2,
@@ -186,14 +190,14 @@
                 pl.BlockSpec((1, 1, rows, shard), column),
                 pl.BlockSpec((1, rows, shard), lambda j, z: (j, 0, 0)),
                 pl.BlockSpec((rows, both), lambda j, z: (0, 0)),
-                pl.BlockSpec((rows, both), lambda j, z: (0, 0)),
+                pl.BlockSpec((pieces, rows, shard), lambda j, z: (count // pieces, 0, 0)),
             ],
             out_specs=[pl.BlockSpec((1, ff, shard), lambda j, z: (j, 0, 0))] * 2,
         ),
         compiler_params=pltpu.CompilerParams(vmem_limit_bytes=VMEM_LIMIT),
-        cost_estimate=cost,
+        cost_estimate=LONG,
         name="pair",
-    )(mine, inputs, mirrored_x, dgu, mirrored_dgu)
+    )(mine, inputs, mirrored_x, dgu, message)
 
 
 def momentum_kernel(scale, count, *refs):
@@ -286,34 +290,36 @@
 
     operands = (mine, inputs, cotangent, w_gate, w_up, w_down)
 
-    dgu1, hidden1, send1, x_send, x_keep = second(*operands, cut, shard)
-    dgu1_mirror = mirrored(dgu1, "dgu")
-    x_send = mirrored(x_send, "x_send")
+    dgu1, hidden1, send1, message, x_keep = second(*operands, cut, cut, shard)
+    message = mirrored(message, "message")
     first1 = swapped(send1, masks[0], "down1_first")
     x_keep = mirrored(x_keep, "x_keep")
-    dgu0, send0, keep0, keep1, dx0, dx1 = rest(*operands, dgu1, hidden1, cut, shard)
+    dgu0, send0, keep0, keep1, dx0, dx1 = rest(*operands, dgu1, hidden1, cut, cut, shard)
     first0 = swapped(send0, masks[0], "down0_first")
-    gate_send, up_send = pair(mine, inputs, x_send, dgu0, dgu1_mirror, cut[half:], shard, COST)
+    for mask in masks[1:]:
+        keep1, send1 = halve(keep1, first1)
+        first1 = swapped(send1, mask, "down1_rest")
+    gate_send, up_send = pair(mine, inputs, message, after(dgu0, send1), message, cut[half:], shard)
     gate = swapped(gate_send, masks[0], "gate_first")
     up = swapped(up_send, masks[0], "up_first")
+    gate_first = gate
     recv0 = shifted(after(dx0, gate_send), -1, "dx_first")
     recv1 = shifted(after(dx1, gate_send), 1, "dx_second")
     grad_in = join(recv0, recv1)
-    gate_keep, up_keep = pair(mine, inputs, x_keep, dgu0, dgu1_mirror, cut[:half], shard, LONG)
-    down_keep, down = jnp.stack([keep0, keep1]), jnp.stack([first0, first1])
+    gate_keep, up_keep = pair(mine, inputs, x_keep, dgu0, message, cut[:half], shard)
     for mask in masks[1:]:
-        down_keep, send = halve(down_keep, down)
-        down = swapped(send, mask, "down_rest")
+        keep0, send = halve(keep0, first0)
+        first0 = swapped(send, mask, "down0_rest")
     for mask in masks[1:]:
         gate_keep, send = halve(gate_keep, gate)
-        gate = swapped(send, mask, "gate_rest")
+        gate = swapped(after(send, first0), mask, "gate_rest")
     for mask in masks[1:]:
         up_keep, send = halve(up_keep, up)
-        up = swapped(after(send, down), mask, "up_rest")
-    mirror = mirrored(add(down_keep[1], down[1]), "down_mirror")
-    new_gate = momentum([mom_gate], (gate_keep, gate), scale)
-    new_down = momentum([mom_down], (down_keep[0], down[0], mirror), scale)
-    new_up = momentum([after(mom_up, (new_down, grad_in))], (up_keep, up), scale)
+        up = swapped(send, mask, "up_rest")
+    mirror = mirrored(after(add(keep1, first1), gate_first), "down_mirror")
+    new_up = momentum([mom_up], (up_keep, up), scale)
+    new_down = momentum([mom_down], (keep0, first0, mirror), scale)
+    new_gate = momentum([after(mom_gate, (new_down, grad_in))], (gate_keep, gate), scale)
     return (grad_in, *new_gate, *new_up, *new_down)
 
 

time: 94.4 us -> 88.5 us (0.937)
  waiting for transfers between devices: 50.5 us -> 45.8 us
  starting transfers between devices: 23.1 us -> 19.8 us
  Pallas kernels: 17.2 us -> 19.3 us
    ppermute x4 -> x3, waiting for transfers between devices: 6.8 us -> 4.08 us  [mirrored(): lax.ppermute(value, 'section', [(i, count - 1 - i) for i in range(count)])]
    pallas_call x2, Pallas kernels: 10.3 us -> 12.4 us  [the longest x1 7.47 us: rest(): pl.pallas_call(functools.partial(rest_kernel, cut, far_cut), out_shape=tu...]
    ppermute x7 -> x8, waiting for transfers between devices: 43.7 us -> 41.7 us  [swapped(): lax.ppermute(value, 'dp', [(i, i ^ mask) for i in range(lax.axis_size('dp...]
    ppermute x4 -> x3, starting transfers between devices: 5.29 us -> 3.58 us  [mirrored(): lax.ppermute(value, 'section', [(i, count - 1 - i) for i in range(count)])]
    ppermute x7 -> x8, starting transfers between devices: 13.5 us -> 11.8 us  [swapped(): lax.ppermute(value, 'dp', [(i, i ^ mask) for i in range(lax.axis_size('dp...]
  transfers between devices with their start and end apart: 13 -> 13, of which waited for: 6 -> 7; matrix products, arithmetic and copies ran while one was open for 1% -> 2% of each run, Pallas kernels for 12% -> 15%
where the time goes in v4:
time: 88.5 us; the launch traced here: 88.3 us
  waiting for transfers between devices  45.8 us (52%)
  starting transfers between devices  19.8 us (22%)
  Pallas kernels  19.3 us (22%)
  other arithmetic  1.58 us (2%)
  local copies, waits for them, and re-layouts  0.99 us (1%)
    ppermute x8, waiting for transfers between devices, swapped(): lax.ppermute(value, 'dp', [(i, i ^ mask) for i in range(lax.axis_size('dp...  41.7 us
    ppermute x8, starting transfers between devices, swapped(): lax.ppermute(value, 'dp', [(i, i ^ mask) for i in range(lax.axis_size('dp...  11.8 us
    pallas_call x1, Pallas kernels, rest(): pl.pallas_call(functools.partial(rest_kernel, cut, far_cut), out_shape=tu...  7.47 us
    pallas_call x1, Pallas kernels, second(): pl.pallas_call(functools.partial(second_kernel, cut, far_cut), out_shape=...  4.98 us
    ppermute x2, starting transfers between devices, shifted(): lax.ppermute(value, 'section', [(i, i + steps) for i in range(first, last)])  4.38 us
    ppermute x3, waiting for transfers between devices, mirrored(): lax.ppermute(value, 'section', [(i, count - 1 - i) for i in range(count)])  4.08 us
    ppermute x3, starting transfers between devices, mirrored(): lax.ppermute(value, 'section', [(i, count - 1 - i) for i in range(count)])  3.58 us
    pallas_call x3, Pallas kernels, momentum(): pl.pallas_call(functools.partial(momentum_kernel, scale, count), out_shap...  3 us
  transfers between devices with their start and end apart: 13, of which 7 were waited for; matrix products, arithmetic and copies ran while one was open for 2% of the time, Pallas kernels for 15%

profile of v4, /device:TPU:0, one launch (start us, length us, event | category | flops | bytes accessed | tf_op | source)
XLA Modules:
  0.0 88.3 jit_solution(1192380065120381975)
XLA Ops:
  0.6 5.0 %second.1 = (bf16[256,512]{1,0:T(8,128)(2,1)}, bf16[256,256]{1,0:T(8,128)(2,1)}, bf16[2,256,512]{2,1,0:T(8,128)(2,1)}, bf16[3,256,512]{2,1,0:T(8,128)(2,1)}, bf16[2,256,512]{2,1,0:T(8,128)(2,1)}) custom-call(s32[1]{0:T(128)} %bitcast.mine, bf16[1,2,256,2048]{3,2,1,0:T(8,128)(2,1)} %x0_ref.3, bf16[1,2,256,2048]{3,2,1,0:T(8,128)(2,1)} %y_hbm.3, ...), custom_call_target="tpu_custom_call" | custom-call | flops 1000 | bytes 1000000000 | tf_op jit(solution)/shard_map/second/pallas_call | solution.py:96
  5.6 3.1 %collective-permute-start.1 = (bf16[2,256,512]{2,1,0:T(8,128)(2,1)}, bf16[2,256,512]{2,1,0:T(8,128)(2,1)S(1)}, u32[]{:S(2)}, u32[]{:S(2)}) collective-permute-start(bf16[2,256,512]{2,1,0:T(8,128)(2,1)} %get-tuple-element.31), channel_id=1, source_target_pairs={{0,1},{1,0},{2,3},{3,2},{4,5},{5,4},{6,7},{7,6},{8,9},{9,8},{10,11... | collective-permute-start | bytes 1572872 | tf_op jit(solution)/shard_map/down1_first/ppermute | solution.py:245
  8.7 1.6 %collective-permute-start = (bf16[3,256,512]{2,1,0:T(8,128)(2,1)}, bf16[3,256,512]{2,1,0:T(8,128)(2,1)S(1)}, u32[]{:S(2)}, u32[]{:S(2)}) collective-permute-start(bf16[3,256,512]{2,1,0:T(8,128)(2,1)} %get-tuple-element.28), channel_id=1, source_target_pairs={{0,28},{4,24},{8,20},{12,16},{16,12},{20,8},{24,4},{28,0},{1,29},{... | collective-permute-start | bytes 2359304 | tf_op jit(solution)/shard_map/message/ppermute | solution.py:240
  10.3 7.5 %rest.1 = (bf16[256,512]{1,0:T(8,128)(2,1)}, bf16[2,256,512]{2,1,0:T(8,128)(2,1)}, bf16[2,256,512]{2,1,0:T(8,128)(2,1)}, bf16[2,256,512]{2,1,0:T(8,128)(2,1)}, b...) custom-call(s32[1]{0:T(128)} %bitcast.mine, bf16[1,2,256,2048]{3,2,1,0:T(8,128)(2,1)} %x0_ref.3, ...), custom_call_target="tpu_custom_call" | custom-call | flops 1000 | bytes 1000000000 | tf_op jit(solution)/shard_map/rest/pallas_call | solution.py:151
  18.3 2.5 %collective-permute-done.1 = bf16[2,256,512]{2,1,0:T(8,128)(2,1)S(1)} collective-permute-done((bf16[2,256,512]{2,1,0:T(8,128)(2,1)}, bf16[2,256,512]{2,1,0:T(8,128)(2,1)S(1)}, u32[]{:S(2)}, u32[]{:S(2)}) %collective-permute-start.1) | collective-permute-done | bytes 524320 | tf_op jit(solution)/shard_map/down1_first/ppermute | solution.py:245
  20.8 1.1 %add_convert_fusion.8 = bf16[1,256,512]{2,1,0:T(8,128)(2,1)S(1)} fusion(bf16[2,256,512]{2,1,0:T(8,128)(2,1)S(1)} %collective-permute-done.1, bf16[2,256,512]{2,1,0:T(8,128)(2,1)} %get-tuple-element.30), kind=kLoop, calls=%fused_computation.8 | loop fusion | flops 524288 | bytes 786432 | tf_op jit(solution)/shard_map/convert_element_type | solution.py:253
  21.9 2.8 %collective-permute-start.6 = (bf16[1,256,512]{2,1,0:T(8,128)(2,1)S(1)}, bf16[1,256,512]{2,1,0:T(8,128)(2,1)S(1)}, u32[]{:S(2)}, u32[]{:S(2)}) collective-permute-start(bf16[1,256,512]{2,1,0:T(8,128)(2,1)S(1)} %add_convert_fusion.8), channel_id=1, source_target_pairs={{0,2},{1,3},{2,0},{3,1},{4,6},{5,7},{6,4},{7,5},{8,10},{9,11},{10,... | collective-permute-start | bytes 786440 | tf_op jit(solution)/shard_map/down1_rest/ppermute | solution.py:245
  25.5 4.1 %collective-permute-done.x1_ref.d1_ref = bf16[3,256,512]{2,1,0:T(8,128)(2,1)S(1)} collective-permute-done((bf16[3,256,512]{2,1,0:T(8,128)(2,1)}, bf16[3,256,512]{2,1,0:T(8,128)(2,1)S(1)}, u32[]{:S(2)}, u32[]{:S(2)}) %collective-permute-start) | collective-permute-done | bytes 786464 | tf_op jit(solution)/shard_map/message/ppermute | solution.py:240
  30.5 1.0 %pair.2 = (bf16[2,256,512]{2,1,0:T(8,128)(2,1)S(1)}, bf16[2,256,512]{2,1,0:T(8,128)(2,1)S(1)}) custom-call(s32[1]{0:T(128)} %bitcast.mine, bf16[1,2,256,2048]{3,2,1,0:T(8,128)(2,1)S(1)} %copy-done, bf16[3,256,512]{2,1,0:T(8,128)(2,1)S(1)} %collective-permute-done.x1_ref.d1_ref, bf16[256,512]{1,0:T(8,128)(2,1)S(1)} %copy-done.1, ...), custom_call_target="tpu_custom_call" | custom-call | flops 1000 | bytes 1000000000 | tf_op jit(solution)/shard_map/pair/pallas_call | solution.py:183
  31.6 2.0 %collective-permute-start.7 = (bf16[2,256,512]{2,1,0:T(8,128)(2,1)S(1)}, bf16[2,256,512]{2,1,0:T(8,128)(2,1)S(1)}, u32[]{:S(2)}, u32[]{:S(2)}) collective-permute-start(bf16[2,256,512]{2,1,0:T(8,128)(2,1)S(1)} %get-tuple-element.33), channel_id=1, source_target_pairs={{0,1},{1,0},{2,3},{3,2},{4,5},{5,4},{6,7},{7,6},{8,9},{9,8},{10,11... | collective-permute-start | bytes 1572872 | tf_op jit(solution)/shard_map/gate_first/ppermute | solution.py:245
  33.6 4.8 %collective-permute-done.4 = bf16[2,256,512]{2,1,0:T(8,128)(2,1)S(1)} collective-permute-done((bf16[2,256,512]{2,1,0:T(8,128)(2,1)}, bf16[2,256,512]{2,1,0:T(8,128)(2,1)S(1)}, u32[]{:S(2)}, u32[]{:S(2)}) %collective-permute-start.4) | collective-permute-done | bytes 524320 | tf_op jit(solution)/shard_map/down0_first/ppermute | solution.py:245
  38.5 1.3 %collective-permute-start.2 = (bf16[256,2048]{1,0:T(8,128)(2,1)S(1)}, bf16[256,2048]{1,0:T(8,128)(2,1)S(1)}, u32[]{:S(2)}, u32[]{:S(2)}) collective-permute-start(bf16[256,2048]{1,0:T(8,128)(2,1)S(1)} %copy-done.9), channel_id=1, source_target_pairs={{4,0},{8,4},{12,8},{16,12},{20,16},{24,20},{28,24},{5,1},{9,5},{13... | collective-permute-start | bytes 3145736 | tf_op jit(solution)/shard_map/dx_first/ppermute | solution.py:234
  39.8 3.1 %collective-permute-start.3 = (bf16[256,2048]{1,0:T(8,128)(2,1)S(1)}, bf16[256,2048]{1,0:T(8,128)(2,1)S(1)}, u32[]{:S(2)}, u32[]{:S(2)}) collective-permute-start(bf16[256,2048]{1,0:T(8,128)(2,1)S(1)} %copy-done.8), channel_id=1, source_target_pairs={{0,4},{4,8},{8,12},{12,16},{16,20},{20,24},{24,28},{1,5},{5,9},{9,... | collective-permute-start | bytes 3145736 | tf_op jit(solution)/shard_map/dx_second/ppermute | solution.py:234
  43.2 1.7 %collective-permute-start.5 = (bf16[1,256,512]{2,1,0:T(8,128)(2,1)S(1)}, bf16[1,256,512]{2,1,0:T(8,128)(2,1)S(1)}, u32[]{:S(2)}, u32[]{:S(2)}) collective-permute-start(bf16[1,256,512]{2,1,0:T(8,128)(2,1)S(1)} %get-tuple-element.50), channel_id=1, source_target_pairs={{0,2},{1,3},{2,0},{3,1},{4,6},{5,7},{6,4},{7,5},{8,10},{9,11},{10,... | collective-permute-start | bytes 786440 | tf_op jit(solution)/shard_map/down0_rest/ppermute | solution.py:245
  44.9 1.0 %pair.3 = (bf16[2,256,512]{2,1,0:T(8,128)(2,1)S(1)}, bf16[2,256,512]{2,1,0:T(8,128)(2,1)S(1)}) custom-call(s32[1]{0:T(128)} %bitcast.mine, bf16[1,2,256,2048]{3,2,1,0:T(8,128)(2,1)S(1)} %copy-done, bf16[2,256,512]{2,1,0:T(8,128)(2,1)S(1)} %collective-permute-done.9.x1_ref, bf16[256,512]{1,0:T(8,128)(2,1)S(1)} %copy-done.2, ...), custom_call_target="tpu_custom_call" | custom-call | flops 1000 | bytes 1000000000 | tf_op jit(solution)/shard_map/pair/pallas_call | solution.py:183
  45.9 9.5 %collective-permute-done.11 = bf16[2,256,512]{2,1,0:T(8,128)(2,1)S(1)} collective-permute-done((bf16[2,256,512]{2,1,0:T(8,128)(2,1)S(1)}, bf16[2,256,512]{2,1,0:T(8,128)(2,1)S(1)}, u32[]{:S(2)}, u32[]{:S(2)}) %collective-permute-start.11) | collective-permute-done | bytes 524320 | tf_op jit(solution)/shard_map/up_first/ppermute | solution.py:245
  55.5 1.6 %collective-permute-start.12 = (bf16[1,256,512]{2,1,0:T(8,128)(2,1)S(1)}, bf16[1,256,512]{2,1,0:T(8,128)(2,1)S(1)}, u32[]{:S(2)}, u32[]{:S(2)}) collective-permute-start(bf16[1,256,512]{2,1,0:T(8,128)(2,1)S(1)} %get-tuple-element.46), channel_id=1, source_target_pairs={{0,2},{1,3},{2,0},{3,1},{4,6},{5,7},{6,4},{7,5},{8,10},{9,11},{10,... | collective-permute-start | bytes 786440 | tf_op jit(solution)/shard_map/up_rest/ppermute | solution.py:245
  57.0 13.4 %collective-permute-done.7 = bf16[2,256,512]{2,1,0:T(8,128)(2,1)S(1)} collective-permute-done((bf16[2,256,512]{2,1,0:T(8,128)(2,1)S(1)}, bf16[2,256,512]{2,1,0:T(8,128)(2,1)S(1)}, u32[]{:S(2)}, u32[]{:S(2)}) %collective-permute-start.7) | collective-permute-done | bytes 524320 | tf_op jit(solution)/shard_map/gate_first/ppermute | solution.py:245
  70.5 1.2 %collective-permute-start.8 = (bf16[1,256,512]{2,1,0:T(8,128)(2,1)S(1)}, bf16[1,256,512]{2,1,0:T(8,128)(2,1)S(1)}, u32[]{:S(2)}, u32[]{:S(2)}) collective-permute-start(bf16[1,256,512]{2,1,0:T(8,128)(2,1)S(1)} %add_convert_fusion.4), channel_id=1, source_target_pairs={{0,28},{4,24},{8,20},{12,16},{16,12},{20,8},{24,4},{28,0},{1,29},{... | collective-permute-start | bytes 786440 | tf_op jit(solution)/shard_map/down_mirror/ppermute | solution.py:240
  71.9 10.2 %collective-permute-done.12.refs_2_ = bf16[1,256,512]{2,1,0:T(8,128)(2,1)S(1)} collective-permute-done((bf16[1,256,512]{2,1,0:T(8,128)(2,1)S(1)}, bf16[1,256,512]{2,1,0:T(8,128)(2,1)S(1)}, u32[]{:S(2)}, u32[]{:S(2)}) %collective-permute-start.12) | collective-permute-done | bytes 262176 | tf_op jit(solution)/shard_map/up_rest/ppermute | solution.py:245
  82.2 1.0 %momentum.5 = f32[1,512,256]{2,1,0:T(8,128)} custom-call(f32[1,512,256]{2,1,0:T(8,128)S(1)} %copy-done.3, bf16[1,256,512]{2,1,0:T(8,128)(2,1)S(1)} %get-tuple-element.47.refs_1_, bf16[1,256,512]{2,1,0:T(8,128)(2,1)S(1)} %collective-permute-done.12.refs_2_), custom_call_target="tpu_custom_call" | custom-call | flops 1000 | bytes 1000 | tf_op jit(solution)/shard_map/momentum/pallas_call | solution.py:218
  83.2 1.0 %momentum.3 = f32[1,512,256]{2,1,0:T(8,128)} custom-call(f32[1,512,256]{2,1,0:T(8,128)S(1)} %copy-done.4, bf16[1,256,512]{2,1,0:T(8,128)(2,1)S(1)} %get-tuple-element.51.refs_1_, bf16[1,256,512]{2,1,0:T(8,128)(2,1)S(1)} %collective-permute-done.5.refs_2_, bf16[1,256,512]{2,1,0:T(8,128)(2,1)S(1)} %collective-permute-done.8.refs_3_), custom_call_target="tpu_custom_call" | custom-call | flops 1000 | bytes 1000 | tf_op jit(solution)/shard_map/momentum/pallas_call | solution.py:218
  84.2 1.9 %join.1 = bf16[1,2,256,2048]{3,2,1,0:T(8,128)(2,1)} custom-call(bf16[256,2048]{1,0:T(8,128)(2,1)S(1)} %collective-permute-done.2.first_ref, bf16[256,2048]{1,0:T(8,128)(2,1)S(1)} %collective-permute-done.3.second_ref), custom_call_target="tpu_custom_call" | custom-call | flops 1000 | bytes 1000000000 | tf_op jit(solution)/shard_map/join/pallas_call | solution.py:269
  86.0 1.2 %collective-permute-done.10.refs_2_ = bf16[1,256,512]{2,1,0:T(8,128)(2,1)S(1)} collective-permute-done((bf16[1,256,512]{2,1,0:T(8,128)(2,1)S(1)}, bf16[1,256,512]{2,1,0:T(8,128)(2,1)S(1)}, u32[]{:S(2)}, u32[]{:S(2)}) %collective-permute-start.10) | collective-permute-done | bytes 262176 | tf_op jit(solution)/shard_map/gate_rest/ppermute | solution.py:245
  (37 shorter events, 3.9 us)
Async XLA Ops:
  5.6 15.2 %collective-permute-start.1 = (bf16[2,256,512]{2,1,0:T(8,128)(2,1)}, bf16[2,256,512]{2,1,0:T(8,128)(2,1)S(1)}, u32[]{:S(2)}, u32[]{:S(2)}) collective-permute-start(bf16[2,256,512]{2,1,0:T(8,128)(2,1)} %get-tuple-element.31), channel_id=1, source_target_pairs={{0,1},{1,0},{2,3},{3,2},{4,5},{5,4},{6,7},{7,6},{8,9},{9,8},{10,11... | collective-permute-start | bytes 1572872 | tf_op jit(solution)/shard_map/down1_first/ppermute | solution.py:245
  8.7 20.8 %collective-permute-start = (bf16[3,256,512]{2,1,0:T(8,128)(2,1)}, bf16[3,256,512]{2,1,0:T(8,128)(2,1)S(1)}, u32[]{:S(2)}, u32[]{:S(2)}) collective-permute-start(bf16[3,256,512]{2,1,0:T(8,128)(2,1)} %get-tuple-element.28), channel_id=1, source_target_pairs={{0,28},{4,24},{8,20},{12,16},{16,12},{20,8},{24,4},{28,0},{1,29},{... | collective-permute-start | bytes 2359304 | tf_op jit(solution)/shard_map/message/ppermute | solution.py:240
  10.3 14.4 %copy-start.10 = (bf16[2,256,512]{2,1,0:T(8,128)(2,1)S(1)}, bf16[2,256,512]{2,1,0:T(8,128)(2,1)}, u32[]{:S(2)}) copy-start(bf16[2,256,512]{2,1,0:T(8,128)(2,1)} %get-tuple-element.41) | copy-start | bytes 1572868
  10.3 19.2 %copy-start = (bf16[1,2,256,2048]{3,2,1,0:T(8,128)(2,1)S(1)}, bf16[1,2,256,2048]{3,2,1,0:T(8,128)(2,1)}, u32[]{:S(2)}) copy-start(bf16[1,2,256,2048]{3,2,1,0:T(8,128)(2,1)} %x0_ref.3) | copy-start | bytes 6291460
  17.8 20.7 %collective-permute-start.4 = (bf16[2,256,512]{2,1,0:T(8,128)(2,1)}, bf16[2,256,512]{2,1,0:T(8,128)(2,1)S(1)}, u32[]{:S(2)}, u32[]{:S(2)}) collective-permute-start(bf16[2,256,512]{2,1,0:T(8,128)(2,1)} %get-tuple-element.38), channel_id=1, source_target_pairs={{0,1},{1,0},{2,3},{3,2},{4,5},{5,4},{6,7},{7,6},{8,9},{9,8},{10,11... | collective-permute-start | bytes 1572872 | tf_op jit(solution)/shard_map/down0_first/ppermute | solution.py:245
  20.8 22.1 %copy-start.6 = (bf16[2,256,512]{2,1,0:T(8,128)(2,1)S(1)}, bf16[2,256,512]{2,1,0:T(8,128)(2,1)}, u32[]{:S(2)}) copy-start(bf16[2,256,512]{2,1,0:T(8,128)(2,1)} %get-tuple-element.37) | copy-start | bytes 1572868
  21.9 17.9 %collective-permute-start.6 = (bf16[1,256,512]{2,1,0:T(8,128)(2,1)S(1)}, bf16[1,256,512]{2,1,0:T(8,128)(2,1)S(1)}, u32[]{:S(2)}, u32[]{:S(2)}) collective-permute-start(bf16[1,256,512]{2,1,0:T(8,128)(2,1)S(1)} %add_convert_fusion.8), channel_id=1, source_target_pairs={{0,2},{1,3},{2,0},{3,1},{4,6},{5,7},{6,4},{7,5},{8,10},{9,11},{10,... | collective-permute-start | bytes 786440 | tf_op jit(solution)/shard_map/down1_rest/ppermute | solution.py:245
  24.7 18.4 %collective-permute-start.9 = (bf16[2,256,512]{2,1,0:T(8,128)(2,1)S(1)}, bf16[2,256,512]{2,1,0:T(8,128)(2,1)S(1)}, u32[]{:S(2)}, u32[]{:S(2)}) collective-permute-start(bf16[2,256,512]{2,1,0:T(8,128)(2,1)S(1)} %copy-done.10), channel_id=1, source_target_pairs={{0,28},{4,24},{8,20},{12,16},{16,12},{20,8},{24,4},{28,0},{1,29},{... | collective-permute-start | bytes 1572872 | tf_op jit(solution)/shard_map/x_keep/ppermute | solution.py:240
  29.6 1.0 %copy-start.1 = (bf16[256,512]{1,0:T(8,128)(2,1)S(1)}, bf16[256,512]{1,0:T(8,128)(2,1)}, u32[]{:S(2)}) copy-start(bf16[256,512]{1,0:T(8,128)(2,1)} %get-tuple-element.32.d0_ref) | copy-start | bytes 786436
  30.5 8.0 %copy-start.9 = (bf16[256,2048]{1,0:T(8,128)(2,1)S(1)}, bf16[256,2048]{1,0:T(8,128)(2,1)}, u32[]{:S(2)}) copy-start(bf16[256,2048]{1,0:T(8,128)(2,1)} %get-tuple-element.34) | copy-start | bytes 3145732
  30.5 9.3 %copy-start.8 = (bf16[256,2048]{1,0:T(8,128)(2,1)S(1)}, bf16[256,2048]{1,0:T(8,128)(2,1)}, u32[]{:S(2)}) copy-start(bf16[256,2048]{1,0:T(8,128)(2,1)} %get-tuple-element.36) | copy-start | bytes 3145732
  30.5 12.5 %copy-start.7 = (bf16[2,256,512]{2,1,0:T(8,128)(2,1)S(1)}, bf16[2,256,512]{2,1,0:T(8,128)(2,1)}, u32[]{:S(2)}) copy-start(bf16[2,256,512]{2,1,0:T(8,128)(2,1)} %get-tuple-element.30) | copy-start | bytes 1572868
  31.5 13.3 %copy-start.2 = (bf16[256,512]{1,0:T(8,128)(2,1)S(1)}, bf16[256,512]{1,0:T(8,128)(2,1)}, u32[]{:S(2)}) copy-start(bf16[256,512]{1,0:T(8,128)(2,1)} %get-tuple-element.32.d0_ref) | copy-start | bytes 786436
  31.6 23.8 %collective-permute-start.11 = (bf16[2,256,512]{2,1,0:T(8,128)(2,1)S(1)}, bf16[2,256,512]{2,1,0:T(8,128)(2,1)S(1)}, u32[]{:S(2)}, u32[]{:S(2)}) collective-permute-start(bf16[2,256,512]{2,1,0:T(8,128)(2,1)S(1)} %get-tuple-element.45), channel_id=1, source_target_pairs={{0,1},{1,0},{2,3},{3,2},{4,5},{5,4},{6,7},{7,6},{8,9},{9,8},{10,11... | collective-permute-start | bytes 1572872 | tf_op jit(solution)/shard_map/up_first/ppermute | solution.py:245
  31.6 38.8 %collective-permute-start.7 = (bf16[2,256,512]{2,1,0:T(8,128)(2,1)S(1)}, bf16[2,256,512]{2,1,0:T(8,128)(2,1)S(1)}, u32[]{:S(2)}, u32[]{:S(2)}) collective-permute-start(bf16[2,256,512]{2,1,0:T(8,128)(2,1)S(1)} %get-tuple-element.33), channel_id=1, source_target_pairs={{0,1},{1,0},{2,3},{3,2},{4,5},{5,4},{6,7},{7,6},{8,9},{9,8},{10,11... | collective-permute-start | bytes 1572872 | tf_op jit(solution)/shard_map/gate_first/ppermute | solution.py:245
  38.5 45.7 %collective-permute-start.2 = (bf16[256,2048]{1,0:T(8,128)(2,1)S(1)}, bf16[256,2048]{1,0:T(8,128)(2,1)S(1)}, u32[]{:S(2)}, u32[]{:S(2)}) collective-permute-start(bf16[256,2048]{1,0:T(8,128)(2,1)S(1)} %copy-done.9), channel_id=1, source_target_pairs={{4,0},{8,4},{12,8},{16,12},{20,16},{24,20},{28,24},{5,1},{9,5},{13... | collective-permute-start | bytes 3145736 | tf_op jit(solution)/shard_map/dx_first/ppermute | solution.py:234
  39.8 44.4 %collective-permute-start.3 = (bf16[256,2048]{1,0:T(8,128)(2,1)S(1)}, bf16[256,2048]{1,0:T(8,128)(2,1)S(1)}, u32[]{:S(2)}, u32[]{:S(2)}) collective-permute-start(bf16[256,2048]{1,0:T(8,128)(2,1)S(1)} %copy-done.8), channel_id=1, source_target_pairs={{0,4},{4,8},{8,12},{12,16},{16,20},{20,24},{24,28},{1,5},{5,9},{9,... | collective-permute-start | bytes 3145736 | tf_op jit(solution)/shard_map/dx_second/ppermute | solution.py:234
  43.2 28.6 %collective-permute-start.5 = (bf16[1,256,512]{2,1,0:T(8,128)(2,1)S(1)}, bf16[1,256,512]{2,1,0:T(8,128)(2,1)S(1)}, u32[]{:S(2)}, u32[]{:S(2)}) collective-permute-start(bf16[1,256,512]{2,1,0:T(8,128)(2,1)S(1)} %get-tuple-element.50), channel_id=1, source_target_pairs={{0,2},{1,3},{2,0},{3,1},{4,6},{5,7},{6,4},{7,5},{8,10},{9,11},{10,... | collective-permute-start | bytes 786440 | tf_op jit(solution)/shard_map/down0_rest/ppermute | solution.py:245
  45.9 36.3 %copy-start.3 = (f32[1,512,256]{2,1,0:T(8,128)S(1)}, f32[1,512,256]{2,1,0:T(8,128)}, u32[]{:S(2)}) copy-start(f32[1,512,256]{2,1,0:T(8,128)} %refs_0_.4) | copy-start | bytes 1572868
  55.3 27.8 %copy-start.4 = (f32[1,512,256]{2,1,0:T(8,128)S(1)}, f32[1,512,256]{2,1,0:T(8,128)}, u32[]{:S(2)}) copy-start(f32[1,512,256]{2,1,0:T(8,128)} %refs_0_.2) | copy-start | bytes 1572868
  55.5 26.7 %collective-permute-start.12 = (bf16[1,256,512]{2,1,0:T(8,128)(2,1)S(1)}, bf16[1,256,512]{2,1,0:T(8,128)(2,1)S(1)}, u32[]{:S(2)}, u32[]{:S(2)}) collective-permute-start(bf16[1,256,512]{2,1,0:T(8,128)(2,1)S(1)} %get-tuple-element.46), channel_id=1, source_target_pairs={{0,2},{1,3},{2,0},{3,1},{4,6},{5,7},{6,4},{7,5},{8,10},{9,11},{10,... | collective-permute-start | bytes 786440 | tf_op jit(solution)/shard_map/up_rest/ppermute | solution.py:245
  70.5 12.7 %collective-permute-start.8 = (bf16[1,256,512]{2,1,0:T(8,128)(2,1)S(1)}, bf16[1,256,512]{2,1,0:T(8,128)(2,1)S(1)}, u32[]{:S(2)}, u32[]{:S(2)}) collective-permute-start(bf16[1,256,512]{2,1,0:T(8,128)(2,1)S(1)} %add_convert_fusion.4), channel_id=1, source_target_pairs={{0,28},{4,24},{8,20},{12,16},{16,12},{20,8},{24,4},{28,0},{1,29},{... | collective-permute-start | bytes 786440 | tf_op jit(solution)/shard_map/down_mirror/ppermute | solution.py:240
  71.8 15.4 %collective-permute-start.10 = (bf16[1,256,512]{2,1,0:T(8,128)(2,1)S(1)}, bf16[1,256,512]{2,1,0:T(8,128)(2,1)S(1)}, u32[]{:S(2)}, u32[]{:S(2)}) collective-permute-start(bf16[1,256,512]{2,1,0:T(8,128)(2,1)S(1)} %get-tuple-element.43), channel_id=1, source_target_pairs={{0,2},{1,3},{2,0},{3,1},{4,6},{5,7},{6,4},{7,5},{8,10},{9,11},{10,... | collective-permute-start | bytes 786440 | tf_op jit(solution)/shard_map/gate_rest/ppermute | solution.py:245
  84.2 3.1 %copy-start.5 = (f32[1,512,256]{2,1,0:T(8,128)S(1)}, f32[1,512,256]{2,1,0:T(8,128)}, u32[]{:S(2)}) copy-start(f32[1,512,256]{2,1,0:T(8,128)} %refs_0_.3) | copy-start | bytes 1572868

commit v5 on v4

--- a/solution.py
+++ b/solution.py
@@ -293,7 +293,7 @@
     dgu1, hidden1, send1, message, x_keep = second(*operands, cut, cut, shard)
     message = mirrored(message, "message")
     first1 = swapped(send1, masks[0], "down1_first")
-    x_keep = mirrored(x_keep, "x_keep")
+    x_keep = mirrored(after(x_keep, message), "x_keep")
     dgu0, send0, keep0, keep1, dx0, dx1 = rest(*operands, dgu1, hidden1, cut, cut, shard)
     first0 = swapped(send0, masks[0], "down0_first")
     for mask in masks[1:]:

time: 88.5 us -> 88.5 us (level)
  waiting for transfers between devices: 45.8 us -> 43.8 us
  starting transfers between devices: 19.8 us -> 21.7 us
    ppermute x8, waiting for transfers between devices: 41.7 us -> 37.8 us  [swapped(): lax.ppermute(value, 'dp', [(i, i ^ mask) for i in range(lax.axis_size('dp...]
    ppermute x3, waiting for transfers between devices: 4.08 us -> 6.01 us  [mirrored(): lax.ppermute(value, 'section', [(i, count - 1 - i) for i in range(count)])]
    ppermute x3, starting transfers between devices: 3.58 us -> 4.58 us  [mirrored(): lax.ppermute(value, 'section', [(i, count - 1 - i) for i in range(count)])]
    ppermute x8, starting transfers between devices: 11.8 us -> 12.8 us  [swapped(): lax.ppermute(value, 'dp', [(i, i ^ mask) for i in range(lax.axis_size('dp...]
  transfers between devices with their start and end apart: 13 -> 13, of which waited for: 7 -> 8; matrix products, arithmetic and copies ran while one was open for 2% -> 2% of each run, Pallas kernels for 15% -> 15%
where the time goes in v5:
time: 88.5 us; the launch traced here: 88.3 us
  waiting for transfers between devices  43.8 us (49%)
  starting transfers between devices  21.7 us (25%)
  Pallas kernels  19.3 us (22%)
  other arithmetic  1.58 us (2%)
  local copies, waits for them, and re-layouts  0.99 us (1%)
    ppermute x8, waiting for transfers between devices, swapped(): lax.ppermute(value, 'dp', [(i, i ^ mask) for i in range(lax.axis_size('dp...  37.8 us
    ppermute x8, starting transfers between devices, swapped(): lax.ppermute(value, 'dp', [(i, i ^ mask) for i in range(lax.axis_size('dp...  12.8 us
    pallas_call x1, Pallas kernels, rest(): pl.pallas_call(functools.partial(rest_kernel, cut, far_cut), out_shape=tu...  7.47 us
    ppermute x3, waiting for transfers between devices, mirrored(): lax.ppermute(value, 'section', [(i, count - 1 - i) for i in range(count)])  6.01 us
    pallas_call x1, Pallas kernels, second(): pl.pallas_call(functools.partial(second_kernel, cut, far_cut), out_shape=...  4.98 us
    ppermute x3, starting transfers between devices, mirrored(): lax.ppermute(value, 'section', [(i, count - 1 - i) for i in range(count)])  4.58 us
    ppermute x2, starting transfers between devices, shifted(): lax.ppermute(value, 'section', [(i, i + steps) for i in range(first, last)])  4.38 us
    pallas_call x3, Pallas kernels, momentum(): pl.pallas_call(functools.partial(momentum_kernel, scale, count), out_shap...  3 us
  transfers between devices with their start and end apart: 13, of which 8 were waited for; matrix products, arithmetic and copies ran while one was open for 2% of the time, Pallas kernels for 15%

profile of v5, /device:TPU:0, one launch (start us, length us, event | category | flops | bytes accessed | tf_op | source)
XLA Modules:
  0.0 88.3 jit_solution(5812300261373580586)
XLA Ops:
  0.6 5.0 %second.1 = (bf16[256,512]{1,0:T(8,128)(2,1)}, bf16[256,256]{1,0:T(8,128)(2,1)}, bf16[2,256,512]{2,1,0:T(8,128)(2,1)}, bf16[3,256,512]{2,1,0:T(8,128)(2,1)}, bf16[2,256,512]{2,1,0:T(8,128)(2,1)}) custom-call(s32[1]{0:T(128)} %bitcast.mine, bf16[1,2,256,2048]{3,2,1,0:T(8,128)(2,1)} %x0_ref.3, bf16[1,2,256,2048]{3,2,1,0:T(8,128)(2,1)} %y_hbm.3, ...), custom_call_target="tpu_custom_call" | custom-call | flops 1000 | bytes 1000000000 | tf_op jit(solution)/shard_map/second/pallas_call | solution.py:96
  5.6 3.1 %collective-permute-start.1 = (bf16[2,256,512]{2,1,0:T(8,128)(2,1)}, bf16[2,256,512]{2,1,0:T(8,128)(2,1)S(1)}, u32[]{:S(2)}, u32[]{:S(2)}) collective-permute-start(bf16[2,256,512]{2,1,0:T(8,128)(2,1)} %get-tuple-element.32), channel_id=1, source_target_pairs={{0,1},{1,0},{2,3},{3,2},{4,5},{5,4},{6,7},{7,6},{8,9},{9,8},{10,11... | collective-permute-start | bytes 1572872 | tf_op jit(solution)/shard_map/down1_first/ppermute | solution.py:245
  8.7 1.6 %collective-permute-start = (bf16[3,256,512]{2,1,0:T(8,128)(2,1)}, bf16[3,256,512]{2,1,0:T(8,128)(2,1)S(1)}, u32[]{:S(2)}, u32[]{:S(2)}) collective-permute-start(bf16[3,256,512]{2,1,0:T(8,128)(2,1)} %get-tuple-element.29), channel_id=1, source_target_pairs={{0,28},{4,24},{8,20},{12,16},{16,12},{20,8},{24,4},{28,0},{1,29},{... | collective-permute-start | bytes 2359304 | tf_op jit(solution)/shard_map/message/ppermute | solution.py:240
  10.3 7.5 %rest.1 = (bf16[256,512]{1,0:T(8,128)(2,1)}, bf16[2,256,512]{2,1,0:T(8,128)(2,1)}, bf16[2,256,512]{2,1,0:T(8,128)(2,1)}, bf16[2,256,512]{2,1,0:T(8,128)(2,1)}, b...) custom-call(s32[1]{0:T(128)} %bitcast.mine, bf16[1,2,256,2048]{3,2,1,0:T(8,128)(2,1)} %x0_ref.3, ...), custom_call_target="tpu_custom_call" | custom-call | flops 1000 | bytes 1000000000 | tf_op jit(solution)/shard_map/rest/pallas_call | solution.py:151
  18.3 2.5 %collective-permute-done.1 = bf16[2,256,512]{2,1,0:T(8,128)(2,1)S(1)} collective-permute-done((bf16[2,256,512]{2,1,0:T(8,128)(2,1)}, bf16[2,256,512]{2,1,0:T(8,128)(2,1)S(1)}, u32[]{:S(2)}, u32[]{:S(2)}) %collective-permute-start.1) | collective-permute-done | bytes 524320 | tf_op jit(solution)/shard_map/down1_first/ppermute | solution.py:245
  20.8 1.1 %add_convert_fusion.8 = bf16[1,256,512]{2,1,0:T(8,128)(2,1)S(1)} fusion(bf16[2,256,512]{2,1,0:T(8,128)(2,1)S(1)} %collective-permute-done.1, bf16[2,256,512]{2,1,0:T(8,128)(2,1)} %get-tuple-element.31), kind=kLoop, calls=%fused_computation.8 | loop fusion | flops 524288 | bytes 786432 | tf_op jit(solution)/shard_map/convert_element_type | solution.py:253
  21.9 2.8 %collective-permute-start.6 = (bf16[1,256,512]{2,1,0:T(8,128)(2,1)S(1)}, bf16[1,256,512]{2,1,0:T(8,128)(2,1)S(1)}, u32[]{:S(2)}, u32[]{:S(2)}) collective-permute-start(bf16[1,256,512]{2,1,0:T(8,128)(2,1)S(1)} %add_convert_fusion.8), channel_id=1, source_target_pairs={{0,2},{1,3},{2,0},{3,1},{4,6},{5,7},{6,4},{7,5},{8,10},{9,11},{10,... | collective-permute-start | bytes 786440 | tf_op jit(solution)/shard_map/down1_rest/ppermute | solution.py:245
  24.7 4.8 %collective-permute-done.x1_ref.d1_ref = bf16[3,256,512]{2,1,0:T(8,128)(2,1)S(1)} collective-permute-done((bf16[3,256,512]{2,1,0:T(8,128)(2,1)}, bf16[3,256,512]{2,1,0:T(8,128)(2,1)S(1)}, u32[]{:S(2)}, u32[]{:S(2)}) %collective-permute-start) | collective-permute-done | bytes 786464 | tf_op jit(solution)/shard_map/message/ppermute | solution.py:240
  29.6 1.7 %collective-permute-start.9 = (bf16[2,256,512]{2,1,0:T(8,128)(2,1)S(1)}, bf16[2,256,512]{2,1,0:T(8,128)(2,1)S(1)}, u32[]{:S(2)}, u32[]{:S(2)}) collective-permute-start(bf16[2,256,512]{2,1,0:T(8,128)(2,1)S(1)} %copy-done.10), channel_id=1, source_target_pairs={{0,28},{4,24},{8,20},{12,16},{16,12},{20,8},{24,4},{28,0},{1,29},{... | collective-permute-start | bytes 1572872 | tf_op jit(solution)/shard_map/x_keep/ppermute | solution.py:240
  32.3 1.0 %pair.2 = (bf16[2,256,512]{2,1,0:T(8,128)(2,1)S(1)}, bf16[2,256,512]{2,1,0:T(8,128)(2,1)S(1)}) custom-call(s32[1]{0:T(128)} %bitcast.mine, bf16[1,2,256,2048]{3,2,1,0:T(8,128)(2,1)S(1)} %copy-done, bf16[3,256,512]{2,1,0:T(8,128)(2,1)S(1)} %collective-permute-done.x1_ref.d1_ref, bf16[256,512]{1,0:T(8,128)(2,1)S(1)} %copy-done.1, ...), custom_call_target="tpu_custom_call" | custom-call | flops 1000 | bytes 1000000000 | tf_op jit(solution)/shard_map/pair/pallas_call | solution.py:183
  33.8 1.6 %collective-permute-start.7 = (bf16[2,256,512]{2,1,0:T(8,128)(2,1)S(1)}, bf16[2,256,512]{2,1,0:T(8,128)(2,1)S(1)}, u32[]{:S(2)}, u32[]{:S(2)}) collective-permute-start(bf16[2,256,512]{2,1,0:T(8,128)(2,1)S(1)} %get-tuple-element.34), channel_id=1, source_target_pairs={{0,1},{1,0},{2,3},{3,2},{4,5},{5,4},{6,7},{7,6},{8,9},{9,8},{10,11... | collective-permute-start | bytes 1572872 | tf_op jit(solution)/shard_map/gate_first/ppermute | solution.py:245
  35.4 3.1 %collective-permute-done.4 = bf16[2,256,512]{2,1,0:T(8,128)(2,1)S(1)} collective-permute-done((bf16[2,256,512]{2,1,0:T(8,128)(2,1)}, bf16[2,256,512]{2,1,0:T(8,128)(2,1)S(1)}, u32[]{:S(2)}, u32[]{:S(2)}) %collective-permute-start.4) | collective-permute-done | bytes 524320 | tf_op jit(solution)/shard_map/down0_first/ppermute | solution.py:245
  38.5 1.3 %collective-permute-start.2 = (bf16[256,2048]{1,0:T(8,128)(2,1)S(1)}, bf16[256,2048]{1,0:T(8,128)(2,1)S(1)}, u32[]{:S(2)}, u32[]{:S(2)}) collective-permute-start(bf16[256,2048]{1,0:T(8,128)(2,1)S(1)} %copy-done.9), channel_id=1, source_target_pairs={{4,0},{8,4},{12,8},{16,12},{20,16},{24,20},{28,24},{5,1},{9,5},{13... | collective-permute-start | bytes 3145736 | tf_op jit(solution)/shard_map/dx_first/ppermute | solution.py:234
  39.8 3.1 %collective-permute-start.3 = (bf16[256,2048]{1,0:T(8,128)(2,1)S(1)}, bf16[256,2048]{1,0:T(8,128)(2,1)S(1)}, u32[]{:S(2)}, u32[]{:S(2)}) collective-permute-start(bf16[256,2048]{1,0:T(8,128)(2,1)S(1)} %copy-done.8), channel_id=1, source_target_pairs={{0,4},{4,8},{8,12},{12,16},{16,20},{20,24},{24,28},{1,5},{5,9},{9,... | collective-permute-start | bytes 3145736 | tf_op jit(solution)/shard_map/dx_second/ppermute | solution.py:234
  43.2 1.2 %collective-permute-done.9.x1_ref = bf16[2,256,512]{2,1,0:T(8,128)(2,1)S(1)} collective-permute-done((bf16[2,256,512]{2,1,0:T(8,128)(2,1)S(1)}, bf16[2,256,512]{2,1,0:T(8,128)(2,1)S(1)}, u32[]{:S(2)}, u32[]{:S(2)}) %collective-permute-start.9) | collective-permute-done | bytes 524320 | tf_op jit(solution)/shard_map/x_keep/ppermute | solution.py:240
  44.4 2.6 %collective-permute-start.5 = (bf16[1,256,512]{2,1,0:T(8,128)(2,1)S(1)}, bf16[1,256,512]{2,1,0:T(8,128)(2,1)S(1)}, u32[]{:S(2)}, u32[]{:S(2)}) collective-permute-start(bf16[1,256,512]{2,1,0:T(8,128)(2,1)S(1)} %get-tuple-element.52), channel_id=1, source_target_pairs={{0,2},{1,3},{2,0},{3,1},{4,6},{5,7},{6,4},{7,5},{8,10},{9,11},{10,... | collective-permute-start | bytes 786440 | tf_op jit(solution)/shard_map/down0_rest/ppermute | solution.py:245
  47.0 1.0 %pair.3 = (bf16[2,256,512]{2,1,0:T(8,128)(2,1)S(1)}, bf16[2,256,512]{2,1,0:T(8,128)(2,1)S(1)}) custom-call(s32[1]{0:T(128)} %bitcast.mine, bf16[1,2,256,2048]{3,2,1,0:T(8,128)(2,1)S(1)} %copy-done, bf16[2,256,512]{2,1,0:T(8,128)(2,1)S(1)} %collective-permute-done.9.x1_ref, bf16[256,512]{1,0:T(8,128)(2,1)S(1)} %copy-done.2, ...), custom_call_target="tpu_custom_call" | custom-call | flops 1000 | bytes 1000000000 | tf_op jit(solution)/shard_map/pair/pallas_call | solution.py:183
  48.0 7.3 %collective-permute-done.11 = bf16[2,256,512]{2,1,0:T(8,128)(2,1)S(1)} collective-permute-done((bf16[2,256,512]{2,1,0:T(8,128)(2,1)S(1)}, bf16[2,256,512]{2,1,0:T(8,128)(2,1)S(1)}, u32[]{:S(2)}, u32[]{:S(2)}) %collective-permute-start.11) | collective-permute-done | bytes 524320 | tf_op jit(solution)/shard_map/up_first/ppermute | solution.py:245
  55.5 1.6 %collective-permute-start.12 = (bf16[1,256,512]{2,1,0:T(8,128)(2,1)S(1)}, bf16[1,256,512]{2,1,0:T(8,128)(2,1)S(1)}, u32[]{:S(2)}, u32[]{:S(2)}) collective-permute-start(bf16[1,256,512]{2,1,0:T(8,128)(2,1)S(1)} %get-tuple-element.48), channel_id=1, source_target_pairs={{0,2},{1,3},{2,0},{3,1},{4,6},{5,7},{6,4},{7,5},{8,10},{9,11},{10,... | collective-permute-start | bytes 786440 | tf_op jit(solution)/shard_map/up_rest/ppermute | solution.py:245
  57.0 13.4 %collective-permute-done.7 = bf16[2,256,512]{2,1,0:T(8,128)(2,1)S(1)} collective-permute-done((bf16[2,256,512]{2,1,0:T(8,128)(2,1)S(1)}, bf16[2,256,512]{2,1,0:T(8,128)(2,1)S(1)}, u32[]{:S(2)}, u32[]{:S(2)}) %collective-permute-start.7) | collective-permute-done | bytes 524320 | tf_op jit(solution)/shard_map/gate_first/ppermute | solution.py:245
  70.5 1.2 %collective-permute-start.8 = (bf16[1,256,512]{2,1,0:T(8,128)(2,1)S(1)}, bf16[1,256,512]{2,1,0:T(8,128)(2,1)S(1)}, u32[]{:S(2)}, u32[]{:S(2)}) collective-permute-start(bf16[1,256,512]{2,1,0:T(8,128)(2,1)S(1)} %add_convert_fusion.4), channel_id=1, source_target_pairs={{0,28},{4,24},{8,20},{12,16},{16,12},{20,8},{24,4},{28,0},{1,29},{... | collective-permute-start | bytes 786440 | tf_op jit(solution)/shard_map/down_mirror/ppermute | solution.py:240
  71.9 10.2 %collective-permute-done.12.refs_2_ = bf16[1,256,512]{2,1,0:T(8,128)(2,1)S(1)} collective-permute-done((bf16[1,256,512]{2,1,0:T(8,128)(2,1)S(1)}, bf16[1,256,512]{2,1,0:T(8,128)(2,1)S(1)}, u32[]{:S(2)}, u32[]{:S(2)}) %collective-permute-start.12) | collective-permute-done | bytes 262176 | tf_op jit(solution)/shard_map/up_rest/ppermute | solution.py:245
  84.2 1.9 %join.1 = bf16[1,2,256,2048]{3,2,1,0:T(8,128)(2,1)} custom-call(bf16[256,2048]{1,0:T(8,128)(2,1)S(1)} %collective-permute-done.2.first_ref, bf16[256,2048]{1,0:T(8,128)(2,1)S(1)} %collective-permute-done.3.second_ref), custom_call_target="tpu_custom_call" | custom-call | flops 1000 | bytes 1000000000 | tf_op jit(solution)/shard_map/join/pallas_call | solution.py:269
  86.0 1.2 %collective-permute-done.10.refs_2_ = bf16[1,256,512]{2,1,0:T(8,128)(2,1)S(1)} collective-permute-done((bf16[1,256,512]{2,1,0:T(8,128)(2,1)S(1)}, bf16[1,256,512]{2,1,0:T(8,128)(2,1)S(1)}, u32[]{:S(2)}, u32[]{:S(2)}) %collective-permute-start.10) | collective-permute-done | bytes 262176 | tf_op jit(solution)/shard_map/gate_rest/ppermute | solution.py:245
  (37 shorter events, 5.6 us)
Async XLA Ops:
  5.6 15.2 %collective-permute-start.1 = (bf16[2,256,512]{2,1,0:T(8,128)(2,1)}, bf16[2,256,512]{2,1,0:T(8,128)(2,1)S(1)}, u32[]{:S(2)}, u32[]{:S(2)}) collective-permute-start(bf16[2,256,512]{2,1,0:T(8,128)(2,1)} %get-tuple-element.32), channel_id=1, source_target_pairs={{0,1},{1,0},{2,3},{3,2},{4,5},{5,4},{6,7},{7,6},{8,9},{9,8},{10,11... | collective-permute-start | bytes 1572872 | tf_op jit(solution)/shard_map/down1_first/ppermute | solution.py:245
  8.7 20.8 %collective-permute-start = (bf16[3,256,512]{2,1,0:T(8,128)(2,1)}, bf16[3,256,512]{2,1,0:T(8,128)(2,1)S(1)}, u32[]{:S(2)}, u32[]{:S(2)}) collective-permute-start(bf16[3,256,512]{2,1,0:T(8,128)(2,1)} %get-tuple-element.29), channel_id=1, source_target_pairs={{0,28},{4,24},{8,20},{12,16},{16,12},{20,8},{24,4},{28,0},{1,29},{... | collective-permute-start | bytes 2359304 | tf_op jit(solution)/shard_map/message/ppermute | solution.py:240
  10.3 19.2 %copy-start.10 = (bf16[2,256,512]{2,1,0:T(8,128)(2,1)S(1)}, bf16[2,256,512]{2,1,0:T(8,128)(2,1)}, u32[]{:S(2)}) copy-start(bf16[2,256,512]{2,1,0:T(8,128)(2,1)} %get-tuple-element.43) | copy-start | bytes 1572868
  10.3 21.0 %copy-start = (bf16[1,2,256,2048]{3,2,1,0:T(8,128)(2,1)S(1)}, bf16[1,2,256,2048]{3,2,1,0:T(8,128)(2,1)}, u32[]{:S(2)}) copy-start(bf16[1,2,256,2048]{3,2,1,0:T(8,128)(2,1)} %x0_ref.3) | copy-start | bytes 6291460
  17.8 20.7 %collective-permute-start.4 = (bf16[2,256,512]{2,1,0:T(8,128)(2,1)}, bf16[2,256,512]{2,1,0:T(8,128)(2,1)S(1)}, u32[]{:S(2)}, u32[]{:S(2)}) collective-permute-start(bf16[2,256,512]{2,1,0:T(8,128)(2,1)} %get-tuple-element.39), channel_id=1, source_target_pairs={{0,1},{1,0},{2,3},{3,2},{4,5},{5,4},{6,7},{7,6},{8,9},{9,8},{10,11... | collective-permute-start | bytes 1572872 | tf_op jit(solution)/shard_map/down0_first/ppermute | solution.py:245
  20.8 22.1 %copy-start.6 = (bf16[2,256,512]{2,1,0:T(8,128)(2,1)S(1)}, bf16[2,256,512]{2,1,0:T(8,128)(2,1)}, u32[]{:S(2)}) copy-start(bf16[2,256,512]{2,1,0:T(8,128)(2,1)} %get-tuple-element.38) | copy-start | bytes 1572868
  21.9 17.9 %collective-permute-start.6 = (bf16[1,256,512]{2,1,0:T(8,128)(2,1)S(1)}, bf16[1,256,512]{2,1,0:T(8,128)(2,1)S(1)}, u32[]{:S(2)}, u32[]{:S(2)}) collective-permute-start(bf16[1,256,512]{2,1,0:T(8,128)(2,1)S(1)} %add_convert_fusion.8), channel_id=1, source_target_pairs={{0,2},{1,3},{2,0},{3,1},{4,6},{5,7},{6,4},{7,5},{8,10},{9,11},{10,... | collective-permute-start | bytes 786440 | tf_op jit(solution)/shard_map/down1_rest/ppermute | solution.py:245
  29.6 14.8 %collective-permute-start.9 = (bf16[2,256,512]{2,1,0:T(8,128)(2,1)S(1)}, bf16[2,256,512]{2,1,0:T(8,128)(2,1)S(1)}, u32[]{:S(2)}, u32[]{:S(2)}) collective-permute-start(bf16[2,256,512]{2,1,0:T(8,128)(2,1)S(1)} %copy-done.10), channel_id=1, source_target_pairs={{0,28},{4,24},{8,20},{12,16},{16,12},{20,8},{24,4},{28,0},{1,29},{... | collective-permute-start | bytes 1572872 | tf_op jit(solution)/shard_map/x_keep/ppermute | solution.py:240
  31.3 1.0 %copy-start.1 = (bf16[256,512]{1,0:T(8,128)(2,1)S(1)}, bf16[256,512]{1,0:T(8,128)(2,1)}, u32[]{:S(2)}) copy-start(bf16[256,512]{1,0:T(8,128)(2,1)} %get-tuple-element.33.d0_ref) | copy-start | bytes 786436
  32.3 6.2 %copy-start.9 = (bf16[256,2048]{1,0:T(8,128)(2,1)S(1)}, bf16[256,2048]{1,0:T(8,128)(2,1)}, u32[]{:S(2)}) copy-start(bf16[256,2048]{1,0:T(8,128)(2,1)} %get-tuple-element.35) | copy-start | bytes 3145732
  32.3 7.5 %copy-start.8 = (bf16[256,2048]{1,0:T(8,128)(2,1)S(1)}, bf16[256,2048]{1,0:T(8,128)(2,1)}, u32[]{:S(2)}) copy-start(bf16[256,2048]{1,0:T(8,128)(2,1)} %get-tuple-element.37) | copy-start | bytes 3145732
  32.3 10.8 %copy-start.7 = (bf16[2,256,512]{2,1,0:T(8,128)(2,1)S(1)}, bf16[2,256,512]{2,1,0:T(8,128)(2,1)}, u32[]{:S(2)}) copy-start(bf16[2,256,512]{2,1,0:T(8,128)(2,1)} %get-tuple-element.31) | copy-start | bytes 1572868
  33.3 13.7 %copy-start.2 = (bf16[256,512]{1,0:T(8,128)(2,1)S(1)}, bf16[256,512]{1,0:T(8,128)(2,1)}, u32[]{:S(2)}) copy-start(bf16[256,512]{1,0:T(8,128)(2,1)} %get-tuple-element.33.d0_ref) | copy-start | bytes 786436
  33.3 22.0 %collective-permute-start.11 = (bf16[2,256,512]{2,1,0:T(8,128)(2,1)S(1)}, bf16[2,256,512]{2,1,0:T(8,128)(2,1)S(1)}, u32[]{:S(2)}, u32[]{:S(2)}) collective-permute-start(bf16[2,256,512]{2,1,0:T(8,128)(2,1)S(1)} %get-tuple-element.47), channel_id=1, source_target_pairs={{0,1},{1,0},{2,3},{3,2},{4,5},{5,4},{6,7},{7,6},{8,9},{9,8},{10,11... | collective-permute-start | bytes 1572872 | tf_op jit(solution)/shard_map/up_first/ppermute | solution.py:245
  33.8 36.7 %collective-permute-start.7 = (bf16[2,256,512]{2,1,0:T(8,128)(2,1)S(1)}, bf16[2,256,512]{2,1,0:T(8,128)(2,1)S(1)}, u32[]{:S(2)}, u32[]{:S(2)}) collective-permute-start(bf16[2,256,512]{2,1,0:T(8,128)(2,1)S(1)} %get-tuple-element.34), channel_id=1, source_target_pairs={{0,1},{1,0},{2,3},{3,2},{4,5},{5,4},{6,7},{7,6},{8,9},{9,8},{10,11... | collective-permute-start | bytes 1572872 | tf_op jit(solution)/shard_map/gate_first/ppermute | solution.py:245
  38.5 45.7 %collective-permute-start.2 = (bf16[256,2048]{1,0:T(8,128)(2,1)S(1)}, bf16[256,2048]{1,0:T(8,128)(2,1)S(1)}, u32[]{:S(2)}, u32[]{:S(2)}) collective-permute-start(bf16[256,2048]{1,0:T(8,128)(2,1)S(1)} %copy-done.9), channel_id=1, source_target_pairs={{4,0},{8,4},{12,8},{16,12},{20,16},{24,20},{28,24},{5,1},{9,5},{13... | collective-permute-start | bytes 3145736 | tf_op jit(solution)/shard_map/dx_first/ppermute | solution.py:234
  39.8 44.4 %collective-permute-start.3 = (bf16[256,2048]{1,0:T(8,128)(2,1)S(1)}, bf16[256,2048]{1,0:T(8,128)(2,1)S(1)}, u32[]{:S(2)}, u32[]{:S(2)}) collective-permute-start(bf16[256,2048]{1,0:T(8,128)(2,1)S(1)} %copy-done.8), channel_id=1, source_target_pairs={{0,4},{4,8},{8,12},{12,16},{16,20},{20,24},{24,28},{1,5},{5,9},{9,... | collective-permute-start | bytes 3145736 | tf_op jit(solution)/shard_map/dx_second/ppermute | solution.py:234
  44.4 27.5 %collective-permute-start.5 = (bf16[1,256,512]{2,1,0:T(8,128)(2,1)S(1)}, bf16[1,256,512]{2,1,0:T(8,128)(2,1)S(1)}, u32[]{:S(2)}, u32[]{:S(2)}) collective-permute-start(bf16[1,256,512]{2,1,0:T(8,128)(2,1)S(1)} %get-tuple-element.52), channel_id=1, source_target_pairs={{0,2},{1,3},{2,0},{3,1},{4,6},{5,7},{6,4},{7,5},{8,10},{9,11},{10,... | collective-permute-start | bytes 786440 | tf_op jit(solution)/shard_map/down0_rest/ppermute | solution.py:245
  48.0 34.1 %copy-start.3 = (f32[1,512,256]{2,1,0:T(8,128)S(1)}, f32[1,512,256]{2,1,0:T(8,128)}, u32[]{:S(2)}) copy-start(f32[1,512,256]{2,1,0:T(8,128)} %refs_0_.4) | copy-start | bytes 1572868
  55.3 27.8 %copy-start.4 = (f32[1,512,256]{2,1,0:T(8,128)S(1)}, f32[1,512,256]{2,1,0:T(8,128)}, u32[]{:S(2)}) copy-start(f32[1,512,256]{2,1,0:T(8,128)} %refs_0_.2) | copy-start | bytes 1572868
  55.5 26.7 %collective-permute-start.12 = (bf16[1,256,512]{2,1,0:T(8,128)(2,1)S(1)}, bf16[1,256,512]{2,1,0:T(8,128)(2,1)S(1)}, u32[]{:S(2)}, u32[]{:S(2)}) collective-permute-start(bf16[1,256,512]{2,1,0:T(8,128)(2,1)S(1)} %get-tuple-element.48), channel_id=1, source_target_pairs={{0,2},{1,3},{2,0},{3,1},{4,6},{5,7},{6,4},{7,5},{8,10},{9,11},{10,... | collective-permute-start | bytes 786440 | tf_op jit(solution)/shard_map/up_rest/ppermute | solution.py:245
  70.5 12.7 %collective-permute-start.8 = (bf16[1,256,512]{2,1,0:T(8,128)(2,1)S(1)}, bf16[1,256,512]{2,1,0:T(8,128)(2,1)S(1)}, u32[]{:S(2)}, u32[]{:S(2)}) collective-permute-start(bf16[1,256,512]{2,1,0:T(8,128)(2,1)S(1)} %add_convert_fusion.4), channel_id=1, source_target_pairs={{0,28},{4,24},{8,20},{12,16},{16,12},{20,8},{24,4},{28,0},{1,29},{... | collective-permute-start | bytes 786440 | tf_op jit(solution)/shard_map/down_mirror/ppermute | solution.py:240
  71.8 15.4 %collective-permute-start.10 = (bf16[1,256,512]{2,1,0:T(8,128)(2,1)S(1)}, bf16[1,256,512]{2,1,0:T(8,128)(2,1)S(1)}, u32[]{:S(2)}, u32[]{:S(2)}) collective-permute-start(bf16[1,256,512]{2,1,0:T(8,128)(2,1)S(1)} %get-tuple-element.45), channel_id=1, source_target_pairs={{0,2},{1,3},{2,0},{3,1},{4,6},{5,7},{6,4},{7,5},{8,10},{9,11},{10,... | collective-permute-start | bytes 786440 | tf_op jit(solution)/shard_map/gate_rest/ppermute | solution.py:245
  84.2 3.1 %copy-start.5 = (f32[1,512,256]{2,1,0:T(8,128)S(1)}, f32[1,512,256]{2,1,0:T(8,128)}, u32[]{:S(2)}) copy-start(f32[1,512,256]{2,1,0:T(8,128)} %refs_0_.3) | copy-start | bytes 1572868

commit v6 on v4

--- a/solution.py
+++ b/solution.py
@@ -214,12 +214,13 @@
     shape = moms[0].shape
     _, shard, ff = shape
     count = len(moms)
-    whole = pl.BlockSpec((1, shard, ff), lambda i: (0, 0, 0))
+    step = shard // 2 if shard % 256 == 0 else shard
+    whole = pl.BlockSpec((1, step, ff), lambda i: (0, i, 0))
     return pl.pallas_call(
         functools.partial(momentum_kernel, scale, count),
         out_shape=(jax.ShapeDtypeStruct(shape, F32),) * count,
-        grid=(1,),
-        in_specs=[whole] * count + [pl.BlockSpec((1, ff * count, shard), lambda i: (0, 0, 0))] * len(parts),
+        grid=(shard // step,),
+        in_specs=[whole] * count + [pl.BlockSpec((1, ff * count, step), lambda i: (0, 0, i))] * len(parts),
         out_specs=[whole] * count,
         compiler_params=pltpu.CompilerParams(vmem_limit_bytes=2 * VMEM_LIMIT),
         cost_estimate=COST,

time: 88.5 us -> 88.5 us (level)
  no operation moved by 1% of the time
where the time goes in v6:
time: 88.5 us; the launch traced here: 88.3 us
  waiting for transfers between devices  45.7 us (52%)
  starting transfers between devices  19.8 us (22%)
  Pallas kernels  19.5 us (22%)
  other arithmetic  1.58 us (2%)
  local copies, waits for them, and re-layouts  0.99 us (1%)
    ppermute x8, waiting for transfers between devices, swapped(): lax.ppermute(value, 'dp', [(i, i ^ mask) for i in range(lax.axis_size('dp...  41.6 us
    ppermute x8, starting transfers between devices, swapped(): lax.ppermute(value, 'dp', [(i, i ^ mask) for i in range(lax.axis_size('dp...  11.8 us
    pallas_call x1, Pallas kernels, rest(): pl.pallas_call(functools.partial(rest_kernel, cut, far_cut), out_shape=tu...  7.47 us
    pallas_call x1, Pallas kernels, second(): pl.pallas_call(functools.partial(second_kernel, cut, far_cut), out_shape=...  4.98 us
    ppermute x2, starting transfers between devices, shifted(): lax.ppermute(value, 'section', [(i, i + steps) for i in range(first, last)])  4.38 us
    ppermute x3, waiting for transfers between devices, mirrored(): lax.ppermute(value, 'section', [(i, count - 1 - i) for i in range(count)])  4.08 us
    ppermute x3, starting transfers between devices, mirrored(): lax.ppermute(value, 'section', [(i, count - 1 - i) for i in range(count)])  3.58 us
    pallas_call x3, Pallas kernels, momentum(): pl.pallas_call(functools.partial(momentum_kernel, scale, count), out_shap...  3.17 us
  transfers between devices with their start and end apart: 13, of which 7 were waited for; matrix products, arithmetic and copies ran while one was open for 2% of the time, Pallas kernels for 15%

profile of v6, /device:TPU:0, one launch (start us, length us, event | category | flops | bytes accessed | tf_op | source)
XLA Modules:
  0.0 88.3 jit_solution(14375560215859023084)
XLA Ops:
  0.6 5.0 %second.1 = (bf16[256,512]{1,0:T(8,128)(2,1)}, bf16[256,256]{1,0:T(8,128)(2,1)}, bf16[2,256,512]{2,1,0:T(8,128)(2,1)}, bf16[3,256,512]{2,1,0:T(8,128)(2,1)}, bf16[2,256,512]{2,1,0:T(8,128)(2,1)}) custom-call(s32[1]{0:T(128)} %bitcast.mine, bf16[1,2,256,2048]{3,2,1,0:T(8,128)(2,1)} %x0_ref.3, bf16[1,2,256,2048]{3,2,1,0:T(8,128)(2,1)} %y_hbm.3, ...), custom_call_target="tpu_custom_call" | custom-call | flops 1000 | bytes 1000000000 | tf_op jit(solution)/shard_map/second/pallas_call | solution.py:96
  5.6 3.1 %collective-permute-start.1 = (bf16[2,256,512]{2,1,0:T(8,128)(2,1)}, bf16[2,256,512]{2,1,0:T(8,128)(2,1)S(1)}, u32[]{:S(2)}, u32[]{:S(2)}) collective-permute-start(bf16[2,256,512]{2,1,0:T(8,128)(2,1)} %get-tuple-element.31), channel_id=1, source_target_pairs={{0,1},{1,0},{2,3},{3,2},{4,5},{5,4},{6,7},{7,6},{8,9},{9,8},{10,11... | collective-permute-start | bytes 1572872 | tf_op jit(solution)/shard_map/down1_first/ppermute | solution.py:246
  8.7 1.6 %collective-permute-start = (bf16[3,256,512]{2,1,0:T(8,128)(2,1)}, bf16[3,256,512]{2,1,0:T(8,128)(2,1)S(1)}, u32[]{:S(2)}, u32[]{:S(2)}) collective-permute-start(bf16[3,256,512]{2,1,0:T(8,128)(2,1)} %get-tuple-element.28), channel_id=1, source_target_pairs={{0,28},{4,24},{8,20},{12,16},{16,12},{20,8},{24,4},{28,0},{1,29},{... | collective-permute-start | bytes 2359304 | tf_op jit(solution)/shard_map/message/ppermute | solution.py:241
  10.3 7.5 %rest.1 = (bf16[256,512]{1,0:T(8,128)(2,1)}, bf16[2,256,512]{2,1,0:T(8,128)(2,1)}, bf16[2,256,512]{2,1,0:T(8,128)(2,1)}, bf16[2,256,512]{2,1,0:T(8,128)(2,1)}, b...) custom-call(s32[1]{0:T(128)} %bitcast.mine, bf16[1,2,256,2048]{3,2,1,0:T(8,128)(2,1)} %x0_ref.3, ...), custom_call_target="tpu_custom_call" | custom-call | flops 1000 | bytes 1000000000 | tf_op jit(solution)/shard_map/rest/pallas_call | solution.py:151
  18.3 2.5 %collective-permute-done.1 = bf16[2,256,512]{2,1,0:T(8,128)(2,1)S(1)} collective-permute-done((bf16[2,256,512]{2,1,0:T(8,128)(2,1)}, bf16[2,256,512]{2,1,0:T(8,128)(2,1)S(1)}, u32[]{:S(2)}, u32[]{:S(2)}) %collective-permute-start.1) | collective-permute-done | bytes 524320 | tf_op jit(solution)/shard_map/down1_first/ppermute | solution.py:246
  20.8 1.1 %add_convert_fusion.8 = bf16[1,256,512]{2,1,0:T(8,128)(2,1)S(1)} fusion(bf16[2,256,512]{2,1,0:T(8,128)(2,1)S(1)} %collective-permute-done.1, bf16[2,256,512]{2,1,0:T(8,128)(2,1)} %get-tuple-element.30), kind=kLoop, calls=%fused_computation.8 | loop fusion | flops 524288 | bytes 786432 | tf_op jit(solution)/shard_map/convert_element_type | solution.py:254
  21.9 2.8 %collective-permute-start.6 = (bf16[1,256,512]{2,1,0:T(8,128)(2,1)S(1)}, bf16[1,256,512]{2,1,0:T(8,128)(2,1)S(1)}, u32[]{:S(2)}, u32[]{:S(2)}) collective-permute-start(bf16[1,256,512]{2,1,0:T(8,128)(2,1)S(1)} %add_convert_fusion.8), channel_id=1, source_target_pairs={{0,2},{1,3},{2,0},{3,1},{4,6},{5,7},{6,4},{7,5},{8,10},{9,11},{10,... | collective-permute-start | bytes 786440 | tf_op jit(solution)/shard_map/down1_rest/ppermute | solution.py:246
  25.5 4.1 %collective-permute-done.x1_ref.d1_ref = bf16[3,256,512]{2,1,0:T(8,128)(2,1)S(1)} collective-permute-done((bf16[3,256,512]{2,1,0:T(8,128)(2,1)}, bf16[3,256,512]{2,1,0:T(8,128)(2,1)S(1)}, u32[]{:S(2)}, u32[]{:S(2)}) %collective-permute-start) | collective-permute-done | bytes 786464 | tf_op jit(solution)/shard_map/message/ppermute | solution.py:241
  30.5 1.0 %pair.2 = (bf16[2,256,512]{2,1,0:T(8,128)(2,1)S(1)}, bf16[2,256,512]{2,1,0:T(8,128)(2,1)S(1)}) custom-call(s32[1]{0:T(128)} %bitcast.mine, bf16[1,2,256,2048]{3,2,1,0:T(8,128)(2,1)S(1)} %copy-done, bf16[3,256,512]{2,1,0:T(8,128)(2,1)S(1)} %collective-permute-done.x1_ref.d1_ref, bf16[256,512]{1,0:T(8,128)(2,1)S(1)} %copy-done.1, ...), custom_call_target="tpu_custom_call" | custom-call | flops 1000 | bytes 1000000000 | tf_op jit(solution)/shard_map/pair/pallas_call | solution.py:183
  31.6 2.0 %collective-permute-start.7 = (bf16[2,256,512]{2,1,0:T(8,128)(2,1)S(1)}, bf16[2,256,512]{2,1,0:T(8,128)(2,1)S(1)}, u32[]{:S(2)}, u32[]{:S(2)}) collective-permute-start(bf16[2,256,512]{2,1,0:T(8,128)(2,1)S(1)} %get-tuple-element.33), channel_id=1, source_target_pairs={{0,1},{1,0},{2,3},{3,2},{4,5},{5,4},{6,7},{7,6},{8,9},{9,8},{10,11... | collective-permute-start | bytes 1572872 | tf_op jit(solution)/shard_map/gate_first/ppermute | solution.py:246
  33.6 4.8 %collective-permute-done.4 = bf16[2,256,512]{2,1,0:T(8,128)(2,1)S(1)} collective-permute-done((bf16[2,256,512]{2,1,0:T(8,128)(2,1)}, bf16[2,256,512]{2,1,0:T(8,128)(2,1)S(1)}, u32[]{:S(2)}, u32[]{:S(2)}) %collective-permute-start.4) | collective-permute-done | bytes 524320 | tf_op jit(solution)/shard_map/down0_first/ppermute | solution.py:246
  38.5 1.3 %collective-permute-start.2 = (bf16[256,2048]{1,0:T(8,128)(2,1)S(1)}, bf16[256,2048]{1,0:T(8,128)(2,1)S(1)}, u32[]{:S(2)}, u32[]{:S(2)}) collective-permute-start(bf16[256,2048]{1,0:T(8,128)(2,1)S(1)} %copy-done.9), channel_id=1, source_target_pairs={{4,0},{8,4},{12,8},{16,12},{20,16},{24,20},{28,24},{5,1},{9,5},{13... | collective-permute-start | bytes 3145736 | tf_op jit(solution)/shard_map/dx_first/ppermute | solution.py:235
  39.8 3.1 %collective-permute-start.3 = (bf16[256,2048]{1,0:T(8,128)(2,1)S(1)}, bf16[256,2048]{1,0:T(8,128)(2,1)S(1)}, u32[]{:S(2)}, u32[]{:S(2)}) collective-permute-start(bf16[256,2048]{1,0:T(8,128)(2,1)S(1)} %copy-done.8), channel_id=1, source_target_pairs={{0,4},{4,8},{8,12},{12,16},{16,20},{20,24},{24,28},{1,5},{5,9},{9,... | collective-permute-start | bytes 3145736 | tf_op jit(solution)/shard_map/dx_second/ppermute | solution.py:235
  43.2 1.7 %collective-permute-start.5 = (bf16[1,256,512]{2,1,0:T(8,128)(2,1)S(1)}, bf16[1,256,512]{2,1,0:T(8,128)(2,1)S(1)}, u32[]{:S(2)}, u32[]{:S(2)}) collective-permute-start(bf16[1,256,512]{2,1,0:T(8,128)(2,1)S(1)} %get-tuple-element.50), channel_id=1, source_target_pairs={{0,2},{1,3},{2,0},{3,1},{4,6},{5,7},{6,4},{7,5},{8,10},{9,11},{10,... | collective-permute-start | bytes 786440 | tf_op jit(solution)/shard_map/down0_rest/ppermute | solution.py:246
  45.9 9.5 %collective-permute-done.11 = bf16[2,256,512]{2,1,0:T(8,128)(2,1)S(1)} collective-permute-done((bf16[2,256,512]{2,1,0:T(8,128)(2,1)S(1)}, bf16[2,256,512]{2,1,0:T(8,128)(2,1)S(1)}, u32[]{:S(2)}, u32[]{:S(2)}) %collective-permute-start.11) | collective-permute-done | bytes 524320 | tf_op jit(solution)/shard_map/up_first/ppermute | solution.py:246
  55.5 1.6 %collective-permute-start.12 = (bf16[1,256,512]{2,1,0:T(8,128)(2,1)S(1)}, bf16[1,256,512]{2,1,0:T(8,128)(2,1)S(1)}, u32[]{:S(2)}, u32[]{:S(2)}) collective-permute-start(bf16[1,256,512]{2,1,0:T(8,128)(2,1)S(1)} %get-tuple-element.46), channel_id=1, source_target_pairs={{0,2},{1,3},{2,0},{3,1},{4,6},{5,7},{6,4},{7,5},{8,10},{9,11},{10,... | collective-permute-start | bytes 786440 | tf_op jit(solution)/shard_map/up_rest/ppermute | solution.py:246
  57.0 13.4 %collective-permute-done.7 = bf16[2,256,512]{2,1,0:T(8,128)(2,1)S(1)} collective-permute-done((bf16[2,256,512]{2,1,0:T(8,128)(2,1)S(1)}, bf16[2,256,512]{2,1,0:T(8,128)(2,1)S(1)}, u32[]{:S(2)}, u32[]{:S(2)}) %collective-permute-start.7) | collective-permute-done | bytes 524320 | tf_op jit(solution)/shard_map/gate_first/ppermute | solution.py:246
  70.5 1.2 %collective-permute-start.8 = (bf16[1,256,512]{2,1,0:T(8,128)(2,1)S(1)}, bf16[1,256,512]{2,1,0:T(8,128)(2,1)S(1)}, u32[]{:S(2)}, u32[]{:S(2)}) collective-permute-start(bf16[1,256,512]{2,1,0:T(8,128)(2,1)S(1)} %add_convert_fusion.4), channel_id=1, source_target_pairs={{0,28},{4,24},{8,20},{12,16},{16,12},{20,8},{24,4},{28,0},{1,29},{... | collective-permute-start | bytes 786440 | tf_op jit(solution)/shard_map/down_mirror/ppermute | solution.py:241
  71.9 10.2 %collective-permute-done.12.refs_2_ = bf16[1,256,512]{2,1,0:T(8,128)(2,1)S(1)} collective-permute-done((bf16[1,256,512]{2,1,0:T(8,128)(2,1)S(1)}, bf16[1,256,512]{2,1,0:T(8,128)(2,1)S(1)}, u32[]{:S(2)}, u32[]{:S(2)}) %collective-permute-start.12) | collective-permute-done | bytes 262176 | tf_op jit(solution)/shard_map/up_rest/ppermute | solution.py:246
  82.2 1.0 %momentum.5 = f32[1,512,256]{2,1,0:T(8,128)} custom-call(f32[1,512,256]{2,1,0:T(8,128)S(1)} %copy-done.3, bf16[1,256,512]{2,1,0:T(8,128)(2,1)S(1)} %get-tuple-element.47.refs_1_, bf16[1,256,512]{2,1,0:T(8,128)(2,1)S(1)} %collective-permute-done.12.refs_2_), custom_call_target="tpu_custom_call" | custom-call | flops 1000 | bytes 1000 | tf_op jit(solution)/shard_map/momentum/pallas_call | solution.py:219
  83.2 1.1 %momentum.3 = f32[1,512,256]{2,1,0:T(8,128)} custom-call(f32[1,512,256]{2,1,0:T(8,128)S(1)} %copy-done.4, bf16[1,256,512]{2,1,0:T(8,128)(2,1)S(1)} %get-tuple-element.51.refs_1_, bf16[1,256,512]{2,1,0:T(8,128)(2,1)S(1)} %collective-permute-done.5.refs_2_, bf16[1,256,512]{2,1,0:T(8,128)(2,1)S(1)} %collective-permute-done.8.refs_3_), custom_call_target="tpu_custom_call" | custom-call | flops 1000 | bytes 1000 | tf_op jit(solution)/shard_map/momentum/pallas_call | solution.py:219
  84.3 1.9 %join.1 = bf16[1,2,256,2048]{3,2,1,0:T(8,128)(2,1)} custom-call(bf16[256,2048]{1,0:T(8,128)(2,1)S(1)} %collective-permute-done.2.first_ref, bf16[256,2048]{1,0:T(8,128)(2,1)S(1)} %collective-permute-done.3.second_ref), custom_call_target="tpu_custom_call" | custom-call | flops 1000 | bytes 1000000000 | tf_op jit(solution)/shard_map/join/pallas_call | solution.py:270
  86.1 1.1 %collective-permute-done.10.refs_2_ = bf16[1,256,512]{2,1,0:T(8,128)(2,1)S(1)} collective-permute-done((bf16[1,256,512]{2,1,0:T(8,128)(2,1)S(1)}, bf16[1,256,512]{2,1,0:T(8,128)(2,1)S(1)}, u32[]{:S(2)}, u32[]{:S(2)}) %collective-permute-start.10) | collective-permute-done | bytes 262176 | tf_op jit(solution)/shard_map/gate_rest/ppermute | solution.py:246
  87.3 1.0 %momentum.4 = f32[1,512,256]{2,1,0:T(8,128)} custom-call(f32[1,512,256]{2,1,0:T(8,128)S(1)} %copy-done.5, bf16[1,256,512]{2,1,0:T(8,128)(2,1)S(1)} %get-tuple-element.49.refs_1_, bf16[1,256,512]{2,1,0:T(8,128)(2,1)S(1)} %collective-permute-done.10.refs_2_), custom_call_target="tpu_custom_call" | custom-call | flops 1000 | bytes 1000 | tf_op jit(solution)/shard_map/momentum/pallas_call | solution.py:219
  (37 shorter events, 3.9 us)
Async XLA Ops:
  5.6 15.2 %collective-permute-start.1 = (bf16[2,256,512]{2,1,0:T(8,128)(2,1)}, bf16[2,256,512]{2,1,0:T(8,128)(2,1)S(1)}, u32[]{:S(2)}, u32[]{:S(2)}) collective-permute-start(bf16[2,256,512]{2,1,0:T(8,128)(2,1)} %get-tuple-element.31), channel_id=1, source_target_pairs={{0,1},{1,0},{2,3},{3,2},{4,5},{5,4},{6,7},{7,6},{8,9},{9,8},{10,11... | collective-permute-start | bytes 1572872 | tf_op jit(solution)/shard_map/down1_first/ppermute | solution.py:246
  8.7 20.8 %collective-permute-start = (bf16[3,256,512]{2,1,0:T(8,128)(2,1)}, bf16[3,256,512]{2,1,0:T(8,128)(2,1)S(1)}, u32[]{:S(2)}, u32[]{:S(2)}) collective-permute-start(bf16[3,256,512]{2,1,0:T(8,128)(2,1)} %get-tuple-element.28), channel_id=1, source_target_pairs={{0,28},{4,24},{8,20},{12,16},{16,12},{20,8},{24,4},{28,0},{1,29},{... | collective-permute-start | bytes 2359304 | tf_op jit(solution)/shard_map/message/ppermute | solution.py:241
  10.3 14.4 %copy-start.10 = (bf16[2,256,512]{2,1,0:T(8,128)(2,1)S(1)}, bf16[2,256,512]{2,1,0:T(8,128)(2,1)}, u32[]{:S(2)}) copy-start(bf16[2,256,512]{2,1,0:T(8,128)(2,1)} %get-tuple-element.41) | copy-start | bytes 1572868
  10.3 19.2 %copy-start = (bf16[1,2,256,2048]{3,2,1,0:T(8,128)(2,1)S(1)}, bf16[1,2,256,2048]{3,2,1,0:T(8,128)(2,1)}, u32[]{:S(2)}) copy-start(bf16[1,2,256,2048]{3,2,1,0:T(8,128)(2,1)} %x0_ref.3) | copy-start | bytes 6291460
  17.8 20.7 %collective-permute-start.4 = (bf16[2,256,512]{2,1,0:T(8,128)(2,1)}, bf16[2,256,512]{2,1,0:T(8,128)(2,1)S(1)}, u32[]{:S(2)}, u32[]{:S(2)}) collective-permute-start(bf16[2,256,512]{2,1,0:T(8,128)(2,1)} %get-tuple-element.38), channel_id=1, source_target_pairs={{0,1},{1,0},{2,3},{3,2},{4,5},{5,4},{6,7},{7,6},{8,9},{9,8},{10,11... | collective-permute-start | bytes 1572872 | tf_op jit(solution)/shard_map/down0_first/ppermute | solution.py:246
  20.8 22.1 %copy-start.6 = (bf16[2,256,512]{2,1,0:T(8,128)(2,1)S(1)}, bf16[2,256,512]{2,1,0:T(8,128)(2,1)}, u32[]{:S(2)}) copy-start(bf16[2,256,512]{2,1,0:T(8,128)(2,1)} %get-tuple-element.37) | copy-start | bytes 1572868
  21.9 17.9 %collective-permute-start.6 = (bf16[1,256,512]{2,1,0:T(8,128)(2,1)S(1)}, bf16[1,256,512]{2,1,0:T(8,128)(2,1)S(1)}, u32[]{:S(2)}, u32[]{:S(2)}) collective-permute-start(bf16[1,256,512]{2,1,0:T(8,128)(2,1)S(1)} %add_convert_fusion.8), channel_id=1, source_target_pairs={{0,2},{1,3},{2,0},{3,1},{4,6},{5,7},{6,4},{7,5},{8,10},{9,11},{10,... | collective-permute-start | bytes 786440 | tf_op jit(solution)/shard_map/down1_rest/ppermute | solution.py:246
  24.7 18.4 %collective-permute-start.9 = (bf16[2,256,512]{2,1,0:T(8,128)(2,1)S(1)}, bf16[2,256,512]{2,1,0:T(8,128)(2,1)S(1)}, u32[]{:S(2)}, u32[]{:S(2)}) collective-permute-start(bf16[2,256,512]{2,1,0:T(8,128)(2,1)S(1)} %copy-done.10), channel_id=1, source_target_pairs={{0,28},{4,24},{8,20},{12,16},{16,12},{20,8},{24,4},{28,0},{1,29},{... | collective-permute-start | bytes 1572872 | tf_op jit(solution)/shard_map/x_keep/ppermute | solution.py:241
  29.6 1.0 %copy-start.1 = (bf16[256,512]{1,0:T(8,128)(2,1)S(1)}, bf16[256,512]{1,0:T(8,128)(2,1)}, u32[]{:S(2)}) copy-start(bf16[256,512]{1,0:T(8,128)(2,1)} %get-tuple-element.32.d0_ref) | copy-start | bytes 786436
  30.5 8.0 %copy-start.9 = (bf16[256,2048]{1,0:T(8,128)(2,1)S(1)}, bf16[256,2048]{1,0:T(8,128)(2,1)}, u32[]{:S(2)}) copy-start(bf16[256,2048]{1,0:T(8,128)(2,1)} %get-tuple-element.34) | copy-start | bytes 3145732
  30.5 9.3 %copy-start.8 = (bf16[256,2048]{1,0:T(8,128)(2,1)S(1)}, bf16[256,2048]{1,0:T(8,128)(2,1)}, u32[]{:S(2)}) copy-start(bf16[256,2048]{1,0:T(8,128)(2,1)} %get-tuple-element.36) | copy-start | bytes 3145732
  30.5 12.5 %copy-start.7 = (bf16[2,256,512]{2,1,0:T(8,128)(2,1)S(1)}, bf16[2,256,512]{2,1,0:T(8,128)(2,1)}, u32[]{:S(2)}) copy-start(bf16[2,256,512]{2,1,0:T(8,128)(2,1)} %get-tuple-element.30) | copy-start | bytes 1572868
  31.5 13.3 %copy-start.2 = (bf16[256,512]{1,0:T(8,128)(2,1)S(1)}, bf16[256,512]{1,0:T(8,128)(2,1)}, u32[]{:S(2)}) copy-start(bf16[256,512]{1,0:T(8,128)(2,1)} %get-tuple-element.32.d0_ref) | copy-start | bytes 786436
  31.6 23.8 %collective-permute-start.11 = (bf16[2,256,512]{2,1,0:T(8,128)(2,1)S(1)}, bf16[2,256,512]{2,1,0:T(8,128)(2,1)S(1)}, u32[]{:S(2)}, u32[]{:S(2)}) collective-permute-start(bf16[2,256,512]{2,1,0:T(8,128)(2,1)S(1)} %get-tuple-element.45), channel_id=1, source_target_pairs={{0,1},{1,0},{2,3},{3,2},{4,5},{5,4},{6,7},{7,6},{8,9},{9,8},{10,11... | collective-permute-start | bytes 1572872 | tf_op jit(solution)/shard_map/up_first/ppermute | solution.py:246
  31.6 38.8 %collective-permute-start.7 = (bf16[2,256,512]{2,1,0:T(8,128)(2,1)S(1)}, bf16[2,256,512]{2,1,0:T(8,128)(2,1)S(1)}, u32[]{:S(2)}, u32[]{:S(2)}) collective-permute-start(bf16[2,256,512]{2,1,0:T(8,128)(2,1)S(1)} %get-tuple-element.33), channel_id=1, source_target_pairs={{0,1},{1,0},{2,3},{3,2},{4,5},{5,4},{6,7},{7,6},{8,9},{9,8},{10,11... | collective-permute-start | bytes 1572872 | tf_op jit(solution)/shard_map/gate_first/ppermute | solution.py:246
  38.5 45.8 %collective-permute-start.2 = (bf16[256,2048]{1,0:T(8,128)(2,1)S(1)}, bf16[256,2048]{1,0:T(8,128)(2,1)S(1)}, u32[]{:S(2)}, u32[]{:S(2)}) collective-permute-start(bf16[256,2048]{1,0:T(8,128)(2,1)S(1)} %copy-done.9), channel_id=1, source_target_pairs={{4,0},{8,4},{12,8},{16,12},{20,16},{24,20},{28,24},{5,1},{9,5},{13... | collective-permute-start | bytes 3145736 | tf_op jit(solution)/shard_map/dx_first/ppermute | solution.py:235
  39.8 44.5 %collective-permute-start.3 = (bf16[256,2048]{1,0:T(8,128)(2,1)S(1)}, bf16[256,2048]{1,0:T(8,128)(2,1)S(1)}, u32[]{:S(2)}, u32[]{:S(2)}) collective-permute-start(bf16[256,2048]{1,0:T(8,128)(2,1)S(1)} %copy-done.8), channel_id=1, source_target_pairs={{0,4},{4,8},{8,12},{12,16},{16,20},{20,24},{24,28},{1,5},{5,9},{9,... | collective-permute-start | bytes 3145736 | tf_op jit(solution)/shard_map/dx_second/ppermute | solution.py:235
  43.2 28.6 %collective-permute-start.5 = (bf16[1,256,512]{2,1,0:T(8,128)(2,1)S(1)}, bf16[1,256,512]{2,1,0:T(8,128)(2,1)S(1)}, u32[]{:S(2)}, u32[]{:S(2)}) collective-permute-start(bf16[1,256,512]{2,1,0:T(8,128)(2,1)S(1)} %get-tuple-element.50), channel_id=1, source_target_pairs={{0,2},{1,3},{2,0},{3,1},{4,6},{5,7},{6,4},{7,5},{8,10},{9,11},{10,... | collective-permute-start | bytes 786440 | tf_op jit(solution)/shard_map/down0_rest/ppermute | solution.py:246
  45.9 36.3 %copy-start.3 = (f32[1,512,256]{2,1,0:T(8,128)S(1)}, f32[1,512,256]{2,1,0:T(8,128)}, u32[]{:S(2)}) copy-start(f32[1,512,256]{2,1,0:T(8,128)} %refs_0_.4) | copy-start | bytes 1572868
  55.3 27.9 %copy-start.4 = (f32[1,512,256]{2,1,0:T(8,128)S(1)}, f32[1,512,256]{2,1,0:T(8,128)}, u32[]{:S(2)}) copy-start(f32[1,512,256]{2,1,0:T(8,128)} %refs_0_.2) | copy-start | bytes 1572868
  55.5 26.7 %collective-permute-start.12 = (bf16[1,256,512]{2,1,0:T(8,128)(2,1)S(1)}, bf16[1,256,512]{2,1,0:T(8,128)(2,1)S(1)}, u32[]{:S(2)}, u32[]{:S(2)}) collective-permute-start(bf16[1,256,512]{2,1,0:T(8,128)(2,1)S(1)} %get-tuple-element.46), channel_id=1, source_target_pairs={{0,2},{1,3},{2,0},{3,1},{4,6},{5,7},{6,4},{7,5},{8,10},{9,11},{10,... | collective-permute-start | bytes 786440 | tf_op jit(solution)/shard_map/up_rest/ppermute | solution.py:246
  70.5 12.7 %collective-permute-start.8 = (bf16[1,256,512]{2,1,0:T(8,128)(2,1)S(1)}, bf16[1,256,512]{2,1,0:T(8,128)(2,1)S(1)}, u32[]{:S(2)}, u32[]{:S(2)}) collective-permute-start(bf16[1,256,512]{2,1,0:T(8,128)(2,1)S(1)} %add_convert_fusion.4), channel_id=1, source_target_pairs={{0,28},{4,24},{8,20},{12,16},{16,12},{20,8},{24,4},{28,0},{1,29},{... | collective-permute-start | bytes 786440 | tf_op jit(solution)/shard_map/down_mirror/ppermute | solution.py:241
  71.8 15.4 %collective-permute-start.10 = (bf16[1,256,512]{2,1,0:T(8,128)(2,1)S(1)}, bf16[1,256,512]{2,1,0:T(8,128)(2,1)S(1)}, u32[]{:S(2)}, u32[]{:S(2)}) collective-permute-start(bf16[1,256,512]{2,1,0:T(8,128)(2,1)S(1)} %get-tuple-element.43), channel_id=1, source_target_pairs={{0,2},{1,3},{2,0},{3,1},{4,6},{5,7},{6,4},{7,5},{8,10},{9,11},{10,... | collective-permute-start | bytes 786440 | tf_op jit(solution)/shard_map/gate_rest/ppermute | solution.py:246
  84.3 3.0 %copy-start.5 = (f32[1,512,256]{2,1,0:T(8,128)S(1)}, f32[1,512,256]{2,1,0:T(8,128)}, u32[]{:S(2)}) copy-start(f32[1,512,256]{2,1,0:T(8,128)} %refs_0_.3) | copy-start | bytes 1572868
